TPU v7x, 32 devices: a whole 2x2x4 slice. The times are simulated.
32 devices in a mesh: row: 4 (over y, core), col: 8 (over z, x).
Axes of the slice: x: 2, y: 2, z: 4, core: 2. Of those that a mesh axis runs over, the one named last changes fastest.
Arguments:
- vectors: bfloat16 [24576, 1024], P(('row', 'col')), may hold values from -6 to 6
- ham_blocks: bfloat16 [192, 5, 128, 128], P(('row', 'col')), as said below
- ham_columns: int32 [192, 5], P(('row', 'col')), may hold values from 0 to 191, as said below
- bounds: float32 [2], replicated, may hold values from -1 to 2.6, as said below
Outputs:
- filtered: bfloat16 [24576, 1024], P(('row', 'col'))
Inputs may be any that keep to these rules, and one draw needn't show every extreme that they name: `ham_columns`: each slot of block row g names a block column (g + o) mod 192 with -2 <= o <= 2; some slot names g itself, every other distance at most once. Slots whose offset is absent name g itself and carry zero blocks; the one slot with offset 0 carries the diagonal block. `ham_blocks`: H is symmetric: the block of block row g at block column h is the transpose of the block of block row h at block column g. bounds[0] < bounds[1].
All inputs are finite; a program needn't handle non-finite values.
Results may differ from a plain program's by a relative error of at most 0.0045.
Values may be sent and summed in bfloat16 or wider, within the bound.
No kernel may reach another device: no remote copies, remote signals or barrier semaphores. Data moves between devices by JAX's collectives and lax.ppermute only.
A program may use at most 64 MiB of HBM per device.

v0:
```python
import jax
import jax.numpy as jnp
from jax import lax
from jax.sharding import PartitionSpec as P

REACH = 2
DEG = 2


def extended(cells, sides, width):
    for axis, dim in sides:
        count = lax.axis_size(axis)
        head = lax.slice_in_dim(cells, 0, width, axis=dim)
        tail = lax.slice_in_dim(cells, cells.shape[dim] - width, cells.shape[dim], axis=dim)
        cells = jnp.concatenate(
            [
                lax.ppermute(tail, axis, [(i, (i + 1) % count) for i in range(count)]),
                cells,
                lax.ppermute(head, axis, [((i + 1) % count, i) for i in range(count)]),
            ],
            axis=dim,
        )
    return cells


def per_device(vectors, ham_blocks, ham_columns, bounds):
    rows_here = ham_blocks.shape[0]
    block_size = ham_blocks.shape[2]
    vec_width = vectors.shape[1]
    total_blocks = lax.axis_size(("row", "col")) * rows_here
    first = lax.axis_index(("row", "col")) * rows_here
    center = 0.5 * (bounds[1] + bounds[0])
    halfwidth = 0.5 * (bounds[1] - bounds[0])
    previous = vectors
    current = vectors
    for degree_step in range(DEG):
        padded = extended(current, ((("row", "col"), 0),), REACH * block_size)
        local_index = jnp.remainder(ham_columns - first + REACH, total_blocks)
        grid = padded.reshape(-1, block_size, vec_width)
        picked = jnp.take(grid, local_index, axis=0)
        product = jnp.einsum(
            "rkij,rkjm->rim", ham_blocks, picked, preferred_element_type=jnp.float32
        )
        image = product.reshape(ham_blocks.shape[0] * block_size, vec_width)
        shifted = (image - center * current.astype(jnp.float32)) / halfwidth
        if degree_step == 0:
            updated = shifted
        else:
            updated = 2.0 * shifted - previous.astype(jnp.float32)
        previous, current = (current, updated.astype(jnp.bfloat16))
    return current


def solution(mesh):
    return jax.shard_map(
        per_device,
        mesh=mesh,
        in_specs=(
            P(("row", "col"), None),
            P(("row", "col"), None, None, None),
            P(("row", "col"), None),
            P(),
        ),
        out_specs=P(("row", "col"), None),
        check_vma=False,
    )
```

profile of v0, /device:TPU:0, one launch (start us, length us, event | category | flops | bytes accessed | tf_op | source)
XLA Modules:
  0.0 86.5 jit_solution(16819173772472155472)
XLA Ops:
  0.0 0.0 copy-start
  0.0 0.0 copy-start.1
  0.0 2.4 %fusion.17 = (bf16[256,1024]{1,0:T(8,128)(2,1)}, bf16[256,1024]{1,0:T(8,128)(2,1)}) fusion(bf16[768,1024]{1,0:T(8,128)(2,1)} %param.6), kind=kLoop, calls=%fused_computation.29 | loop fusion | bytes 2097152 | tf_op jit(solution)/shard_map/slice | solution.py:14
  2.4 2.9 %collective-permute-start = (bf16[256,1024]{1,0:T(8,128)(2,1)}, bf16[256,1024]{1,0:T(8,128)(2,1)S(1)}, u32[]{:S(2)}, u32[]{:S(2)}) collective-permute-start(bf16[256,1024]{1,0:T(8,128)(2,1)} %get-tuple-element.10), channel_id=1, source_target_pairs={{0,1},{1,2},{2,3},{3,4},{4,5},{5,6},{6,7},{7,8},{8,9},{9,10},{10,1... | collective-permute-start | bytes 1572872 | tf_op jit(solution)/shard_map/ppermute | solution.py:17
  5.3 3.4 %collective-permute-start.1 = (bf16[256,1024]{1,0:T(8,128)(2,1)}, bf16[256,1024]{1,0:T(8,128)(2,1)}, u32[]{:S(2)}, u32[]{:S(2)}) collective-permute-start(bf16[256,1024]{1,0:T(8,128)(2,1)} %get-tuple-element.11), channel_id=1, source_target_pairs={{1,0},{2,1},{3,2},{4,3},{5,4},{6,5},{7,6},{8,7},{9,8},{10,9},{11,1... | collective-permute-start | bytes 1572872 | tf_op jit(solution)/shard_map/ppermute | solution.py:19
  8.8 1.4 %fusion.18 = (f32[1]{0:T(128)}, f32[1]{0:T(128)}) fusion(f32[2]{0:T(128)} %param.9), kind=kLoop, calls=%fused_computation.30 | loop fusion | bytes 16 | tf_op jit(solution)/shard_map/slice | solution.py:32
  12.7 0.7 compare_and_fusion
  13.4 0.1 reshape.47
  13.5 14.6 %collective-permute-done = bf16[256,1024]{1,0:T(8,128)(2,1)S(1)} collective-permute-done((bf16[256,1024]{1,0:T(8,128)(2,1)}, bf16[256,1024]{1,0:T(8,128)(2,1)S(1)}, u32[]{:S(2)}, u32[]{:S(2)}) %collective-permute-start) | collective-permute-done | bytes 524320 | tf_op jit(solution)/shard_map/ppermute | solution.py:17
  28.1 2.2 %collective-permute-done.1 = bf16[256,1024]{1,0:T(8,128)(2,1)} collective-permute-done((bf16[256,1024]{1,0:T(8,128)(2,1)}, bf16[256,1024]{1,0:T(8,128)(2,1)}, u32[]{:S(2)}, u32[]{:S(2)}) %collective-permute-start.1) | collective-permute-done | bytes 524320 | tf_op jit(solution)/shard_map/ppermute | solution.py:19
  30.3 0.0 copy-done.1
  30.3 2.8 %pad_maximum_fusion = bf16[1280,1024]{1,0:T(8,128)(2,1)} fusion(bf16[256,1024]{1,0:T(8,128)(2,1)} %collective-permute-done.1, bf16[768,1024]{1,0:T(8,128)(2,1)S(1)} %copy-done.1, bf16[256,1024]{1,0:T(8,128)(2,1)S(1)} %collective-permute-done), kind=kLoop, calls=%fused_computation.19 | loop fusion | flops 7864320 | bytes 5242880 | tf_op jit(solution)/shard_map/concatenate | solution.py:15
  33.1 6.6 %gather_fusion = bf16[30,128,1024]{2,1,0:T(8,128)(2,1)} fusion(bf16[10,128,1024]{2,1,0:T(8,128)(2,1)} %bitcast.29, s32[1024]{0:T(1024)S(1)} %pad_clamp_fusion), kind=kCustom, calls=%fused_computation.clone | custom fusion | bytes 15728760 | tf_op jit(solution)/shard_map/jit(_take)/gather | solution.py:40
  39.7 0.0 copy-done
  39.7 4.8 %fusion.2 = f32[6,1024,128,1]{1,2,3,0:T(8,128)S(1)} fusion(bf16[6,5,128,128]{3,2,1,0:T(8,128)(2,1)S(1)} %copy-done, bf16[6,5,128,1024]{3,2,1,0:T(8,128)(2,1)} %bitcast.31, pred[6,5]{1,0:T(8,128)(4,1)S(1)} %get-tuple-element.6), kind=kOutput, calls=%fused_computation.4 | convolution fusion | flops 1010565120 | bytes 11993118 | tf_op jit(solution)/shard_map/rkij,rkjm->rim/dot_general | solution.py:41
  44.5 0.7 fusion.10
  45.2 0.0 copy-start.2
  45.2 0.1 fusion.16
  45.3 0.2 collective-permute-start.2
  45.5 5.2 %collective-permute-start.3 = (bf16[256,1024]{1,0:T(8,128)(2,1)S(1)}, bf16[256,1024]{1,0:T(8,128)(2,1)S(1)}, u32[]{:S(2)}, u32[]{:S(2)}) collective-permute-start(bf16[256,1024]{1,0:T(8,128)(2,1)S(1)} %get-tuple-element.9), channel_id=1, source_target_pairs={{1,0},{2,1},{3,2},{4,3},{5,4},{6,5},{7,6},{8,7},{9,8},{10,9},{11,1... | collective-permute-start | bytes 1572872 | tf_op jit(solution)/shard_map/ppermute | solution.py:19
  50.7 16.4 %collective-permute-done.2 = bf16[256,1024]{1,0:T(8,128)(2,1)S(1)} collective-permute-done((bf16[256,1024]{1,0:T(8,128)(2,1)S(1)}, bf16[256,1024]{1,0:T(8,128)(2,1)S(1)}, u32[]{:S(2)}, u32[]{:S(2)}) %collective-permute-start.2) | collective-permute-done | bytes 524320 | tf_op jit(solution)/shard_map/ppermute | solution.py:17
  67.1 4.0 %collective-permute-done.3 = bf16[256,1024]{1,0:T(8,128)(2,1)S(1)} collective-permute-done((bf16[256,1024]{1,0:T(8,128)(2,1)S(1)}, bf16[256,1024]{1,0:T(8,128)(2,1)S(1)}, u32[]{:S(2)}, u32[]{:S(2)}) %collective-permute-start.3) | collective-permute-done | bytes 524320 | tf_op jit(solution)/shard_map/ppermute | solution.py:19
  71.1 1.8 %pad_maximum_fusion.1 = bf16[1280,1024]{1,0:T(8,128)(2,1)} fusion(bf16[256,1024]{1,0:T(8,128)(2,1)S(1)} %collective-permute-done.3, bf16[768,1024]{1,0:T(8,128)(2,1)S(1)} %fusion.10, bf16[256,1024]{1,0:T(8,128)(2,1)S(1)} %collective-permute-done.2), kind=kLoop, calls=%fused_computation.20 | loop fusion | flops 7864320 | bytes 5242880 | tf_op jit(solution)/shard_map/concatenate | solution.py:15
  72.9 0.0 copy-done.2
  72.9 6.6 %gather_fusion.1 = bf16[30,128,1024]{2,1,0:T(8,128)(2,1)} fusion(bf16[10,128,1024]{2,1,0:T(8,128)(2,1)} %bitcast.28, s32[1024]{0:T(1024)S(1)} %pad_clamp_fusion), kind=kCustom, calls=%fused_computation.1.clone | custom fusion | bytes 15728760 | tf_op jit(solution)/shard_map/jit(_take)/gather | solution.py:40
  79.5 0.0 copy-start.3
  79.5 4.9 %fusion = f32[6,1024,128,1]{1,2,3,0:T(8,128)S(1)} fusion(bf16[6,5,128,128]{3,2,1,0:T(8,128)(2,1)S(1)} %copy-done, bf16[6,5,128,1024]{3,2,1,0:T(8,128)(2,1)} %bitcast.30, pred[6,5]{1,0:T(8,128)(4,1)S(1)} %get-tuple-element.6), kind=kOutput, calls=%fused_computation.2 | convolution fusion | flops 1010565120 | bytes 11993118 | tf_op jit(solution)/shard_map/rkij,rkjm->rim/dot_general | solution.py:41
  84.4 0.0 copy-done.3
  84.4 2.1 %fusion.11 = bf16[768,1024]{1,0:T(8,128)(2,1)} fusion(bf16[768,1024]{1,0:T(8,128)(2,1)S(1)} %copy-done.1, f32[6,1024,128,1]{1,2,3,0:T(8,128)S(1)} %fusion, bf16[768,1024]{1,0:T(8,128)(2,1)S(1)} %copy-done.3, f32[]{:T(128)} %bitcast.7, f32[]{:T(128)} %bitcast.6), kind=kLoop, calls=%fused_computation.15 | loop fusion | flops 6291456 | bytes 7864328 | tf_op jit(solution)/shard_map/convert_element_type | solution.py:50
  (1 shorter events, 0.0 us)
Async XLA Ops:
  0.0 39.7 %copy-start = (bf16[6,5,128,128]{3,2,1,0:T(8,128)(2,1)S(1)}, bf16[6,5,128,128]{3,2,1,0:T(8,128)(2,1)}, u32[]{:S(2)}) copy-start(bf16[6,5,128,128]{3,2,1,0:T(8,128)(2,1)} %param.7) | copy-start | bytes 2949124
  0.0 30.3 %copy-start.1 = (bf16[768,1024]{1,0:T(8,128)(2,1)S(1)}, bf16[768,1024]{1,0:T(8,128)(2,1)}, u32[]{:S(2)}) copy-start(bf16[768,1024]{1,0:T(8,128)(2,1)} %param.6) | copy-start | bytes 4718596
  2.4 25.7 %collective-permute-start = (bf16[256,1024]{1,0:T(8,128)(2,1)}, bf16[256,1024]{1,0:T(8,128)(2,1)S(1)}, u32[]{:S(2)}, u32[]{:S(2)}) collective-permute-start(bf16[256,1024]{1,0:T(8,128)(2,1)} %get-tuple-element.10), channel_id=1, source_target_pairs={{0,1},{1,2},{2,3},{3,4},{4,5},{5,6},{6,7},{7,8},{8,9},{9,10},{10,1... | collective-permute-start | bytes 1572872 | tf_op jit(solution)/shard_map/ppermute | solution.py:17
  5.3 24.9 %collective-permute-start.1 = (bf16[256,1024]{1,0:T(8,128)(2,1)}, bf16[256,1024]{1,0:T(8,128)(2,1)}, u32[]{:S(2)}, u32[]{:S(2)}) collective-permute-start(bf16[256,1024]{1,0:T(8,128)(2,1)} %get-tuple-element.11), channel_id=1, source_target_pairs={{1,0},{2,1},{3,2},{4,3},{5,4},{6,5},{7,6},{8,7},{9,8},{10,9},{11,1... | collective-permute-start | bytes 1572872 | tf_op jit(solution)/shard_map/ppermute | solution.py:19
  45.2 27.7 %copy-start.2 = (bf16[768,1024]{1,0:T(8,128)(2,1)}, bf16[768,1024]{1,0:T(8,128)(2,1)S(1)}, u32[]{:S(2)}) copy-start(bf16[768,1024]{1,0:T(8,128)(2,1)S(1)} %fusion.10) | copy-start | bytes 4718596
  45.3 21.8 %collective-permute-start.2 = (bf16[256,1024]{1,0:T(8,128)(2,1)S(1)}, bf16[256,1024]{1,0:T(8,128)(2,1)S(1)}, u32[]{:S(2)}, u32[]{:S(2)}) collective-permute-start(bf16[256,1024]{1,0:T(8,128)(2,1)S(1)} %get-tuple-element.8), channel_id=1, source_target_pairs={{0,1},{1,2},{2,3},{3,4},{4,5},{5,6},{6,7},{7,8},{8,9},{9,10},{10,1... | collective-permute-start | bytes 1572872 | tf_op jit(solution)/shard_map/ppermute | solution.py:17
  45.5 25.6 %collective-permute-start.3 = (bf16[256,1024]{1,0:T(8,128)(2,1)S(1)}, bf16[256,1024]{1,0:T(8,128)(2,1)S(1)}, u32[]{:S(2)}, u32[]{:S(2)}) collective-permute-start(bf16[256,1024]{1,0:T(8,128)(2,1)S(1)} %get-tuple-element.9), channel_id=1, source_target_pairs={{1,0},{2,1},{3,2},{4,3},{5,4},{6,5},{7,6},{8,7},{9,8},{10,9},{11,1... | collective-permute-start | bytes 1572872 | tf_op jit(solution)/shard_map/ppermute | solution.py:19
  79.5 4.9 %copy-start.3 = (bf16[768,1024]{1,0:T(8,128)(2,1)S(1)}, bf16[768,1024]{1,0:T(8,128)(2,1)}, u32[]{:S(2)}) copy-start(bf16[768,1024]{1,0:T(8,128)(2,1)} %copy-done.2) | copy-start | bytes 4718596
where the time goes:
time: 86.9 us; the launch traced here: 86.5 us
  waiting for transfers between devices  37.2 us (43%)
  local copies, waits for them, and re-layouts  17.1 us (20%)
  starting transfers between devices  11.8 us (14%)
  matrix products  9.74 us (11%)
  other arithmetic  8.11 us (9%)
  between operations  2.58 us (3%)
    ppermute x2, waiting for transfers between devices, extended(): lax.ppermute(tail, axis, [(i, (i + 1) % count) for i in range(count)])  31 us
    gather x2, local copies, waits for them, and re-layouts, per_device(): picked = jnp.take(grid, local_index, axis=0)  13.2 us
    dot_general x2, matrix products, per_device(): jnp.einsum('rkij,rkjm->rim', ham_blocks, picked, preferred_element_type=j...  9.74 us
    ppermute x2, starting transfers between devices, extended(): lax.ppermute(head, axis, [((i + 1) % count, i) for i in range(count)])  8.62 us
    ppermute x2, waiting for transfers between devices, extended(): lax.ppermute(head, axis, [((i + 1) % count, i) for i in range(count)])  6.24 us
    concatenate x2, other arithmetic, extended(): jnp.concatenate([lax.ppermute(tail, axis, [(i, (i + 1) % count) for i in...  4.64 us
    ppermute x2, starting transfers between devices, extended(): lax.ppermute(tail, axis, [(i, (i + 1) % count) for i in range(count)])  3.15 us
    convert_element_type x2, other arithmetic, per_device(): previous, current = (current, updated.astype(jnp.bfloat16))  2.75 us
  transfers between devices with their start and end apart: 4, of which 4 were waited for; matrix products, arithmetic and copies ran while one was open for 3% of the time, Pallas kernels for 0%

commit v1 on v0

v1 whole, which is shorter than its diff:
```python
import functools

import jax
import jax.numpy as jnp
from jax import lax
from jax.experimental import pallas as pl
from jax.experimental.pallas import tpu as pltpu
from jax.sharding import PartitionSpec as P

AXES = ("row", "col")
B = 128
PAIR = 2 * B
HEAD = 6 * B
X_SLABS = (5, 3)
D_SLABS = (3, 5)
LIMIT = pltpu.CompilerParams(vmem_limit_bytes=16 * 1024 * 1024)
FREE = pl.CostEstimate(flops=0, bytes_accessed=0, transcendentals=0)


def place():
    return lax.axis_index("row") * lax.axis_size("col") + lax.axis_index("col")


def dot(a, b):
    return jnp.dot(a, b, preferred_element_type=jnp.float32)


def turn(block):
    return block.astype(jnp.float32).T.astype(block.dtype)


def natural(pair, pairs):
    odd = lax.rem(place(), 2)
    return pl.ds(pl.multiple_of(jnp.where(odd == 1, pairs - 1 - pair, pair) * PAIR, PAIR), PAIR)


def head(c):
    return HEAD if c == 0 else 0


def pack_kernel(total_blocks, cols_ref, blocks_ref, v_ref, own_ref, *sent):
    x_refs, d_refs = sent[: len(X_SLABS)], sent[len(X_SLABS) :]
    here = place()
    odd = lax.rem(here, 2)
    rows_here, slots = blocks_ref.shape[0], blocks_ref.shape[1]
    pairs = rows_here // 2
    first = here * rows_here
    own_ref[...] = jnp.zeros_like(own_ref)
    for r in range(rows_here):
        j, i = r // 2, r % 2
        row = pl.multiple_of(jnp.where(odd == 1, pairs - 1 - j, j) * PAIR + i * B, B)
        for k in range(slots):
            offset = lax.rem(cols_ref[r, k] - (first + r) + 2 + total_blocks, total_blocks)
            at = offset + i
            turned = (2 - at // 2) * 2 + lax.rem(at, 2)
            col = pl.multiple_of(jnp.where(odd == 1, turned, at) * B, B)
            own_ref[pl.ds(row, B), pl.ds(col, B)] += blocks_ref[r, k]
    last = (pairs - 1) * PAIR
    for out, row, near, mid in ((x_refs[0], last, PAIR, 0), (d_refs[0], 0, PAIR, 2 * PAIR)):
        out[0:B, :] = own_ref[row : row + B, near : near + B]
        out[B : 2 * B, :] = own_ref[row : row + B, near + B : near + 2 * B]
        out[2 * B : 3 * B, :] = own_ref[row + B : row + 2 * B, near + B : near + 2 * B]
        out[3 * B : 4 * B, :] = own_ref[row : row + B, mid : mid + B]
        out[4 * B : 5 * B, :] = (
            own_ref[row : row + B, mid + B : mid + 2 * B]
            + own_ref[row + B : row + 2 * B, mid : mid + B]
        )
        out[5 * B : 6 * B, :] = own_ref[row + B : row + 2 * B, mid + B : mid + 2 * B]
    for refs, split, edge in ((x_refs, X_SLABS, pairs - 1), (d_refs, D_SLABS, 0)):
        slab = 0
        for c, slabs in enumerate(split):
            for s in range(slabs):
                at = head(c) + s * PAIR
                refs[c][at : at + PAIR, :] = v_ref[
                    natural(edge, pairs), slice(slab * B, (slab + 1) * B)
                ]
                slab += 1


def scales(bounds_ref):
    low, high = bounds_ref[0], bounds_ref[1]
    return 0.5 * (high + low), 0.5 * (high - low)


def core_kernel(bounds_ref, v_ref, own_ref, one_ref, g0_ref, g2_ref, h0_ref, h1_ref, h2_ref):
    pairs = v_ref.shape[0] // PAIR
    center, halfwidth = scales(bounds_ref)
    for at in range(0, v_ref.shape[1], PAIR):
        lanes = slice(at, at + PAIR)
        v0, v1, v2 = (v_ref[natural(j, pairs), lanes] for j in range(3))
        v = jnp.concatenate([v0, v1, v2], axis=0)
        g0_ref[:, lanes] = dot(own_ref[0:PAIR, PAIR:], v[: 2 * PAIR])
        g2_ref[:, lanes] = dot(own_ref[2 * PAIR :, : 2 * PAIR], v[PAIR:])
        image = dot(own_ref[PAIR : 2 * PAIR, :], v)
        one = ((image - center * v1.astype(jnp.float32)) / halfwidth).astype(one_ref.dtype)
        one_ref[:, lanes] = one
        h0_ref[:, lanes] = dot(own_ref[0:PAIR, 2 * PAIR :], one)
        h1_ref[:, lanes] = dot(own_ref[PAIR : 2 * PAIR, PAIR : 2 * PAIR], one)
        h2_ref[:, lanes] = dot(own_ref[2 * PAIR :, 0:PAIR], one)


def halo_kernel(side, own_ref, sent_ref, halo_ref):
    odd = lax.rem(place(), 2)
    halo_ref[...] = jnp.zeros_like(halo_ref)
    if side == 0:
        known, low = own_ref[0:PAIR, 0:PAIR], odd
    else:
        known, low = own_ref[2 * PAIR :, 2 * PAIR :], 1 - odd
    halo_ref[:, 0:PAIR] = turn(known)
    near, far = PAIR, 2 * PAIR
    halo_ref[0:B, near : near + B] = sent_ref[0:B, :]
    halo_ref[0:B, near + B : near + PAIR] = sent_ref[B : 2 * B, :]
    halo_ref[B:PAIR, near : near + B] = turn(sent_ref[B : 2 * B, :])
    halo_ref[B:PAIR, near + B : near + PAIR] = sent_ref[2 * B : 3 * B, :]
    halo_ref[0:B, far : far + B] = sent_ref[3 * B : 4 * B, :]
    halo_ref[
        pl.ds(pl.multiple_of(low * B, B), B), pl.ds(pl.multiple_of(far + (1 - low) * B, B), B)
    ] = sent_ref[4 * B : 5 * B, :]
    halo_ref[B:PAIR, far + B : far + PAIR] = sent_ref[5 * B : 6 * B, :]


def side_kernel(
    side, first_slab, slabs, top, bounds_ref, v_ref, near_ref, low_ref, high_ref, own_ref, halo_ref,
    one_ref, g_ref, h_ref, h1_ref, *rest
):
    if side == 0:
        h1_out, out_ref, end_ref, sems = rest[-4:]
    else:
        out_ref, end_ref, mid_ref, sems = rest[-4:]
    pairs = v_ref.shape[0] // PAIR
    center, halfwidth = scales(bounds_ref)
    edge = 0 if side == 0 else 2
    rows = slice(edge * PAIR, (edge + 1) * PAIR)
    outward = slice(0, PAIR) if side == 0 else slice(2 * PAIR, 3 * PAIR)
    step = 2 if slabs % 2 == 0 else slabs
    for s in range(0, slabs, step):
        lanes = slice((first_slab + s) * B, (first_slab + s + step) * B)
        here = slice(s * B, (s + step) * B)
        near = jnp.concatenate(
            [near_ref[top + t * PAIR : top + (t + 1) * PAIR, :] for t in range(s, s + step)], axis=1
        )
        v = v_ref[natural(edge, pairs), lanes]
        stack = jnp.concatenate([v, near, low_ref[:, lanes], high_ref[:, lanes]], axis=0)
        v32 = v.astype(jnp.float32)
        image = g_ref[:, lanes] + dot(own_ref[rows, outward], near)
        edge_one = ((image - center * v32) / halfwidth).astype(v.dtype)
        image = dot(halo_ref[...], stack)
        near_one = ((image - center * near.astype(jnp.float32)) / halfwidth).astype(v.dtype)
        h1 = h1_ref[:, lanes] + dot(own_ref[PAIR : 2 * PAIR, outward], edge_one)
        if side == 0:
            h1_out[:, lanes] = h1
        else:
            one, v1 = one_ref[:, lanes].astype(jnp.float32), v_ref[natural(1, pairs), lanes].astype(jnp.float32)
            mid_ref[:, here] = (2.0 * ((h1 - center * one) / halfwidth) - v1).astype(v.dtype)
        image = h_ref[:, lanes] + (
            dot(own_ref[rows, PAIR : 2 * PAIR], edge_one) + dot(own_ref[rows, outward], near_one)
        )
        end_ref[:, here] = (
            2.0 * ((image - center * edge_one.astype(jnp.float32)) / halfwidth) - v32
        ).astype(v.dtype)
    lanes = slice(first_slab * B, (first_slab + slabs) * B)
    copies = [pltpu.make_async_copy(end_ref, out_ref.at[natural(edge, pairs), lanes], sems.at[0])]
    if side:
        copies.append(pltpu.make_async_copy(mid_ref, out_ref.at[natural(1, pairs), lanes], sems.at[1]))
    for copy in copies:
        copy.start()
    for copy in copies:
        copy.wait()


def whole(ref_space=pltpu.VMEM):
    return pl.BlockSpec(memory_space=ref_space)


def call(body, out_shape, args, name, aliases=None, scratch=()):
    aliases = aliases or {}
    outs = out_shape if isinstance(out_shape, list) else [out_shape]
    spaces = [
        pltpu.SMEM if a.size < 1024 else pl.ANY if isinstance(outs[aliases.get(i, 0)], jax.ShapeDtypeStruct) and i in aliases else pltpu.VMEM
        for i, a in enumerate(args)
    ]
    return pl.pallas_call(
        body,
        out_shape=out_shape,
        in_specs=[whole(space) for space in spaces],
        out_specs=jax.tree.map(
            lambda o: whole(pl.ANY if isinstance(o, jax.ShapeDtypeStruct) else pltpu.VMEM), out_shape
        ),
        scratch_shapes=scratch,
        input_output_aliases=aliases,
        compiler_params=LIMIT,
        cost_estimate=FREE,
        name=name,
    )(
        *(
            pltpu.with_memory_space_constraint(a, pltpu.VMEM) if space == pltpu.VMEM else a
            for a, space in zip(args, spaces, strict=True)
        )
    )


def per_device(vectors, ham_blocks, ham_columns, bounds):
    rows, vec_width = vectors.shape
    rows_here = ham_blocks.shape[0]
    ring = lax.axis_size(AXES)
    dtype = vectors.dtype
    swap_x = [(i, i ^ 1) for i in range(ring)]
    swap_d = [(i, (i + 1) % ring if i % 2 else (i - 1) % ring) for i in range(ring)]
    onward = [(i, (i - 2) % ring if i % 2 else (i + 2) % ring) for i in range(ring)]
    send = functools.partial(lax.ppermute, axis_name=AXES)

    def message(c, slabs):
        return pltpu.VMEM((head(c) + slabs * PAIR, B), dtype)

    middle = [lax.slice_in_dim(vectors, rows // 2 + at, rows // 2 + at + B, axis=0) for at in (-B, 0)]
    own, *parts = call(
        functools.partial(pack_kernel, ring * rows_here),
        [pltpu.VMEM((rows, 3 * PAIR), dtype)]
        + [message(c, slabs) for split in (X_SLABS, D_SLABS) for c, slabs in enumerate(split)],
        [ham_columns, ham_blocks, vectors],
        "pack",
    )
    to_x, to_d = parts[: len(X_SLABS)], parts[len(X_SLABS) :]
    def after(token, value):
        return lax.optimization_barrier((token, value))

    m0, m1 = (send(part, perm=swap_x) for part in middle)
    m0, to_d[0] = after(m0, to_d[0])
    m1, to_d[1] = after(m1, to_d[1])
    far_x = [m0, m1]
    far_d = [send(part, perm=onward) for part in far_x]
    got = [send(part, perm=swap_x) for part in to_d]
    far_d[0], to_x[0] = after(far_d[0], to_x[0])
    got[0], to_x[0] = after(got[0], to_x[0])
    far_d[1], got[1] = after(far_d[1], got[1])
    got[1], to_x[1] = after(got[1], to_x[1])
    near_d = [send(part, perm=onward) for part in got]
    near_x = [send(part, perm=swap_x) for part in to_x]

    wide = lambda kind: pltpu.VMEM((PAIR, vec_width), kind)
    one, g0, g2, h0, h1, h2 = call(
        core_kernel, [wide(dtype)] + [wide(jnp.float32)] * 5, [bounds, vectors, own], "core"
    )
    band = pltpu.VMEM((PAIR, 3 * PAIR), dtype)
    result, out = None, jax.ShapeDtypeStruct((rows, vec_width), dtype)
    for side, near, split, far, g, h in (
        (0, near_d, D_SLABS, far_d, g0, h0),
        (1, near_x, X_SLABS, far_x, g2, h2),
    ):
        if result is not None:
            near[0], result = lax.optimization_barrier((near[0], result))
        halo = call(functools.partial(halo_kernel, side), band, [own, near[0]], "halo")
        first_slab = 0
        for c, slabs in enumerate(split):
            args = [bounds, vectors, near[c], *far, own, halo, one, g, h, h1]
            outs, aliases = [out], {}
            if side == 0:
                outs, aliases = [wide(jnp.float32), out], {len(args) - 1: 0}
            if result is not None:
                aliases[len(args)] = len(outs) - 1
                args.append(result)
            *rest, result = call(
                functools.partial(side_kernel, side, first_slab, slabs, head(c)),
                outs,
                args,
                "side",
                aliases=aliases,
                scratch=[pltpu.VMEM((PAIR, slabs * B), dtype)] * (1 + side)
                + [pltpu.SemaphoreType.DMA((2,))],
            )
            h1 = rest[0] if rest else h1
            first_slab += slabs
    return result


def solution(mesh):
    return jax.shard_map(
        per_device,
        mesh=mesh,
        in_specs=(P(AXES, None), P(AXES, None, None, None), P(AXES, None), P()),
        out_specs=P(AXES, None),
        check_vma=False,
    )
```

time: 86.9 us -> 55.5 us (0.64)
  waiting for transfers between devices: 37.2 us -> 21 us
  local copies, waits for them, and re-layouts: 17.1 us -> 3.25 us
  Pallas kernels: 0 us -> 12.9 us
  matrix products: 9.74 us -> 0 us
  other arithmetic: 8.11 us -> 0 us
  starting transfers between devices: 11.8 us -> 18 us
  between operations: 2.58 us -> 0.08 us
    ppermute x4 -> x10, waiting for transfers between devices: 37.2 us -> 21 us  [the longest x2 7.2 us: per_device(): near_d = [send(part, perm=onward) for part in got]]
    gather x2 -> x0, local copies, waits for them, and re-layouts: 13.2 us -> none  [per_device(): picked = jnp.take(grid, local_index, axis=0)]
    pallas_call x0 -> x8, Pallas kernels: none -> 12.9 us  [call(): pl.pallas_call(body, out_shape=out_shape, in_specs=[whole(space) for spac...]
    dot_general x2 -> x0, matrix products: 9.74 us -> none  [per_device(): jnp.einsum('rkij,rkjm->rim', ham_blocks, picked, preferred_element_type=j...]
    ppermute x4 -> x10, starting transfers between devices: 11.8 us -> 18 us  [the longest x2 4.12 us: per_device(): got = [send(part, perm=swap_x) for part in to_d]]
    concatenate x2 -> x0, other arithmetic: 4.64 us -> none  [extended(): jnp.concatenate([lax.ppermute(tail, axis, [(i, (i + 1) % count) for i in...]
    convert_element_type x2 -> x0, other arithmetic: 2.75 us -> none  [per_device(): previous, current = (current, updated.astype(jnp.bfloat16))]
    slice x3 -> x1, local copies, waits for them, and re-layouts: 3.83 us -> 1.15 us  [per_device(): lax.slice_in_dim(vectors, rows // 2 + at, rows // 2 + at + B, axis=0)]
  transfers between devices with their start and end apart: 4 -> 10, of which waited for: 4 -> 8; matrix products, arithmetic and copies ran while one was open for 3% -> 0% of each run, Pallas kernels for 0% -> 20%
where the time goes in v1:
time: 55.5 us; the launch traced here: 55.3 us
  waiting for transfers between devices  21 us (38%)
  starting transfers between devices  18 us (32%)
  Pallas kernels  12.9 us (23%)
  local copies, waits for them, and re-layouts  3.25 us (6%)
    pallas_call x8, Pallas kernels, call(): pl.pallas_call(body, out_shape=out_shape, in_specs=[whole(space) for spac...  12.9 us
    ppermute x2, waiting for transfers between devices, per_device(): near_d = [send(part, perm=onward) for part in got]  7.2 us
    ppermute x2, waiting for transfers between devices, per_device(): m0, m1 = (send(part, perm=swap_x) for part in middle)  5.65 us
    ppermute x2, waiting for transfers between devices, per_device(): far_d = [send(part, perm=onward) for part in far_x]  4.74 us
    ppermute x2, starting transfers between devices, per_device(): got = [send(part, perm=swap_x) for part in to_d]  4.12 us
    ppermute x2, starting transfers between devices, per_device(): near_x = [send(part, perm=swap_x) for part in to_x]  3.95 us
    ppermute x2, starting transfers between devices, per_device(): near_d = [send(part, perm=onward) for part in got]  3.72 us
    ppermute x2, waiting for transfers between devices, per_device(): got = [send(part, perm=swap_x) for part in to_d]  3.44 us
  transfers between devices with their start and end apart: 10, of which 8 were waited for; matrix products, arithmetic and copies ran while one was open for 0% of the time, Pallas kernels for 20%

profile of v1, /device:TPU:0, one launch (start us, length us, event | category | flops | bytes accessed | tf_op | source)
XLA Modules:
  0.0 55.3 jit_solution(15896908988111908077)
XLA Ops:
  0.0 0.0 copy-start.2
  0.0 0.0 copy-start.3
  0.0 1.1 %fusion = (bf16[128,1024]{1,0:T(8,128)(2,1)S(1)}, bf16[128,1024]{1,0:T(8,128)(2,1)S(1)}) fusion(bf16[768,1024]{1,0:T(8,128)(2,1)} %v_ref.11), kind=kLoop, calls=%fused_computation | loop fusion | bytes 1048576 | tf_op jit(solution)/shard_map/slice | solution.py:215
  1.2 3.0 %collective-permute-start.4 = (bf16[128,1024]{1,0:T(8,128)(2,1)S(1)}, bf16[128,1024]{1,0:T(8,128)(2,1)S(1)}, u32[]{:S(2)}, u32[]{:S(2)}) collective-permute-start(bf16[128,1024]{1,0:T(8,128)(2,1)S(1)} %get-tuple-element.63), channel_id=1, source_target_pairs={{0,1},{1,0},{2,3},{3,2},{4,5},{5,4},{6,7},{7,6},{8,9},{9,8},{10,11... | collective-permute-start | bytes 786440 | tf_op jit(solution)/shard_map/ppermute | solution.py:227
  4.2 0.1 collective-permute-start
  4.2 0.0 copy-done.2
  4.2 0.0 copy-start
  4.2 1.4 %copy-done = bf16[768,1024]{1,0:T(8,128)(2,1)S(1)} copy-done((bf16[768,1024]{1,0:T(8,128)(2,1)S(1)}, bf16[768,1024]{1,0:T(8,128)(2,1)}, u32[]{:S(2)}) %copy-start) | copy-done | bytes 1572888
  5.7 0.0 copy-start.4
  5.7 0.7 %copy-done.4 = s32[6,5]{1,0:T(8,128)S(1)} copy-done((s32[6,5]{1,0:T(8,128)S(1)}, s32[6,5]{1,0:T(8,128)}, u32[]{:S(2)}) %copy-start.4) | copy-done | bytes 144
  6.3 0.0 copy-start.1
  6.3 1.3 %pack.1 = (bf16[768,768]{1,0:T(8,128)(2,1)S(1)}, bf16[2048,128]{1,0:T(8,128)(2,1)S(1)}, bf16[768,128]{1,0:T(8,128)(2,1)S(1)}, bf16[1536,128]{1,0:T(8,128)(2,1)S(1)}, bf16[1280,128]{1,0:T(8,128)(2,1)S(1)}) custom-call(s32[6,5]{1,0:T(8,128)S(1)} %copy-done.4, bf16[6,5,128,128]{3,2,1,0:T(8,128)(2,1)S(1)} %copy-done.2, bf16[768,1024]{1,0:T(8,128)(2,1)S(1)} %copy-done), custom_call_target="tpu_custom_call" | custom-call | tf_op jit(solution)/shard_map/pack/pallas_call | solution.py:182
  7.6 3.7 %collective-permute-done.4.low_ref = bf16[128,1024]{1,0:T(8,128)(2,1)S(1)} collective-permute-done((bf16[128,1024]{1,0:T(8,128)(2,1)S(1)}, bf16[128,1024]{1,0:T(8,128)(2,1)S(1)}, u32[]{:S(2)}, u32[]{:S(2)}) %collective-permute-start.4) | collective-permute-done | bytes 262176 | tf_op jit(solution)/shard_map/ppermute | solution.py:227
  11.3 2.1 %collective-permute-start.5 = (bf16[1536,128]{1,0:T(8,128)(2,1)S(1)}, bf16[1536,128]{1,0:T(8,128)(2,1)S(1)}, u32[]{:S(2)}, u32[]{:S(2)}) collective-permute-start(bf16[1536,128]{1,0:T(8,128)(2,1)S(1)} %get-tuple-element.43), channel_id=1, source_target_pairs={{0,1},{1,0},{2,3},{3,2},{4,5},{5,4},{6,7},{7,6},{8,9},{9,8},{10,11... | collective-permute-start | bytes 1179656 | tf_op jit(solution)/shard_map/ppermute | solution.py:232
  13.4 1.6 %collective-permute-start.6 = (bf16[128,1024]{1,0:T(8,128)(2,1)S(1)}, bf16[128,1024]{1,0:T(8,128)(2,1)S(1)}, u32[]{:S(2)}, u32[]{:S(2)}) collective-permute-start(bf16[128,1024]{1,0:T(8,128)(2,1)S(1)} %collective-permute-done.4.low_ref), channel_id=1, source_target_pairs={{0,2},{1,31},{2,4},{3,1},{4,6},{5,3},{6,8},{7,5},{8,10},{9,7},{10,... | collective-permute-start | bytes 786440 | tf_op jit(solution)/shard_map/ppermute | solution.py:231
  14.9 2.0 %collective-permute-done.high_ref = bf16[128,1024]{1,0:T(8,128)(2,1)S(1)} collective-permute-done((bf16[128,1024]{1,0:T(8,128)(2,1)S(1)}, bf16[128,1024]{1,0:T(8,128)(2,1)S(1)}, u32[]{:S(2)}, u32[]{:S(2)}) %collective-permute-start) | collective-permute-done | bytes 262176 | tf_op jit(solution)/shard_map/ppermute | solution.py:227
  16.9 2.1 %collective-permute-start.2 = (bf16[1280,128]{1,0:T(8,128)(2,1)S(1)}, bf16[1280,128]{1,0:T(8,128)(2,1)S(1)}, u32[]{:S(2)}, u32[]{:S(2)}) collective-permute-start(bf16[1280,128]{1,0:T(8,128)(2,1)S(1)} %get-tuple-element.36), channel_id=1, source_target_pairs={{0,1},{1,0},{2,3},{3,2},{4,5},{5,4},{6,7},{7,6},{8,9},{9,8},{10,11... | collective-permute-start | bytes 983048 | tf_op jit(solution)/shard_map/ppermute | solution.py:232
  19.0 1.6 %collective-permute-start.1 = (bf16[128,1024]{1,0:T(8,128)(2,1)S(1)}, bf16[128,1024]{1,0:T(8,128)(2,1)S(1)}, u32[]{:S(2)}, u32[]{:S(2)}) collective-permute-start(bf16[128,1024]{1,0:T(8,128)(2,1)S(1)} %collective-permute-done.high_ref), channel_id=1, source_target_pairs={{0,2},{1,31},{2,4},{3,1},{4,6},{5,3},{6,8},{7,5},{8,10},{9,7},{10,... | collective-permute-start | bytes 786440 | tf_op jit(solution)/shard_map/ppermute | solution.py:231
  20.5 3.8 %collective-permute-done.6.low_ref = bf16[128,1024]{1,0:T(8,128)(2,1)S(1)} collective-permute-done((bf16[128,1024]{1,0:T(8,128)(2,1)S(1)}, bf16[128,1024]{1,0:T(8,128)(2,1)S(1)}, u32[]{:S(2)}, u32[]{:S(2)}) %collective-permute-start.6) | collective-permute-done | bytes 262176 | tf_op jit(solution)/shard_map/ppermute | solution.py:231
  24.3 1.0 %collective-permute-done.5 = bf16[1536,128]{1,0:T(8,128)(2,1)S(1)} collective-permute-done((bf16[1536,128]{1,0:T(8,128)(2,1)S(1)}, bf16[1536,128]{1,0:T(8,128)(2,1)S(1)}, u32[]{:S(2)}, u32[]{:S(2)}) %collective-permute-start.5) | collective-permute-done | bytes 393248 | tf_op jit(solution)/shard_map/ppermute | solution.py:232
  25.3 2.1 %collective-permute-start.7 = (bf16[2048,128]{1,0:T(8,128)(2,1)S(1)}, bf16[2048,128]{1,0:T(8,128)(2,1)S(1)}, u32[]{:S(2)}, u32[]{:S(2)}) collective-permute-start(bf16[2048,128]{1,0:T(8,128)(2,1)S(1)} %get-tuple-element.46), channel_id=1, source_target_pairs={{0,1},{1,0},{2,3},{3,2},{4,5},{5,4},{6,7},{7,6},{8,9},{9,8},{10,11... | collective-permute-start | bytes 1572872 | tf_op jit(solution)/shard_map/ppermute | solution.py:238
  27.4 1.6 %collective-permute-start.9 = (bf16[1536,128]{1,0:T(8,128)(2,1)S(1)}, bf16[1536,128]{1,0:T(8,128)(2,1)S(1)}, u32[]{:S(2)}, u32[]{:S(2)}) collective-permute-start(bf16[1536,128]{1,0:T(8,128)(2,1)S(1)} %collective-permute-done.5), channel_id=1, source_target_pairs={{0,2},{1,31},{2,4},{3,1},{4,6},{5,3},{6,8},{7,5},{8,10},{9,7},{10,... | collective-permute-start | bytes 1179656 | tf_op jit(solution)/shard_map/ppermute | solution.py:237
  29.0 1.0 %collective-permute-done.1.high_ref = bf16[128,1024]{1,0:T(8,128)(2,1)S(1)} collective-permute-done((bf16[128,1024]{1,0:T(8,128)(2,1)S(1)}, bf16[128,1024]{1,0:T(8,128)(2,1)S(1)}, u32[]{:S(2)}, u32[]{:S(2)}) %collective-permute-start.1) | collective-permute-done | bytes 262176 | tf_op jit(solution)/shard_map/ppermute | solution.py:231
  29.9 2.4 %collective-permute-done.2 = bf16[1280,128]{1,0:T(8,128)(2,1)S(1)} collective-permute-done((bf16[1280,128]{1,0:T(8,128)(2,1)S(1)}, bf16[1280,128]{1,0:T(8,128)(2,1)S(1)}, u32[]{:S(2)}, u32[]{:S(2)}) %collective-permute-start.2) | collective-permute-done | bytes 327712 | tf_op jit(solution)/shard_map/ppermute | solution.py:232
  32.4 2.1 %collective-permute-start.8 = (bf16[1280,128]{1,0:T(8,128)(2,1)S(1)}, bf16[1280,128]{1,0:T(8,128)(2,1)S(1)}, u32[]{:S(2)}, u32[]{:S(2)}) collective-permute-start(bf16[1280,128]{1,0:T(8,128)(2,1)S(1)} %collective-permute-done.2), channel_id=1, source_target_pairs={{0,2},{1,31},{2,4},{3,1},{4,6},{5,3},{6,8},{7,5},{8,10},{9,7},{10,... | collective-permute-start | bytes 983048 | tf_op jit(solution)/shard_map/ppermute | solution.py:237
  34.5 1.9 %collective-permute-start.3 = (bf16[768,128]{1,0:T(8,128)(2,1)S(1)}, bf16[768,128]{1,0:T(8,128)(2,1)S(1)}, u32[]{:S(2)}, u32[]{:S(2)}) collective-permute-start(bf16[768,128]{1,0:T(8,128)(2,1)S(1)} %get-tuple-element.39), channel_id=1, source_target_pairs={{0,1},{1,0},{2,3},{3,2},{4,5},{5,4},{6,7},{7,6},{8,9},{9,8},{10,11... | collective-permute-start | bytes 589832 | tf_op jit(solution)/shard_map/ppermute | solution.py:238
  36.4 0.0 copy-done.3
  36.4 0.0 copy-done.1
  36.4 2.4 %core.1 = (bf16[256,1024]{1,0:T(8,128)(2,1)S(1)}, f32[256,1024]{1,0:T(8,128)S(1)}, f32[256,1024]{1,0:T(8,128)S(1)}, f32[256,1024]{1,0:T(8,128)S(1)}, f32[256,1024]{1,0:T(8,128)S(1)}, /*index=5*/f32[256,1024]{1,0:T(8,128)S(1)}) custom-call(f32[2]{0:T(128)S(1)} %copy-done.3, bf16[768,1024]{1,0:T(8,128)(2,1)S(1)} %copy-done.1, ...), custom_call_target="tpu_custom_call" | custom-call | tf_op jit(solution)/shard_map/core/pallas_call | solution.py:182
  38.8 2.4 %collective-permute-done.9.sent_ref.near_ref = bf16[1536,128]{1,0:T(8,128)(2,1)S(1)} collective-permute-done((bf16[1536,128]{1,0:T(8,128)(2,1)S(1)}, bf16[1536,128]{1,0:T(8,128)(2,1)S(1)}, u32[]{:S(2)}, u32[]{:S(2)}) %collective-permute-start.9) | collective-permute-done | bytes 393248 | tf_op jit(solution)/shard_map/ppermute | solution.py:237
  41.2 0.1 halo.2.halo_ref
  41.3 2.0 %side.4 = (f32[256,1024]{1,0:T(8,128)S(1)}, bf16[768,1024]{1,0:T(8,128)(2,1)}) custom-call(f32[2]{0:T(128)S(1)} %copy-done.3, bf16[768,1024]{1,0:T(8,128)(2,1)S(1)} %copy-done.1, bf16[1536,128]{1,0:T(8,128)(2,1)S(1)} %collective-permute-done.9.sent_ref.near_ref, ...), custom_call_target="tpu_custom_call", output_to_operand_aliasing={{0}: (10, {})} | custom-call | tf_op jit(solution)/shard_map/side/pallas_call | solution.py:182
  43.4 4.8 %collective-permute-done.8.near_ref = bf16[1280,128]{1,0:T(8,128)(2,1)S(1)} collective-permute-done((bf16[1280,128]{1,0:T(8,128)(2,1)S(1)}, bf16[1280,128]{1,0:T(8,128)(2,1)S(1)}, u32[]{:S(2)}, u32[]{:S(2)}) %collective-permute-start.8) | collective-permute-done | bytes 327712 | tf_op jit(solution)/shard_map/ppermute | solution.py:237
  48.2 2.4 %side.5 = (f32[256,1024]{1,0:T(8,128)S(1)}, bf16[768,1024]{1,0:T(8,128)(2,1)}) custom-call(f32[2]{0:T(128)S(1)} %copy-done.3, bf16[768,1024]{1,0:T(8,128)(2,1)S(1)} %copy-done.1, bf16[1280,128]{1,0:T(8,128)(2,1)S(1)} %collective-permute-done.8.near_ref, ...), custom_call_target="tpu_custom_call", output_to_operand_aliasing={{0}: (10, {}), {1}: (11, {})} | custom-call | tf_op jit(solution)/shard_map/side/pallas_call | solution.py:182
  50.6 0.0 collective-permute-done.7.sent_ref.near_ref
  50.6 0.1 halo.3.halo_ref
  50.7 2.5 %side.6.rest_0_ = bf16[768,1024]{1,0:T(8,128)(2,1)} custom-call(f32[2]{0:T(128)S(1)} %copy-done.3, bf16[768,1024]{1,0:T(8,128)(2,1)S(1)} %copy-done.1, bf16[2048,128]{1,0:T(8,128)(2,1)S(1)} %collective-permute-done.7.sent_ref.near_ref, bf16[128,1024]{1,0:T(8,128)(2,1)S(1)} %collective-permute-done.4.low_ref, ...), custom_call_target="tpu_custom_call", output_to_operand_aliasing={{}: (11, {})} | custom-call | tf_op jit(solution)/shard_map/side/pallas_call | solution.py:182
  53.2 0.0 collective-permute-done.3.near_ref
  53.2 2.1 %side.7 = bf16[768,1024]{1,0:T(8,128)(2,1)} custom-call(f32[2]{0:T(128)S(1)} %copy-done.3, bf16[768,1024]{1,0:T(8,128)(2,1)S(1)} %copy-done.1, bf16[768,128]{1,0:T(8,128)(2,1)S(1)} %collective-permute-done.3.near_ref, bf16[128,1024]{1,0:T(8,128)(2,1)S(1)} %collective-permute-done.4.low_ref, ...), custom_call_target="tpu_custom_call", output_to_operand_aliasing={{}: (11, {})} | custom-call | tf_op jit(solution)/shard_map/side/pallas_call | solution.py:182
Async XLA Ops:
  0.0 4.2 %copy-start.2 = (bf16[6,5,128,128]{3,2,1,0:T(8,128)(2,1)S(1)}, bf16[6,5,128,128]{3,2,1,0:T(8,128)(2,1)}, u32[]{:S(2)}) copy-start(bf16[6,5,128,128]{3,2,1,0:T(8,128)(2,1)} %blocks_ref.1) | copy-start | bytes 2949124
  0.0 36.4 %copy-start.3 = (f32[2]{0:T(128)S(1)}, f32[2]{0:T(128)}, u32[]{:S(2)}) copy-start(f32[2]{0:T(128)} %bounds_ref.9) | copy-start | bytes 28
  1.2 10.1 %collective-permute-start.4 = (bf16[128,1024]{1,0:T(8,128)(2,1)S(1)}, bf16[128,1024]{1,0:T(8,128)(2,1)S(1)}, u32[]{:S(2)}, u32[]{:S(2)}) collective-permute-start(bf16[128,1024]{1,0:T(8,128)(2,1)S(1)} %get-tuple-element.63), channel_id=1, source_target_pairs={{0,1},{1,0},{2,3},{3,2},{4,5},{5,4},{6,7},{7,6},{8,9},{9,8},{10,11... | collective-permute-start | bytes 786440 | tf_op jit(solution)/shard_map/ppermute | solution.py:227
  4.2 12.8 %collective-permute-start = (bf16[128,1024]{1,0:T(8,128)(2,1)S(1)}, bf16[128,1024]{1,0:T(8,128)(2,1)S(1)}, u32[]{:S(2)}, u32[]{:S(2)}) collective-permute-start(bf16[128,1024]{1,0:T(8,128)(2,1)S(1)} %get-tuple-element.64), channel_id=1, source_target_pairs={{0,1},{1,0},{2,3},{3,2},{4,5},{5,4},{6,7},{7,6},{8,9},{9,8},{10,11... | collective-permute-start | bytes 786440 | tf_op jit(solution)/shard_map/ppermute | solution.py:227
  4.2 1.4 %copy-start = (bf16[768,1024]{1,0:T(8,128)(2,1)S(1)}, bf16[768,1024]{1,0:T(8,128)(2,1)}, u32[]{:S(2)}) copy-start(bf16[768,1024]{1,0:T(8,128)(2,1)} %v_ref.11) | copy-start | bytes 4718596
  5.7 0.7 %copy-start.4 = (s32[6,5]{1,0:T(8,128)S(1)}, s32[6,5]{1,0:T(8,128)}, u32[]{:S(2)}) copy-start(s32[6,5]{1,0:T(8,128)} %cols_ref.1) | copy-start | bytes 364
  6.3 30.1 %copy-start.1 = (bf16[768,1024]{1,0:T(8,128)(2,1)S(1)}, bf16[768,1024]{1,0:T(8,128)(2,1)}, u32[]{:S(2)}) copy-start(bf16[768,1024]{1,0:T(8,128)(2,1)} %v_ref.11) | copy-start | bytes 4718596
  11.3 14.0 %collective-permute-start.5 = (bf16[1536,128]{1,0:T(8,128)(2,1)S(1)}, bf16[1536,128]{1,0:T(8,128)(2,1)S(1)}, u32[]{:S(2)}, u32[]{:S(2)}) collective-permute-start(bf16[1536,128]{1,0:T(8,128)(2,1)S(1)} %get-tuple-element.43), channel_id=1, source_target_pairs={{0,1},{1,0},{2,3},{3,2},{4,5},{5,4},{6,7},{7,6},{8,9},{9,8},{10,11... | collective-permute-start | bytes 1179656 | tf_op jit(solution)/shard_map/ppermute | solution.py:232
  13.4 11.0 %collective-permute-start.6 = (bf16[128,1024]{1,0:T(8,128)(2,1)S(1)}, bf16[128,1024]{1,0:T(8,128)(2,1)S(1)}, u32[]{:S(2)}, u32[]{:S(2)}) collective-permute-start(bf16[128,1024]{1,0:T(8,128)(2,1)S(1)} %collective-permute-done.4.low_ref), channel_id=1, source_target_pairs={{0,2},{1,31},{2,4},{3,1},{4,6},{5,3},{6,8},{7,5},{8,10},{9,7},{10,... | collective-permute-start | bytes 786440 | tf_op jit(solution)/shard_map/ppermute | solution.py:231
  16.9 15.4 %collective-permute-start.2 = (bf16[1280,128]{1,0:T(8,128)(2,1)S(1)}, bf16[1280,128]{1,0:T(8,128)(2,1)S(1)}, u32[]{:S(2)}, u32[]{:S(2)}) collective-permute-start(bf16[1280,128]{1,0:T(8,128)(2,1)S(1)} %get-tuple-element.36), channel_id=1, source_target_pairs={{0,1},{1,0},{2,3},{3,2},{4,5},{5,4},{6,7},{7,6},{8,9},{9,8},{10,11... | collective-permute-start | bytes 983048 | tf_op jit(solution)/shard_map/ppermute | solution.py:232
  19.0 11.0 %collective-permute-start.1 = (bf16[128,1024]{1,0:T(8,128)(2,1)S(1)}, bf16[128,1024]{1,0:T(8,128)(2,1)S(1)}, u32[]{:S(2)}, u32[]{:S(2)}) collective-permute-start(bf16[128,1024]{1,0:T(8,128)(2,1)S(1)} %collective-permute-done.high_ref), channel_id=1, source_target_pairs={{0,2},{1,31},{2,4},{3,1},{4,6},{5,3},{6,8},{7,5},{8,10},{9,7},{10,... | collective-permute-start | bytes 786440 | tf_op jit(solution)/shard_map/ppermute | solution.py:231
  25.3 25.2 %collective-permute-start.7 = (bf16[2048,128]{1,0:T(8,128)(2,1)S(1)}, bf16[2048,128]{1,0:T(8,128)(2,1)S(1)}, u32[]{:S(2)}, u32[]{:S(2)}) collective-permute-start(bf16[2048,128]{1,0:T(8,128)(2,1)S(1)} %get-tuple-element.46), channel_id=1, source_target_pairs={{0,1},{1,0},{2,3},{3,2},{4,5},{5,4},{6,7},{7,6},{8,9},{9,8},{10,11... | collective-permute-start | bytes 1572872 | tf_op jit(solution)/shard_map/ppermute | solution.py:238
  27.4 13.8 %collective-permute-start.9 = (bf16[1536,128]{1,0:T(8,128)(2,1)S(1)}, bf16[1536,128]{1,0:T(8,128)(2,1)S(1)}, u32[]{:S(2)}, u32[]{:S(2)}) collective-permute-start(bf16[1536,128]{1,0:T(8,128)(2,1)S(1)} %collective-permute-done.5), channel_id=1, source_target_pairs={{0,2},{1,31},{2,4},{3,1},{4,6},{5,3},{6,8},{7,5},{8,10},{9,7},{10,... | collective-permute-start | bytes 1179656 | tf_op jit(solution)/shard_map/ppermute | solution.py:237
  32.4 15.8 %collective-permute-start.8 = (bf16[1280,128]{1,0:T(8,128)(2,1)S(1)}, bf16[1280,128]{1,0:T(8,128)(2,1)S(1)}, u32[]{:S(2)}, u32[]{:S(2)}) collective-permute-start(bf16[1280,128]{1,0:T(8,128)(2,1)S(1)} %collective-permute-done.2), channel_id=1, source_target_pairs={{0,2},{1,31},{2,4},{3,1},{4,6},{5,3},{6,8},{7,5},{8,10},{9,7},{10,... | collective-permute-start | bytes 983048 | tf_op jit(solution)/shard_map/ppermute | solution.py:237
  34.5 18.7 %collective-permute-start.3 = (bf16[768,128]{1,0:T(8,128)(2,1)S(1)}, bf16[768,128]{1,0:T(8,128)(2,1)S(1)}, u32[]{:S(2)}, u32[]{:S(2)}) collective-permute-start(bf16[768,128]{1,0:T(8,128)(2,1)S(1)} %get-tuple-element.39), channel_id=1, source_target_pairs={{0,1},{1,0},{2,3},{3,2},{4,5},{5,4},{6,7},{7,6},{8,9},{9,8},{10,11... | collective-permute-start | bytes 589832 | tf_op jit(solution)/shard_map/ppermute | solution.py:238

commit v2 on v1

v2 whole, which is shorter than its diff:
```python
import functools

import jax
import jax.numpy as jnp
from jax import lax
from jax.experimental import pallas as pl
from jax.experimental.pallas import tpu as pltpu
from jax.sharding import PartitionSpec as P

AXES = ("row", "col")
B = 128
PAIR = 2 * B
HEAD = 5 * B + 16
LIMIT = pltpu.CompilerParams(vmem_limit_bytes=16 * 1024 * 1024)
FREE = pl.CostEstimate(flops=0, bytes_accessed=0, transcendentals=0)
TO_X = ((HEAD, 4), (0, 4))
DIRECT = ((HEAD, 0),)
VIA_X = ((0, 4), (0, 4))


def place():
    return lax.axis_index("row") * lax.axis_size("col") + lax.axis_index("col")


def dot(a, b):
    return jnp.dot(a, b, preferred_element_type=jnp.float32)


def turn(block):
    return block.astype(jnp.float32).T.astype(block.dtype)


def grid():
    return (lax.broadcasted_iota(jnp.int32, (B, B), axis) for axis in (0, 1))


def natural(pair, pairs):
    odd = lax.rem(place(), 2)
    return pl.ds(pl.multiple_of(jnp.where(odd == 1, pairs - 1 - pair, pair) * PAIR, PAIR), PAIR)


def pack_kernel(total_blocks, cols_ref, blocks_ref, v_ref, own_ref, *sent):
    x_refs, d_refs = sent[: len(TO_X)], sent[len(TO_X) :]
    here = place()
    odd = lax.rem(here, 2)
    rows_here, slots = blocks_ref.shape[0], blocks_ref.shape[1]
    pairs = rows_here // 2
    first = here * rows_here
    own_ref[...] = jnp.zeros_like(own_ref)
    for r in range(rows_here):
        j, i = r // 2, r % 2
        row = pl.multiple_of(jnp.where(odd == 1, pairs - 1 - j, j) * PAIR + i * B, B)
        for k in range(slots):
            offset = lax.rem(cols_ref[r, k] - (first + r) + 2 + total_blocks, total_blocks)
            at = offset + i
            turned = (2 - at // 2) * 2 + lax.rem(at, 2)
            col = pl.multiple_of(jnp.where(odd == 1, turned, at) * B, B)
            own_ref[pl.ds(row, B), pl.ds(col, B)] += blocks_ref[r, k]
    last = (pairs - 1) * PAIR
    for out, row, near, mid in ((x_refs[0], last, PAIR, 0), (d_refs[0], 0, PAIR, 2 * PAIR)):
        upper, lower = slice(row, row + B), slice(row + B, row + 2 * B)
        first_block, second = (
            own_ref[rows, near + at : near + at + B].astype(jnp.float32)
            for rows, at in ((upper, 0), (lower, B))
        )
        i, j = grid()
        out[0:B, :] = jnp.where(j >= i, first_block, second).astype(out.dtype)
        diagonal = jnp.sum(jnp.where(i == j, second, 0.0), axis=0, keepdims=True)
        out[5 * B : HEAD, :] = jnp.broadcast_to(diagonal, (HEAD - 5 * B, B)).astype(out.dtype)
        out[B : 2 * B, :] = own_ref[upper, near + B : near + 2 * B]
        out[2 * B : 3 * B, :] = own_ref[upper, mid : mid + B]
        out[3 * B : 4 * B, :] = (
            own_ref[upper, mid + B : mid + 2 * B] + own_ref[lower, mid : mid + B]
        )
        out[4 * B : 5 * B, :] = own_ref[lower, mid + B : mid + 2 * B]
    for refs, layout, edge in ((x_refs, TO_X, pairs - 1), (d_refs, DIRECT + VIA_X, 0)):
        slab = 0
        for ref, (head, slabs) in zip(refs, layout, strict=True):
            for s in range(slabs):
                at = head + s * PAIR
                ref[at : at + PAIR, :] = v_ref[natural(edge, pairs), slab * B : (slab + 1) * B]
                slab += 1


def scales(bounds_ref):
    low, high = bounds_ref[0], bounds_ref[1]
    return 0.5 * (high + low), 0.5 * (high - low)


def core_kernel(bounds_ref, v_ref, own_ref, one_ref, g0_ref, g2_ref, h0_ref, h1_ref, h2_ref):
    pairs = v_ref.shape[0] // PAIR
    center, halfwidth = scales(bounds_ref)
    for at in range(0, v_ref.shape[1], PAIR):
        lanes = slice(at, at + PAIR)
        v0, v1, v2 = (v_ref[natural(j, pairs), lanes] for j in range(3))
        v = jnp.concatenate([v0, v1, v2], axis=0)
        g0_ref[:, lanes] = dot(own_ref[0:PAIR, PAIR:], v[: 2 * PAIR])
        g2_ref[:, lanes] = dot(own_ref[2 * PAIR :, : 2 * PAIR], v[PAIR:])
        image = dot(own_ref[PAIR : 2 * PAIR, :], v)
        one = ((image - center * v1.astype(jnp.float32)) / halfwidth).astype(one_ref.dtype)
        one_ref[:, lanes] = one
        h0_ref[:, lanes] = dot(own_ref[0:PAIR, 2 * PAIR :], one)
        h1_ref[:, lanes] = dot(own_ref[PAIR : 2 * PAIR, PAIR : 2 * PAIR], one)
        h2_ref[:, lanes] = dot(own_ref[2 * PAIR :, 0:PAIR], one)


def halo_kernel(side, own_ref, sent_ref, halo_ref):
    odd = lax.rem(place(), 2)
    halo_ref[...] = jnp.zeros_like(halo_ref)
    if side == 0:
        known, low = own_ref[0:PAIR, 0:PAIR], odd
    else:
        known, low = own_ref[2 * PAIR :, 2 * PAIR :], 1 - odd
    halo_ref[:, 0:PAIR] = turn(known)
    near, far = PAIR, 2 * PAIR
    halves = sent_ref[0:B, :].astype(jnp.float32)
    i, j = grid()
    diagonal = jnp.broadcast_to(sent_ref[5 * B : HEAD, :].astype(jnp.float32)[0:1], (B, B))
    halo_ref[0:B, near : near + B] = jnp.where(j >= i, halves, halves.T).astype(halo_ref.dtype)
    halo_ref[B:PAIR, near + B : near + PAIR] = jnp.where(
        j < i, halves, jnp.where(j > i, halves.T, diagonal)
    ).astype(halo_ref.dtype)
    halo_ref[0:B, near + B : near + PAIR] = sent_ref[B : 2 * B, :]
    halo_ref[B:PAIR, near : near + B] = turn(sent_ref[B : 2 * B, :])
    halo_ref[0:B, far : far + B] = sent_ref[2 * B : 3 * B, :]
    halo_ref[
        pl.ds(pl.multiple_of(low * B, B), B), pl.ds(pl.multiple_of(far + (1 - low) * B, B), B)
    ] = sent_ref[3 * B : 4 * B, :]
    halo_ref[B:PAIR, far + B : far + PAIR] = sent_ref[4 * B : 5 * B, :]


def side_kernel(side, first_slab, layout, bounds_ref, v_ref, own_ref, halo_ref, low_ref, high_ref, *refs):
    near_refs, refs = refs[: len(layout)], refs[len(layout) :]
    if side == 0:
        g_ref, h_ref, h1_ref, h1_out, end_out = refs
    else:
        g_ref, h_ref, h1_ref, one_ref, zero_ref = refs[:5]
        out_ref, end_ref, mid_ref, sems = refs[-4:]
    pairs = v_ref.shape[0] // PAIR
    center, halfwidth = scales(bounds_ref)
    edge = 0 if side == 0 else 2
    rows = slice(edge * PAIR, (edge + 1) * PAIR)
    outward = slice(0, PAIR) if side == 0 else slice(2 * PAIR, 3 * PAIR)
    slabs = [
        near_ref[head + s * PAIR : head + (s + 1) * PAIR, :]
        for near_ref, (head, count) in zip(near_refs, layout, strict=True)
        for s in range(count)
    ]
    width = len(slabs) * B
    all_lanes = slice(first_slab * B, first_slab * B + width)
    copies = []
    if side == 1:
        copies = [
            pltpu.make_async_copy(source, out_ref.at[natural(pair, pairs), all_lanes], sems.at[pair])
            for pair, source in enumerate((zero_ref, mid_ref, end_ref))
        ]
        copies[0].start()
    for at in range(0, width, PAIR):
        lanes = slice(first_slab * B + at, first_slab * B + at + PAIR)
        here = slice(at, at + PAIR)
        near = jnp.concatenate(slabs[at // B : at // B + 2], axis=1)
        v = v_ref[natural(edge, pairs), lanes]
        stack = jnp.concatenate([v, near, low_ref[:, lanes], high_ref[:, lanes]], axis=0)
        v32 = v.astype(jnp.float32)
        image = g_ref[:, lanes] + dot(own_ref[rows, outward], near)
        edge_one = ((image - center * v32) / halfwidth).astype(v.dtype)
        image = dot(halo_ref[...], stack)
        near_one = ((image - center * near.astype(jnp.float32)) / halfwidth).astype(v.dtype)
        h1 = dot(own_ref[PAIR : 2 * PAIR, outward], edge_one)
        if side == 0:
            h1_out[:, here] = h1_ref[:, lanes] + h1
        else:
            h1 += h1_ref[:, here]
            one = one_ref[:, lanes].astype(jnp.float32)
            v1 = v_ref[natural(1, pairs), lanes].astype(jnp.float32)
            mid_ref[:, here] = (2.0 * ((h1 - center * one) / halfwidth) - v1).astype(v.dtype)
        image = h_ref[:, lanes] + (
            dot(own_ref[rows, PAIR : 2 * PAIR], edge_one) + dot(own_ref[rows, outward], near_one)
        )
        end = (2.0 * ((image - center * edge_one.astype(jnp.float32)) / halfwidth) - v32).astype(v.dtype)
        if side == 0:
            end_out[:, here] = end
        else:
            end_ref[:, here] = end
    for copy in copies[1:]:
        copy.start()
    for copy in copies:
        copy.wait()


def whole(ref_space=pltpu.VMEM):
    return pl.BlockSpec(memory_space=ref_space)


def call(body, outs, args, name, aliases=None, scratch=()):
    aliases = aliases or {}

    def in_hbm(out):
        return isinstance(out, jax.ShapeDtypeStruct)

    spaces = [
        pltpu.SMEM
        if a.size < 1024
        else pl.ANY
        if i in aliases and in_hbm(outs[aliases[i]])
        else pltpu.VMEM
        for i, a in enumerate(args)
    ]
    return pl.pallas_call(
        body,
        out_shape=outs,
        in_specs=[whole(space) for space in spaces],
        out_specs=[whole(pl.ANY if in_hbm(out) else pltpu.VMEM) for out in outs],
        scratch_shapes=scratch,
        input_output_aliases=aliases,
        compiler_params=LIMIT,
        cost_estimate=FREE,
        name=name,
    )(
        *(
            pltpu.with_memory_space_constraint(a, pltpu.VMEM) if space == pltpu.VMEM else a
            for a, space in zip(args, spaces, strict=True)
        )
    )


def after(token, value):
    return lax.optimization_barrier((token, value))


def per_device(vectors, ham_blocks, ham_columns, bounds):
    rows, vec_width = vectors.shape
    rows_here = ham_blocks.shape[0]
    ring = lax.axis_size(AXES)
    dtype = vectors.dtype
    over_x = [(i, i ^ 1) for i in range(ring)]
    direct = [(i, (i + 1) % ring if i % 2 else (i - 1) % ring) for i in range(ring)]
    onward = [(i, (i - 2) % ring if i % 2 else (i + 2) % ring) for i in range(ring)]

    def send(part, perm):
        return lax.ppermute(part, AXES, perm)

    middle = [lax.slice_in_dim(vectors, rows // 2 + at, rows // 2 + at + B, axis=0) for at in (-B, 0)]
    own, *parts = call(
        functools.partial(pack_kernel, ring * rows_here),
        [pltpu.VMEM((rows, 3 * PAIR), dtype)]
        + [
            pltpu.VMEM((head + slabs * PAIR, B), dtype) for head, slabs in TO_X + DIRECT + VIA_X
        ],
        [ham_columns, ham_blocks, vectors],
        "pack",
    )
    to_x, parts = parts[: len(TO_X)], parts[len(TO_X) :]
    to_d, via_x = parts[: len(DIRECT)], parts[len(DIRECT) :]

    far_x = [send(part, over_x) for part in middle]
    near_d = [send(part, direct) for part in to_d]
    far_x[0], via_x[0] = after(far_x[0], via_x[0])
    far_x[1], via_x[1] = after(far_x[1], via_x[1])
    far_d = [send(part, onward) for part in far_x]
    passing = [send(part, over_x) for part in via_x]
    far_d[0], to_x[0] = after(far_d[0], to_x[0])
    near_d[0], to_x[0] = after(near_d[0], to_x[0])
    passing[0], to_x[0] = after(passing[0], to_x[0])
    far_d[1], passing[1] = after(far_d[1], passing[1])
    passing[1], to_x[1] = after(passing[1], to_x[1])
    near_d += [send(part, onward) for part in passing]
    near_x = [send(part, over_x) for part in to_x]

    wide = lambda kind: pltpu.VMEM((PAIR, vec_width), kind)
    one, g0, g2, h0, h1, h2 = call(
        core_kernel, [wide(dtype)] + [wide(jnp.float32)] * 5, [bounds, vectors, own], "core"
    )
    band = [pltpu.VMEM((PAIR, 3 * PAIR), dtype)]
    (halo_d,) = call(functools.partial(halo_kernel, 0), band, [own, near_d[0]], "halo_d")
    result = None
    first_slab = 0
    for c, (head, slabs) in enumerate(TO_X):
        if c == 0:
            layout, near = (DIRECT + VIA_X)[:2], near_d[:2]
        else:
            layout, near = VIA_X[c : c + 1], near_d[c + 1 : c + 2]
            near[0], result = after(near[0], result)
        chunk = lambda kind, slabs=slabs: pltpu.VMEM((PAIR, slabs * B), kind)
        mid, zero = call(
            functools.partial(side_kernel, 0, first_slab, layout),
            [chunk(jnp.float32), chunk(dtype)],
            [bounds, vectors, own, halo_d, *far_d, *near, g0, h0, h1],
            "side_d",
        )
        near_x[c], zero = after(near_x[c], zero)
        if c == 0:
            (halo_x,) = call(functools.partial(halo_kernel, 1), band, [own, near_x[0]], "halo_x")
        args = [bounds, vectors, own, halo_x, *far_x, near_x[c], g2, h2, mid, one, zero]
        aliases = {}
        if result is not None:
            aliases[len(args)] = 0
            args.append(result)
        (result,) = call(
            functools.partial(side_kernel, 1, first_slab, ((head, slabs),)),
            [jax.ShapeDtypeStruct((rows, vec_width), dtype)],
            args,
            "side_x",
            aliases=aliases,
            scratch=[chunk(dtype)] * 2 + [pltpu.SemaphoreType.DMA((3,))],
        )
        first_slab += slabs
    return result


def solution(mesh):
    return jax.shard_map(
        per_device,
        mesh=mesh,
        in_specs=(P(AXES, None), P(AXES, None, None, None), P(AXES, None), P()),
        out_specs=P(AXES, None),
        check_vma=False,
    )
```

time: 55.5 us -> 48.8 us (0.88)
  waiting for transfers between devices: 21 us -> 9.33 us
  starting transfers between devices: 18 us -> 23.8 us
  Pallas kernels: 12.9 us -> 12.1 us
    ppermute x10 -> x11, waiting for transfers between devices: 21 us -> 9.33 us  [send(): return lax.ppermute(part, AXES, perm)]
    ppermute x10 -> x11, starting transfers between devices: 18 us -> 23.8 us  [send(): return lax.ppermute(part, AXES, perm)]
    pallas_call x8, Pallas kernels: 12.9 us -> 12.1 us  [call(): pl.pallas_call(body, out_shape=outs, in_specs=[whole(space) for space in...]
  transfers between devices with their start and end apart: 10 -> 11, of which waited for: 8 -> 6; matrix products, arithmetic and copies ran while one was open for 0% -> 0% of each run, Pallas kernels for 20% -> 20%
where the time goes in v2:
time: 48.8 us; the launch traced here: 48.6 us
  starting transfers between devices  23.8 us (49%)
  Pallas kernels  12.1 us (25%)
  waiting for transfers between devices  9.33 us (19%)
  local copies, waits for them, and re-layouts  3.25 us (7%)
    ppermute x11, starting transfers between devices, send(): return lax.ppermute(part, AXES, perm)  23.8 us
    pallas_call x8, Pallas kernels, call(): pl.pallas_call(body, out_shape=outs, in_specs=[whole(space) for space in...  12.1 us
    ppermute x11, waiting for transfers between devices, send(): return lax.ppermute(part, AXES, perm)  9.33 us
    unnamed x10, local copies, waits for them, and re-layouts  2.11 us
    slice x1, local copies, waits for them, and re-layouts, per_device(): lax.slice_in_dim(vectors, rows // 2 + at, rows // 2 + at + B, axis=0)  1.15 us
  transfers between devices with their start and end apart: 11, of which 6 were waited for; matrix products, arithmetic and copies ran while one was open for 0% of the time, Pallas kernels for 20%

profile of v2, /device:TPU:0, one launch (start us, length us, event | category | flops | bytes accessed | tf_op | source)
XLA Modules:
  0.0 48.6 jit_solution(8482231262247681731)
XLA Ops:
  0.0 0.0 copy-start.2
  0.0 0.0 copy-start.3
  0.0 1.1 %fusion = (bf16[128,1024]{1,0:T(8,128)(2,1)S(1)}, bf16[128,1024]{1,0:T(8,128)(2,1)S(1)}) fusion(bf16[768,1024]{1,0:T(8,128)(2,1)} %v_ref.11), kind=kLoop, calls=%fused_computation | loop fusion | bytes 1048576 | tf_op jit(solution)/shard_map/slice | solution.py:243
  1.2 3.0 %collective-permute-start = (bf16[128,1024]{1,0:T(8,128)(2,1)S(1)}, bf16[128,1024]{1,0:T(8,128)(2,1)S(1)}, u32[]{:S(2)}, u32[]{:S(2)}) collective-permute-start(bf16[128,1024]{1,0:T(8,128)(2,1)S(1)} %get-tuple-element.78), channel_id=1, source_target_pairs={{0,1},{1,0},{2,3},{3,2},{4,5},{5,4},{6,7},{7,6},{8,9},{9,8},{10,11... | collective-permute-start | bytes 786440 | tf_op jit(solution)/shard_map/ppermute | solution.py:241
  4.2 0.1 collective-permute-start.5
  4.2 0.0 copy-done.2
  4.2 0.0 copy-start
  4.2 1.4 %copy-done = bf16[768,1024]{1,0:T(8,128)(2,1)S(1)} copy-done((bf16[768,1024]{1,0:T(8,128)(2,1)S(1)}, bf16[768,1024]{1,0:T(8,128)(2,1)}, u32[]{:S(2)}) %copy-start) | copy-done | bytes 1572888
  5.7 0.0 copy-start.4
  5.7 0.7 %copy-done.4 = s32[6,5]{1,0:T(8,128)S(1)} copy-done((s32[6,5]{1,0:T(8,128)S(1)}, s32[6,5]{1,0:T(8,128)}, u32[]{:S(2)}) %copy-start.4) | copy-done | bytes 144
  6.3 0.0 copy-start.1
  6.3 1.3 %pack.1 = (bf16[768,768]{1,0:T(8,128)(2,1)S(1)}, bf16[1680,128]{1,0:T(8,128)(2,1)S(1)}, bf16[1024,128]{1,0:T(8,128)(2,1)S(1)}, bf16[656,128]{1,0:T(8,128)(2,1)S(...) custom-call(s32[6,5]{1,0:T(8,128)S(1)} %copy-done.4, bf16[6,5,128,128]{3,2,1,0:T(8,128)(2,1)S(1)} %copy-done.2, ...), custom_call_target="tpu_custom_call" | custom-call | tf_op jit(solution)/shard_map/pack/pallas_call | solution.py:209
  7.6 3.7 %collective-permute-done.low_ref = bf16[128,1024]{1,0:T(8,128)(2,1)S(1)} collective-permute-done((bf16[128,1024]{1,0:T(8,128)(2,1)S(1)}, bf16[128,1024]{1,0:T(8,128)(2,1)S(1)}, u32[]{:S(2)}, u32[]{:S(2)}) %collective-permute-start) | collective-permute-done | bytes 262176 | tf_op jit(solution)/shard_map/ppermute | solution.py:241
  11.3 2.1 %collective-permute-start.3 = (bf16[128,1024]{1,0:T(8,128)(2,1)S(1)}, bf16[128,1024]{1,0:T(8,128)(2,1)S(1)}, u32[]{:S(2)}, u32[]{:S(2)}) collective-permute-start(bf16[128,1024]{1,0:T(8,128)(2,1)S(1)} %collective-permute-done.low_ref), channel_id=1, source_target_pairs={{0,2},{1,31},{2,4},{3,1},{4,6},{5,3},{6,8},{7,5},{8,10},{9,7},{10,... | collective-permute-start | bytes 786440 | tf_op jit(solution)/shard_map/ppermute | solution.py:241
  13.4 1.9 %collective-permute-start.1 = (bf16[1024,128]{1,0:T(8,128)(2,1)S(1)}, bf16[1024,128]{1,0:T(8,128)(2,1)S(1)}, u32[]{:S(2)}, u32[]{:S(2)}) collective-permute-start(bf16[1024,128]{1,0:T(8,128)(2,1)S(1)} %get-tuple-element.43), channel_id=1, source_target_pairs={{0,1},{1,0},{2,3},{3,2},{4,5},{5,4},{6,7},{7,6},{8,9},{9,8},{10,11... | collective-permute-start | bytes 786440 | tf_op jit(solution)/shard_map/ppermute | solution.py:241
  15.3 1.6 %collective-permute-start.2 = (bf16[656,128]{1,0:T(8,128)(2,1)S(1)}, bf16[656,128]{1,0:T(8,128)(2,1)S(1)}, u32[]{:S(2)}, u32[]{:S(2)}) collective-permute-start(bf16[656,128]{1,0:T(8,128)(2,1)S(1)} %get-tuple-element.44), channel_id=1, source_target_pairs={{0,31},{1,2},{2,1},{3,4},{4,3},{5,6},{6,5},{7,8},{8,7},{9,10},{10,... | collective-permute-start | bytes 503816 | tf_op jit(solution)/shard_map/ppermute | solution.py:241
  16.9 0.0 collective-permute-done.5.high_ref
  16.9 0.9 %collective-permute-start.7 = (bf16[1024,128]{1,0:T(8,128)(2,1)S(1)}, bf16[1024,128]{1,0:T(8,128)(2,1)S(1)}, u32[]{:S(2)}, u32[]{:S(2)}) collective-permute-start(bf16[1024,128]{1,0:T(8,128)(2,1)S(1)} %get-tuple-element.54), channel_id=1, source_target_pairs={{0,1},{1,0},{2,3},{3,2},{4,5},{5,4},{6,7},{7,6},{8,9},{9,8},{10,11... | collective-permute-start | bytes 786440 | tf_op jit(solution)/shard_map/ppermute | solution.py:241
  17.8 4.0 %collective-permute-start.6 = (bf16[128,1024]{1,0:T(8,128)(2,1)S(1)}, bf16[128,1024]{1,0:T(8,128)(2,1)S(1)}, u32[]{:S(2)}, u32[]{:S(2)}) collective-permute-start(bf16[128,1024]{1,0:T(8,128)(2,1)S(1)} %collective-permute-done.5.high_ref), channel_id=1, source_target_pairs={{0,2},{1,31},{2,4},{3,1},{4,6},{5,3},{6,8},{7,5},{8,10},{9,7},{10,... | collective-permute-start | bytes 786440 | tf_op jit(solution)/shard_map/ppermute | solution.py:241
  21.8 0.0 collective-permute-done.3.low_ref
  21.8 2.6 %collective-permute-done.2.sent_ref.refs_0_ = bf16[656,128]{1,0:T(8,128)(2,1)S(1)} collective-permute-done((bf16[656,128]{1,0:T(8,128)(2,1)S(1)}, bf16[656,128]{1,0:T(8,128)(2,1)S(1)}, u32[]{:S(2)}, u32[]{:S(2)}) %collective-permute-start.2) | collective-permute-done | bytes 167968 | tf_op jit(solution)/shard_map/ppermute | solution.py:241
  24.4 0.0 collective-permute-done.1
  24.4 3.9 %collective-permute-start.4 = (bf16[1680,128]{1,0:T(8,128)(2,1)S(1)}, bf16[1680,128]{1,0:T(8,128)(2,1)S(1)}, u32[]{:S(2)}, u32[]{:S(2)}) collective-permute-start(bf16[1680,128]{1,0:T(8,128)(2,1)S(1)} %get-tuple-element.49), channel_id=1, source_target_pairs={{0,1},{1,0},{2,3},{3,2},{4,5},{5,4},{6,7},{7,6},{8,9},{9,8},{10,11... | collective-permute-start | bytes 1290248 | tf_op jit(solution)/shard_map/ppermute | solution.py:241
  28.3 1.5 %collective-permute-start.8 = (bf16[1024,128]{1,0:T(8,128)(2,1)S(1)}, bf16[1024,128]{1,0:T(8,128)(2,1)S(1)}, u32[]{:S(2)}, u32[]{:S(2)}) collective-permute-start(bf16[1024,128]{1,0:T(8,128)(2,1)S(1)} %collective-permute-done.1), channel_id=1, source_target_pairs={{0,2},{1,31},{2,4},{3,1},{4,6},{5,3},{6,8},{7,5},{8,10},{9,7},{10,... | collective-permute-start | bytes 786440 | tf_op jit(solution)/shard_map/ppermute | solution.py:241
  29.8 1.2 %collective-permute-done.7 = bf16[1024,128]{1,0:T(8,128)(2,1)S(1)} collective-permute-done((bf16[1024,128]{1,0:T(8,128)(2,1)S(1)}, bf16[1024,128]{1,0:T(8,128)(2,1)S(1)}, u32[]{:S(2)}, u32[]{:S(2)}) %collective-permute-start.7) | collective-permute-done | bytes 262176 | tf_op jit(solution)/shard_map/ppermute | solution.py:241
  30.9 0.1 collective-permute-done.6.high_ref
  31.0 2.9 %collective-permute-start.10 = (bf16[1024,128]{1,0:T(8,128)(2,1)S(1)}, bf16[1024,128]{1,0:T(8,128)(2,1)S(1)}, u32[]{:S(2)}, u32[]{:S(2)}) collective-permute-start(bf16[1024,128]{1,0:T(8,128)(2,1)S(1)} %collective-permute-done.7), channel_id=1, source_target_pairs={{0,2},{1,31},{2,4},{3,1},{4,6},{5,3},{6,8},{7,5},{8,10},{9,7},{10,... | collective-permute-start | bytes 786440 | tf_op jit(solution)/shard_map/ppermute | solution.py:241
  33.9 1.9 %collective-permute-start.9 = (bf16[1024,128]{1,0:T(8,128)(2,1)S(1)}, bf16[1024,128]{1,0:T(8,128)(2,1)S(1)}, u32[]{:S(2)}, u32[]{:S(2)}) collective-permute-start(bf16[1024,128]{1,0:T(8,128)(2,1)S(1)} %get-tuple-element.64), channel_id=1, source_target_pairs={{0,1},{1,0},{2,3},{3,2},{4,5},{5,4},{6,7},{7,6},{8,9},{9,8},{10,11... | collective-permute-start | bytes 786440 | tf_op jit(solution)/shard_map/ppermute | solution.py:241
  35.8 0.0 copy-done.3
  35.8 0.0 copy-done.1
  35.8 2.4 %core.1 = (bf16[256,1024]{1,0:T(8,128)(2,1)S(1)}, f32[256,1024]{1,0:T(8,128)S(1)}, f32[256,1024]{1,0:T(8,128)S(1)}, f32[256,1024]{1,0:T(8,128)S(1)}, f32[256,1024]{1,0:T(8,128)S(1)}, /*index=5*/f32[256,1024]{1,0:T(8,128)S(1)}) custom-call(f32[2]{0:T(128)S(1)} %copy-done.3, bf16[768,1024]{1,0:T(8,128)(2,1)S(1)} %copy-done.1, ...), custom_call_target="tpu_custom_call" | custom-call | tf_op jit(solution)/shard_map/core/pallas_call | solution.py:209
  38.2 0.1 halo_d.1.halo_ref
  38.4 0.5 %collective-permute-done.8.refs_1_ = bf16[1024,128]{1,0:T(8,128)(2,1)S(1)} collective-permute-done((bf16[1024,128]{1,0:T(8,128)(2,1)S(1)}, bf16[1024,128]{1,0:T(8,128)(2,1)S(1)}, u32[]{:S(2)}, u32[]{:S(2)}) %collective-permute-start.8) | collective-permute-done | bytes 262176 | tf_op jit(solution)/shard_map/ppermute | solution.py:241
  38.9 1.7 %side_d.2 = (f32[256,512]{1,0:T(8,128)S(1)}, bf16[256,512]{1,0:T(8,128)(2,1)S(1)}) custom-call(f32[2]{0:T(128)S(1)} %copy-done.3, bf16[768,1024]{1,0:T(8,128)(2,1)S(1)} %copy-done.1, bf16[768,768]{1,0:T(8,128)(2,1)S(1)} %get-tuple-element.41.own_ref, bf16[256,768]{1,0:T(8,128)(2,1)S(1)} %halo_d.1.halo_ref, ...), custom_call_target="tpu_custom_call" | custom-call | tf_op jit(solution)/shard_map/side_d/pallas_call | solution.py:209
  40.5 0.0 collective-permute-done.4.sent_ref.refs_0_
  40.6 0.1 halo_x.1.halo_ref
  40.7 2.4 %side_x.2.refs_6_ = bf16[768,1024]{1,0:T(8,128)(2,1)} custom-call(f32[2]{0:T(128)S(1)} %copy-done.3, bf16[768,1024]{1,0:T(8,128)(2,1)S(1)} %copy-done.1, bf16[768,768]{1,0:T(8,128)(2,1)S(1)} %get-tuple-element.41.own_ref, bf16[256,768]{1,0:T(8,128)(2,1)S(1)} %halo_x.1.halo_ref, bf16[128,1024]{1,0:T(8,128)(2,1)S(1)} %collective-permute-done.low_ref, ...), custom_call_target="tpu_custom_call" | custom-call | tf_op jit(solution)/shard_map/side_x/pallas_call | solution.py:209
  43.1 1.3 %collective-permute-done.10.refs_0_ = bf16[1024,128]{1,0:T(8,128)(2,1)S(1)} collective-permute-done((bf16[1024,128]{1,0:T(8,128)(2,1)S(1)}, bf16[1024,128]{1,0:T(8,128)(2,1)S(1)}, u32[]{:S(2)}, u32[]{:S(2)}) %collective-permute-start.10) | collective-permute-done | bytes 262176 | tf_op jit(solution)/shard_map/ppermute | solution.py:241
  44.5 1.7 %side_d.3 = (f32[256,512]{1,0:T(8,128)S(1)}, bf16[256,512]{1,0:T(8,128)(2,1)S(1)}) custom-call(f32[2]{0:T(128)S(1)} %copy-done.3, bf16[768,1024]{1,0:T(8,128)(2,1)S(1)} %copy-done.1, bf16[768,768]{1,0:T(8,128)(2,1)S(1)} %get-tuple-element.41.own_ref, bf16[256,768]{1,0:T(8,128)(2,1)S(1)} %halo_d.1.halo_ref, ...), custom_call_target="tpu_custom_call" | custom-call | tf_op jit(solution)/shard_map/side_d/pallas_call | solution.py:209
  46.2 0.0 collective-permute-done.9.refs_0_
  46.2 2.4 %side_x.3 = bf16[768,1024]{1,0:T(8,128)(2,1)} custom-call(f32[2]{0:T(128)S(1)} %copy-done.3, bf16[768,1024]{1,0:T(8,128)(2,1)S(1)} %copy-done.1, bf16[768,768]{1,0:T(8,128)(2,1)S(1)} %get-tuple-element.41.own_ref, bf16[256,768]{1,0:T(8,128)(2,1)S(1)} %halo_x.1.halo_ref, ...), custom_call_target="tpu_custom_call", output_to_operand_aliasing={{}: (12, {})} | custom-call | tf_op jit(solution)/shard_map/side_x/pallas_call | solution.py:209
Async XLA Ops:
  0.0 4.2 %copy-start.2 = (bf16[6,5,128,128]{3,2,1,0:T(8,128)(2,1)S(1)}, bf16[6,5,128,128]{3,2,1,0:T(8,128)(2,1)}, u32[]{:S(2)}) copy-start(bf16[6,5,128,128]{3,2,1,0:T(8,128)(2,1)} %blocks_ref.1) | copy-start | bytes 2949124
  0.0 35.8 %copy-start.3 = (f32[2]{0:T(128)S(1)}, f32[2]{0:T(128)}, u32[]{:S(2)}) copy-start(f32[2]{0:T(128)} %bounds_ref.9) | copy-start | bytes 28
  1.2 10.1 %collective-permute-start = (bf16[128,1024]{1,0:T(8,128)(2,1)S(1)}, bf16[128,1024]{1,0:T(8,128)(2,1)S(1)}, u32[]{:S(2)}, u32[]{:S(2)}) collective-permute-start(bf16[128,1024]{1,0:T(8,128)(2,1)S(1)} %get-tuple-element.78), channel_id=1, source_target_pairs={{0,1},{1,0},{2,3},{3,2},{4,5},{5,4},{6,7},{7,6},{8,9},{9,8},{10,11... | collective-permute-start | bytes 786440 | tf_op jit(solution)/shard_map/ppermute | solution.py:241
  4.2 12.8 %collective-permute-start.5 = (bf16[128,1024]{1,0:T(8,128)(2,1)S(1)}, bf16[128,1024]{1,0:T(8,128)(2,1)S(1)}, u32[]{:S(2)}, u32[]{:S(2)}) collective-permute-start(bf16[128,1024]{1,0:T(8,128)(2,1)S(1)} %get-tuple-element.77), channel_id=1, source_target_pairs={{0,1},{1,0},{2,3},{3,2},{4,5},{5,4},{6,7},{7,6},{8,9},{9,8},{10,11... | collective-permute-start | bytes 786440 | tf_op jit(solution)/shard_map/ppermute | solution.py:241
  4.2 1.4 %copy-start = (bf16[768,1024]{1,0:T(8,128)(2,1)S(1)}, bf16[768,1024]{1,0:T(8,128)(2,1)}, u32[]{:S(2)}) copy-start(bf16[768,1024]{1,0:T(8,128)(2,1)} %v_ref.11) | copy-start | bytes 4718596
  5.7 0.7 %copy-start.4 = (s32[6,5]{1,0:T(8,128)S(1)}, s32[6,5]{1,0:T(8,128)}, u32[]{:S(2)}) copy-start(s32[6,5]{1,0:T(8,128)} %cols_ref.1) | copy-start | bytes 364
  6.3 29.5 %copy-start.1 = (bf16[768,1024]{1,0:T(8,128)(2,1)S(1)}, bf16[768,1024]{1,0:T(8,128)(2,1)}, u32[]{:S(2)}) copy-start(bf16[768,1024]{1,0:T(8,128)(2,1)} %v_ref.11) | copy-start | bytes 4718596
  11.3 10.6 %collective-permute-start.3 = (bf16[128,1024]{1,0:T(8,128)(2,1)S(1)}, bf16[128,1024]{1,0:T(8,128)(2,1)S(1)}, u32[]{:S(2)}, u32[]{:S(2)}) collective-permute-start(bf16[128,1024]{1,0:T(8,128)(2,1)S(1)} %collective-permute-done.low_ref), channel_id=1, source_target_pairs={{0,2},{1,31},{2,4},{3,1},{4,6},{5,3},{6,8},{7,5},{8,10},{9,7},{10,... | collective-permute-start | bytes 786440 | tf_op jit(solution)/shard_map/ppermute | solution.py:241
  13.4 11.0 %collective-permute-start.1 = (bf16[1024,128]{1,0:T(8,128)(2,1)S(1)}, bf16[1024,128]{1,0:T(8,128)(2,1)S(1)}, u32[]{:S(2)}, u32[]{:S(2)}) collective-permute-start(bf16[1024,128]{1,0:T(8,128)(2,1)S(1)} %get-tuple-element.43), channel_id=1, source_target_pairs={{0,1},{1,0},{2,3},{3,2},{4,5},{5,4},{6,7},{7,6},{8,9},{9,8},{10,11... | collective-permute-start | bytes 786440 | tf_op jit(solution)/shard_map/ppermute | solution.py:241
  15.3 9.1 %collective-permute-start.2 = (bf16[656,128]{1,0:T(8,128)(2,1)S(1)}, bf16[656,128]{1,0:T(8,128)(2,1)S(1)}, u32[]{:S(2)}, u32[]{:S(2)}) collective-permute-start(bf16[656,128]{1,0:T(8,128)(2,1)S(1)} %get-tuple-element.44), channel_id=1, source_target_pairs={{0,31},{1,2},{2,1},{3,4},{4,3},{5,6},{6,5},{7,8},{8,7},{9,10},{10,... | collective-permute-start | bytes 503816 | tf_op jit(solution)/shard_map/ppermute | solution.py:241
  16.9 14.0 %collective-permute-start.7 = (bf16[1024,128]{1,0:T(8,128)(2,1)S(1)}, bf16[1024,128]{1,0:T(8,128)(2,1)S(1)}, u32[]{:S(2)}, u32[]{:S(2)}) collective-permute-start(bf16[1024,128]{1,0:T(8,128)(2,1)S(1)} %get-tuple-element.54), channel_id=1, source_target_pairs={{0,1},{1,0},{2,3},{3,2},{4,5},{5,4},{6,7},{7,6},{8,9},{9,8},{10,11... | collective-permute-start | bytes 786440 | tf_op jit(solution)/shard_map/ppermute | solution.py:241
  17.8 13.2 %collective-permute-start.6 = (bf16[128,1024]{1,0:T(8,128)(2,1)S(1)}, bf16[128,1024]{1,0:T(8,128)(2,1)S(1)}, u32[]{:S(2)}, u32[]{:S(2)}) collective-permute-start(bf16[128,1024]{1,0:T(8,128)(2,1)S(1)} %collective-permute-done.5.high_ref), channel_id=1, source_target_pairs={{0,2},{1,31},{2,4},{3,1},{4,6},{5,3},{6,8},{7,5},{8,10},{9,7},{10,... | collective-permute-start | bytes 786440 | tf_op jit(solution)/shard_map/ppermute | solution.py:241
  24.4 16.1 %collective-permute-start.4 = (bf16[1680,128]{1,0:T(8,128)(2,1)S(1)}, bf16[1680,128]{1,0:T(8,128)(2,1)S(1)}, u32[]{:S(2)}, u32[]{:S(2)}) collective-permute-start(bf16[1680,128]{1,0:T(8,128)(2,1)S(1)} %get-tuple-element.49), channel_id=1, source_target_pairs={{0,1},{1,0},{2,3},{3,2},{4,5},{5,4},{6,7},{7,6},{8,9},{9,8},{10,11... | collective-permute-start | bytes 1290248 | tf_op jit(solution)/shard_map/ppermute | solution.py:241
  28.3 10.6 %collective-permute-start.8 = (bf16[1024,128]{1,0:T(8,128)(2,1)S(1)}, bf16[1024,128]{1,0:T(8,128)(2,1)S(1)}, u32[]{:S(2)}, u32[]{:S(2)}) collective-permute-start(bf16[1024,128]{1,0:T(8,128)(2,1)S(1)} %collective-permute-done.1), channel_id=1, source_target_pairs={{0,2},{1,31},{2,4},{3,1},{4,6},{5,3},{6,8},{7,5},{8,10},{9,7},{10,... | collective-permute-start | bytes 786440 | tf_op jit(solution)/shard_map/ppermute | solution.py:241
  31.0 13.5 %collective-permute-start.10 = (bf16[1024,128]{1,0:T(8,128)(2,1)S(1)}, bf16[1024,128]{1,0:T(8,128)(2,1)S(1)}, u32[]{:S(2)}, u32[]{:S(2)}) collective-permute-start(bf16[1024,128]{1,0:T(8,128)(2,1)S(1)} %collective-permute-done.7), channel_id=1, source_target_pairs={{0,2},{1,31},{2,4},{3,1},{4,6},{5,3},{6,8},{7,5},{8,10},{9,7},{10,... | collective-permute-start | bytes 786440 | tf_op jit(solution)/shard_map/ppermute | solution.py:241
  33.9 12.3 %collective-permute-start.9 = (bf16[1024,128]{1,0:T(8,128)(2,1)S(1)}, bf16[1024,128]{1,0:T(8,128)(2,1)S(1)}, u32[]{:S(2)}, u32[]{:S(2)}) collective-permute-start(bf16[1024,128]{1,0:T(8,128)(2,1)S(1)} %get-tuple-element.64), channel_id=1, source_target_pairs={{0,1},{1,0},{2,3},{3,2},{4,5},{5,4},{6,7},{7,6},{8,9},{9,8},{10,11... | collective-permute-start | bytes 786440 | tf_op jit(solution)/shard_map/ppermute | solution.py:241

commit v3 on v2

--- a/solution.py
+++ b/solution.py
@@ -10,6 +10,7 @@
 AXES = ("row", "col")
 B = 128
 PAIR = 2 * B
+STEP = 4 * B
 HEAD = 5 * B + 16
 LIMIT = pltpu.CompilerParams(vmem_limit_bytes=16 * 1024 * 1024)
 FREE = pl.CostEstimate(flops=0, bytes_accessed=0, transcendentals=0)
@@ -39,7 +40,10 @@
     return pl.ds(pl.multiple_of(jnp.where(odd == 1, pairs - 1 - pair, pair) * PAIR, PAIR), PAIR)
 
 
-def pack_kernel(total_blocks, cols_ref, blocks_ref, v_ref, own_ref, *sent):
+def pack_kernel(total_blocks, cols_ref, bounds_ref, blocks_ref, v_ref, scales_ref, own_ref, *sent):
+    low, high = bounds_ref[0], bounds_ref[1]
+    scales_ref[0:1, :] = jnp.full((1, B), 0.5 * (high + low), jnp.float32)
+    scales_ref[1:2, :] = jnp.full((1, B), 0.5 * (high - low), jnp.float32)
     x_refs, d_refs = sent[: len(TO_X)], sent[len(TO_X) :]
     here = place()
     odd = lax.rem(here, 2)
@@ -82,16 +86,15 @@
                 slab += 1
 
 
-def scales(bounds_ref):
-    low, high = bounds_ref[0], bounds_ref[1]
-    return 0.5 * (high + low), 0.5 * (high - low)
-
-
-def core_kernel(bounds_ref, v_ref, own_ref, one_ref, g0_ref, g2_ref, h0_ref, h1_ref, h2_ref):
+def scales(scales_ref):
+    return scales_ref[0:1, 0:1], scales_ref[1:2, 0:1]
+
+
+def core_kernel(scales_ref, v_ref, own_ref, one_ref, g0_ref, g2_ref, h0_ref, h1_ref, h2_ref):
     pairs = v_ref.shape[0] // PAIR
-    center, halfwidth = scales(bounds_ref)
-    for at in range(0, v_ref.shape[1], PAIR):
-        lanes = slice(at, at + PAIR)
+    center, halfwidth = scales(scales_ref)
+    for at in range(0, v_ref.shape[1], STEP):
+        lanes = slice(at, at + STEP)
         v0, v1, v2 = (v_ref[natural(j, pairs), lanes] for j in range(3))
         v = jnp.concatenate([v0, v1, v2], axis=0)
         g0_ref[:, lanes] = dot(own_ref[0:PAIR, PAIR:], v[: 2 * PAIR])
@@ -129,7 +132,7 @@
     halo_ref[B:PAIR, far + B : far + PAIR] = sent_ref[4 * B : 5 * B, :]
 
 
-def side_kernel(side, first_slab, layout, bounds_ref, v_ref, own_ref, halo_ref, low_ref, high_ref, *refs):
+def side_kernel(side, first_slab, layout, scales_ref, v_ref, own_ref, halo_ref, low_ref, high_ref, *refs):
     near_refs, refs = refs[: len(layout)], refs[len(layout) :]
     if side == 0:
         g_ref, h_ref, h1_ref, h1_out, end_out = refs
@@ -137,7 +140,7 @@
         g_ref, h_ref, h1_ref, one_ref, zero_ref = refs[:5]
         out_ref, end_ref, mid_ref, sems = refs[-4:]
     pairs = v_ref.shape[0] // PAIR
-    center, halfwidth = scales(bounds_ref)
+    center, halfwidth = scales(scales_ref)
     edge = 0 if side == 0 else 2
     rows = slice(edge * PAIR, (edge + 1) * PAIR)
     outward = slice(0, PAIR) if side == 0 else slice(2 * PAIR, 3 * PAIR)
@@ -155,18 +158,26 @@
             for pair, source in enumerate((zero_ref, mid_ref, end_ref))
         ]
         copies[0].start()
-    for at in range(0, width, PAIR):
-        lanes = slice(first_slab * B + at, first_slab * B + at + PAIR)
-        here = slice(at, at + PAIR)
-        near = jnp.concatenate(slabs[at // B : at // B + 2], axis=1)
+    for at in range(0, width, STEP):
+        to = min(at + STEP, width)
+        lanes = slice(first_slab * B + at, first_slab * B + to)
+        here = slice(at, to)
+        near = jnp.concatenate(slabs[at // B : to // B], axis=1)
         v = v_ref[natural(edge, pairs), lanes]
-        stack = jnp.concatenate([v, near, low_ref[:, lanes], high_ref[:, lanes]], axis=0)
+        others = jnp.concatenate([v, low_ref[:, lanes], high_ref[:, lanes]], axis=0)
         v32 = v.astype(jnp.float32)
-        image = g_ref[:, lanes] + dot(own_ref[rows, outward], near)
+        by_near = dot(jnp.concatenate([own_ref[rows, outward], halo_ref[:, PAIR : 2 * PAIR]], axis=0), near)
+        image = g_ref[:, lanes] + by_near[:PAIR]
         edge_one = ((image - center * v32) / halfwidth).astype(v.dtype)
-        image = dot(halo_ref[...], stack)
+        image = by_near[PAIR:] + dot(
+            jnp.concatenate([halo_ref[:, :PAIR], halo_ref[:, 2 * PAIR :]], axis=1), others
+        )
         near_one = ((image - center * near.astype(jnp.float32)) / halfwidth).astype(v.dtype)
-        h1 = dot(own_ref[PAIR : 2 * PAIR, outward], edge_one)
+        by_edge = dot(
+            jnp.concatenate([own_ref[PAIR : 2 * PAIR, outward], own_ref[rows, PAIR : 2 * PAIR]], axis=0),
+            edge_one,
+        )
+        h1 = by_edge[:PAIR]
         if side == 0:
             h1_out[:, here] = h1_ref[:, lanes] + h1
         else:
@@ -174,9 +185,7 @@
             one = one_ref[:, lanes].astype(jnp.float32)
             v1 = v_ref[natural(1, pairs), lanes].astype(jnp.float32)
             mid_ref[:, here] = (2.0 * ((h1 - center * one) / halfwidth) - v1).astype(v.dtype)
-        image = h_ref[:, lanes] + (
-            dot(own_ref[rows, PAIR : 2 * PAIR], edge_one) + dot(own_ref[rows, outward], near_one)
-        )
+        image = h_ref[:, lanes] + (by_edge[PAIR:] + dot(own_ref[rows, outward], near_one))
         end = (2.0 * ((image - center * edge_one.astype(jnp.float32)) / halfwidth) - v32).astype(v.dtype)
         if side == 0:
             end_out[:, here] = end
@@ -240,14 +249,16 @@
     def send(part, perm):
         return lax.ppermute(part, AXES, perm)
 
-    middle = [lax.slice_in_dim(vectors, rows // 2 + at, rows // 2 + at + B, axis=0) for at in (-B, 0)]
-    own, *parts = call(
+    low = lax.slice_in_dim(vectors, rows // 2 - B, rows // 2, axis=0)
+    low, rest = after(low, vectors)
+    middle = [low, lax.slice_in_dim(rest, rows // 2, rows // 2 + B, axis=0)]
+    scale, own, *parts = call(
         functools.partial(pack_kernel, ring * rows_here),
-        [pltpu.VMEM((rows, 3 * PAIR), dtype)]
+        [pltpu.VMEM((8, B), jnp.float32), pltpu.VMEM((rows, 3 * PAIR), dtype)]
         + [
             pltpu.VMEM((head + slabs * PAIR, B), dtype) for head, slabs in TO_X + DIRECT + VIA_X
         ],
-        [ham_columns, ham_blocks, vectors],
+        [ham_columns, bounds, ham_blocks, rest],
         "pack",
     )
     to_x, parts = parts[: len(TO_X)], parts[len(TO_X) :]
@@ -269,7 +280,7 @@
 
     wide = lambda kind: pltpu.VMEM((PAIR, vec_width), kind)
     one, g0, g2, h0, h1, h2 = call(
-        core_kernel, [wide(dtype)] + [wide(jnp.float32)] * 5, [bounds, vectors, own], "core"
+        core_kernel, [wide(dtype)] + [wide(jnp.float32)] * 5, [scale, vectors, own], "core"
     )
     band = [pltpu.VMEM((PAIR, 3 * PAIR), dtype)]
     (halo_d,) = call(functools.partial(halo_kernel, 0), band, [own, near_d[0]], "halo_d")
@@ -285,13 +296,13 @@
         mid, zero = call(
             functools.partial(side_kernel, 0, first_slab, layout),
             [chunk(jnp.float32), chunk(dtype)],
-            [bounds, vectors, own, halo_d, *far_d, *near, g0, h0, h1],
+            [scale, vectors, own, halo_d, *far_d, *near, g0, h0, h1],
             "side_d",
         )
         near_x[c], zero = after(near_x[c], zero)
         if c == 0:
             (halo_x,) = call(functools.partial(halo_kernel, 1), band, [own, near_x[0]], "halo_x")
-        args = [bounds, vectors, own, halo_x, *far_x, near_x[c], g2, h2, mid, one, zero]
+        args = [scale, vectors, own, halo_x, *far_x, near_x[c], g2, h2, mid, one, zero]
         aliases = {}
         if result is not None:
             aliases[len(args)] = 0

time: 48.8 us -> 47.7 us (0.977)
  Pallas kernels: 12.1 us -> 7.95 us
  local copies, waits for them, and re-layouts: 3.25 us -> 4.77 us
  waiting for transfers between devices: 9.33 us -> 10.6 us
    pallas_call x8, Pallas kernels: 12.1 us -> 7.95 us  [call(): pl.pallas_call(body, out_shape=outs, in_specs=[whole(space) for space in...]
    ppermute x11, waiting for transfers between devices: 9.33 us -> 10.6 us  [send(): return lax.ppermute(part, AXES, perm)]
    slice x1 -> x2, local copies, waits for them, and re-layouts: 1.15 us -> 2.02 us  [the longest x1 1.05 us: per_device(): low = lax.slice_in_dim(vectors, rows // 2 - B, rows // 2, axis=0)]
    unnamed x10, local copies, waits for them, and re-layouts: 2.11 us -> 2.75 us
  transfers between devices with their start and end apart: 11 -> 11, of which waited for: 6 -> 8; matrix products, arithmetic and copies ran while one was open for 0% -> 2% of each run, Pallas kernels for 20% -> 14%
where the time goes in v3:
time: 47.7 us; the launch traced here: 47.2 us
  starting transfers between devices  23.8 us (50%)
  waiting for transfers between devices  10.6 us (22%)
  Pallas kernels  7.95 us (17%)
  local copies, waits for them, and re-layouts  4.77 us (10%)
    ppermute x11, starting transfers between devices, send(): return lax.ppermute(part, AXES, perm)  23.8 us
    ppermute x11, waiting for transfers between devices, send(): return lax.ppermute(part, AXES, perm)  10.6 us
    pallas_call x8, Pallas kernels, call(): pl.pallas_call(body, out_shape=outs, in_specs=[whole(space) for space in...  7.95 us
    unnamed x10, local copies, waits for them, and re-layouts  2.75 us
    slice x1, local copies, waits for them, and re-layouts, per_device(): low = lax.slice_in_dim(vectors, rows // 2 - B, rows // 2, axis=0)  1.05 us
    slice x1, local copies, waits for them, and re-layouts, per_device(): middle = [low, lax.slice_in_dim(rest, rows // 2, rows // 2 + B, axis=0)]  0.97 us
  transfers between devices with their start and end apart: 11, of which 8 were waited for; matrix products, arithmetic and copies ran while one was open for 2% of the time, Pallas kernels for 14%

profile of v3, /device:TPU:0, one launch (start us, length us, event | category | flops | bytes accessed | tf_op | source)
XLA Modules:
  0.0 47.2 jit_solution(4498331996286257056)
XLA Ops:
  0.0 0.0 copy-start.2
  0.0 1.1 %slice.6 = bf16[128,1024]{1,0:T(8,128)(2,1)S(1)} slice(bf16[768,1024]{1,0:T(8,128)(2,1)} %v_ref.10), slice={[256:384], [0:1024]} | slice | bytes 524288 | tf_op jit(solution)/shard_map/slice | solution.py:252
  1.1 3.0 %collective-permute-start = (bf16[128,1024]{1,0:T(8,128)(2,1)S(1)}, bf16[128,1024]{1,0:T(8,128)(2,1)S(1)}, u32[]{:S(2)}, u32[]{:S(2)}) collective-permute-start(bf16[128,1024]{1,0:T(8,128)(2,1)S(1)} %slice.6), channel_id=1, source_target_pairs={{0,1},{1,0},{2,3},{3,2},{4,5},{5,4},{6,7},{7,6},{8,9},{9,8},{10,11... | collective-permute-start | bytes 786440 | tf_op jit(solution)/shard_map/ppermute | solution.py:250
  4.1 1.0 %slice.7 = bf16[128,1024]{1,0:T(8,128)(2,1)S(1)} slice(bf16[768,1024]{1,0:T(8,128)(2,1)} %v_ref.10), slice={[384:512], [0:1024]} | slice | bytes 524288 | tf_op jit(solution)/shard_map/slice | solution.py:254
  5.0 0.1 collective-permute-start.5
  5.1 0.0 copy-done.2
  5.1 0.0 copy-start
  5.1 1.4 %copy-done = bf16[768,1024]{1,0:T(8,128)(2,1)S(1)} copy-done((bf16[768,1024]{1,0:T(8,128)(2,1)S(1)}, bf16[768,1024]{1,0:T(8,128)(2,1)}, u32[]{:S(2)}) %copy-start) | copy-done | bytes 1572888
  6.5 0.0 copy-start.3
  6.5 0.7 %copy-done.3 = s32[6,5]{1,0:T(8,128)S(1)} copy-done((s32[6,5]{1,0:T(8,128)S(1)}, s32[6,5]{1,0:T(8,128)}, u32[]{:S(2)}) %copy-start.3) | copy-done | bytes 144
  7.2 0.0 copy-start.4
  7.2 0.7 %copy-done.4 = f32[2]{0:T(128)S(1)} copy-done((f32[2]{0:T(128)S(1)}, f32[2]{0:T(128)}, u32[]{:S(2)}) %copy-start.4) | copy-done | bytes 32
  7.9 0.0 copy-start.1
  7.9 1.3 %pack.1 = (f32[8,128]{1,0:T(8,128)S(1)}, bf16[768,768]{1,0:T(8,128)(2,1)S(1)}, bf16[1680,128]{1,0:T(8,128)(2,1)S(1)}, bf16[1024,128]{1,0:T(8,128)(2,1)S(1)}, bf1...) custom-call(s32[6,5]{1,0:T(8,128)S(1)} %copy-done.3, f32[2]{0:T(128)S(1)} %copy-done.4, ...), custom_call_target="tpu_custom_call" | custom-call | tf_op jit(solution)/shard_map/pack/pallas_call | solution.py:218
  9.2 2.0 %collective-permute-done.low_ref = bf16[128,1024]{1,0:T(8,128)(2,1)S(1)} collective-permute-done((bf16[128,1024]{1,0:T(8,128)(2,1)S(1)}, bf16[128,1024]{1,0:T(8,128)(2,1)S(1)}, u32[]{:S(2)}, u32[]{:S(2)}) %collective-permute-start) | collective-permute-done | bytes 262176 | tf_op jit(solution)/shard_map/ppermute | solution.py:250
  11.2 2.1 %collective-permute-start.3 = (bf16[128,1024]{1,0:T(8,128)(2,1)S(1)}, bf16[128,1024]{1,0:T(8,128)(2,1)S(1)}, u32[]{:S(2)}, u32[]{:S(2)}) collective-permute-start(bf16[128,1024]{1,0:T(8,128)(2,1)S(1)} %collective-permute-done.low_ref), channel_id=1, source_target_pairs={{0,2},{1,31},{2,4},{3,1},{4,6},{5,3},{6,8},{7,5},{8,10},{9,7},{10,... | collective-permute-start | bytes 786440 | tf_op jit(solution)/shard_map/ppermute | solution.py:250
  13.3 1.9 %collective-permute-start.1 = (bf16[1024,128]{1,0:T(8,128)(2,1)S(1)}, bf16[1024,128]{1,0:T(8,128)(2,1)S(1)}, u32[]{:S(2)}, u32[]{:S(2)}) collective-permute-start(bf16[1024,128]{1,0:T(8,128)(2,1)S(1)} %get-tuple-element.49), channel_id=1, source_target_pairs={{0,1},{1,0},{2,3},{3,2},{4,5},{5,4},{6,7},{7,6},{8,9},{9,8},{10,11... | collective-permute-start | bytes 786440 | tf_op jit(solution)/shard_map/ppermute | solution.py:250
  15.2 1.6 %collective-permute-start.2 = (bf16[656,128]{1,0:T(8,128)(2,1)S(1)}, bf16[656,128]{1,0:T(8,128)(2,1)S(1)}, u32[]{:S(2)}, u32[]{:S(2)}) collective-permute-start(bf16[656,128]{1,0:T(8,128)(2,1)S(1)} %get-tuple-element.50), channel_id=1, source_target_pairs={{0,31},{1,2},{2,1},{3,4},{4,3},{5,6},{6,5},{7,8},{8,7},{9,10},{10,... | collective-permute-start | bytes 503816 | tf_op jit(solution)/shard_map/ppermute | solution.py:250
  16.8 0.0 collective-permute-done.5.high_ref
  16.8 0.9 %collective-permute-start.7 = (bf16[1024,128]{1,0:T(8,128)(2,1)S(1)}, bf16[1024,128]{1,0:T(8,128)(2,1)S(1)}, u32[]{:S(2)}, u32[]{:S(2)}) collective-permute-start(bf16[1024,128]{1,0:T(8,128)(2,1)S(1)} %get-tuple-element.60), channel_id=1, source_target_pairs={{0,1},{1,0},{2,3},{3,2},{4,5},{5,4},{6,7},{7,6},{8,9},{9,8},{10,11... | collective-permute-start | bytes 786440 | tf_op jit(solution)/shard_map/ppermute | solution.py:250
  17.7 4.0 %collective-permute-start.6 = (bf16[128,1024]{1,0:T(8,128)(2,1)S(1)}, bf16[128,1024]{1,0:T(8,128)(2,1)S(1)}, u32[]{:S(2)}, u32[]{:S(2)}) collective-permute-start(bf16[128,1024]{1,0:T(8,128)(2,1)S(1)} %collective-permute-done.5.high_ref), channel_id=1, source_target_pairs={{0,2},{1,31},{2,4},{3,1},{4,6},{5,3},{6,8},{7,5},{8,10},{9,7},{10,... | collective-permute-start | bytes 786440 | tf_op jit(solution)/shard_map/ppermute | solution.py:250
  21.7 0.0 collective-permute-done.3.low_ref
  21.7 2.6 %collective-permute-done.2.sent_ref.refs_0_ = bf16[656,128]{1,0:T(8,128)(2,1)S(1)} collective-permute-done((bf16[656,128]{1,0:T(8,128)(2,1)S(1)}, bf16[656,128]{1,0:T(8,128)(2,1)S(1)}, u32[]{:S(2)}, u32[]{:S(2)}) %collective-permute-start.2) | collective-permute-done | bytes 167968 | tf_op jit(solution)/shard_map/ppermute | solution.py:250
  24.3 0.0 collective-permute-done.1
  24.3 3.9 %collective-permute-start.4 = (bf16[1680,128]{1,0:T(8,128)(2,1)S(1)}, bf16[1680,128]{1,0:T(8,128)(2,1)S(1)}, u32[]{:S(2)}, u32[]{:S(2)}) collective-permute-start(bf16[1680,128]{1,0:T(8,128)(2,1)S(1)} %get-tuple-element.55), channel_id=1, source_target_pairs={{0,1},{1,0},{2,3},{3,2},{4,5},{5,4},{6,7},{7,6},{8,9},{9,8},{10,11... | collective-permute-start | bytes 1290248 | tf_op jit(solution)/shard_map/ppermute | solution.py:250
  28.2 1.5 %collective-permute-start.8 = (bf16[1024,128]{1,0:T(8,128)(2,1)S(1)}, bf16[1024,128]{1,0:T(8,128)(2,1)S(1)}, u32[]{:S(2)}, u32[]{:S(2)}) collective-permute-start(bf16[1024,128]{1,0:T(8,128)(2,1)S(1)} %collective-permute-done.1), channel_id=1, source_target_pairs={{0,2},{1,31},{2,4},{3,1},{4,6},{5,3},{6,8},{7,5},{8,10},{9,7},{10,... | collective-permute-start | bytes 786440 | tf_op jit(solution)/shard_map/ppermute | solution.py:250
  29.7 1.2 %collective-permute-done.7 = bf16[1024,128]{1,0:T(8,128)(2,1)S(1)} collective-permute-done((bf16[1024,128]{1,0:T(8,128)(2,1)S(1)}, bf16[1024,128]{1,0:T(8,128)(2,1)S(1)}, u32[]{:S(2)}, u32[]{:S(2)}) %collective-permute-start.7) | collective-permute-done | bytes 262176 | tf_op jit(solution)/shard_map/ppermute | solution.py:250
  30.8 0.1 collective-permute-done.6.high_ref
  30.9 2.9 %collective-permute-start.10 = (bf16[1024,128]{1,0:T(8,128)(2,1)S(1)}, bf16[1024,128]{1,0:T(8,128)(2,1)S(1)}, u32[]{:S(2)}, u32[]{:S(2)}) collective-permute-start(bf16[1024,128]{1,0:T(8,128)(2,1)S(1)} %collective-permute-done.7), channel_id=1, source_target_pairs={{0,2},{1,31},{2,4},{3,1},{4,6},{5,3},{6,8},{7,5},{8,10},{9,7},{10,... | collective-permute-start | bytes 786440 | tf_op jit(solution)/shard_map/ppermute | solution.py:250
  33.8 1.9 %collective-permute-start.9 = (bf16[1024,128]{1,0:T(8,128)(2,1)S(1)}, bf16[1024,128]{1,0:T(8,128)(2,1)S(1)}, u32[]{:S(2)}, u32[]{:S(2)}) collective-permute-start(bf16[1024,128]{1,0:T(8,128)(2,1)S(1)} %get-tuple-element.70), channel_id=1, source_target_pairs={{0,1},{1,0},{2,3},{3,2},{4,5},{5,4},{6,7},{7,6},{8,9},{9,8},{10,11... | collective-permute-start | bytes 786440 | tf_op jit(solution)/shard_map/ppermute | solution.py:250
  35.7 0.0 copy-done.1
  35.7 1.8 %core.1 = (bf16[256,1024]{1,0:T(8,128)(2,1)S(1)}, f32[256,1024]{1,0:T(8,128)S(1)}, f32[256,1024]{1,0:T(8,128)S(1)}, f32[256,1024]{1,0:T(8,128)S(1)}, f32[256,1024]{1,0:T(8,128)S(1)}, /*index=5*/f32[256,1024]{1,0:T(8,128)S(1)}) custom-call(f32[8,128]{1,0:T(8,128)S(1)} %get-tuple-element.45.scales_ref, bf16[768,1024]{1,0:T(8,128)(2,1)S(1)} %copy-done.1, ...), custom_call_target="tpu_custom_call" | custom-call | tf_op jit(solution)/shard_map/core/pallas_call | solution.py:218
  37.5 0.1 halo_d.1.halo_ref
  37.7 1.1 %collective-permute-done.8.refs_1_ = bf16[1024,128]{1,0:T(8,128)(2,1)S(1)} collective-permute-done((bf16[1024,128]{1,0:T(8,128)(2,1)S(1)}, bf16[1024,128]{1,0:T(8,128)(2,1)S(1)}, u32[]{:S(2)}, u32[]{:S(2)}) %collective-permute-start.8) | collective-permute-done | bytes 262176 | tf_op jit(solution)/shard_map/ppermute | solution.py:250
  38.8 0.8 %side_d.2 = (f32[256,512]{1,0:T(8,128)S(1)}, bf16[256,512]{1,0:T(8,128)(2,1)S(1)}) custom-call(f32[8,128]{1,0:T(8,128)S(1)} %get-tuple-element.45.scales_ref, bf16[768,1024]{1,0:T(8,128)(2,1)S(1)} %copy-done.1, bf16[768,768]{1,0:T(8,128)(2,1)S(1)} %get-tuple-element.46.own_ref, bf16[256,768]{1,0:T(8,128)(2,1)S(1)} %halo_d.1.halo_ref, ...), custom_call_target="tpu_custom_call" | custom-call | tf_op jit(solution)/shard_map/side_d/pallas_call | solution.py:218
  39.5 0.5 %collective-permute-done.4.sent_ref.refs_0_ = bf16[1680,128]{1,0:T(8,128)(2,1)S(1)} collective-permute-done((bf16[1680,128]{1,0:T(8,128)(2,1)S(1)}, bf16[1680,128]{1,0:T(8,128)(2,1)S(1)}, u32[]{:S(2)}, u32[]{:S(2)}) %collective-permute-start.4) | collective-permute-done | bytes 430112 | tf_op jit(solution)/shard_map/ppermute | solution.py:250
  40.0 0.1 halo_x.1.halo_ref
  40.2 1.5 %side_x.2.refs_6_ = bf16[768,1024]{1,0:T(8,128)(2,1)} custom-call(f32[8,128]{1,0:T(8,128)S(1)} %get-tuple-element.45.scales_ref, bf16[768,1024]{1,0:T(8,128)(2,1)S(1)} %copy-done.1, bf16[768,768]{1,0:T(8,128)(2,1)S(1)} %get-tuple-element.46.own_ref, bf16[256,768]{1,0:T(8,128)(2,1)S(1)} %halo_x.1.halo_ref, ...), custom_call_target="tpu_custom_call" | custom-call | tf_op jit(solution)/shard_map/side_x/pallas_call | solution.py:218
  41.7 2.6 %collective-permute-done.10.refs_0_ = bf16[1024,128]{1,0:T(8,128)(2,1)S(1)} collective-permute-done((bf16[1024,128]{1,0:T(8,128)(2,1)S(1)}, bf16[1024,128]{1,0:T(8,128)(2,1)S(1)}, u32[]{:S(2)}, u32[]{:S(2)}) %collective-permute-start.10) | collective-permute-done | bytes 262176 | tf_op jit(solution)/shard_map/ppermute | solution.py:250
  44.4 0.8 %side_d.3 = (f32[256,512]{1,0:T(8,128)S(1)}, bf16[256,512]{1,0:T(8,128)(2,1)S(1)}) custom-call(f32[8,128]{1,0:T(8,128)S(1)} %get-tuple-element.45.scales_ref, bf16[768,1024]{1,0:T(8,128)(2,1)S(1)} %copy-done.1, bf16[768,768]{1,0:T(8,128)(2,1)S(1)} %get-tuple-element.46.own_ref, bf16[256,768]{1,0:T(8,128)(2,1)S(1)} %halo_d.1.halo_ref, ...), custom_call_target="tpu_custom_call" | custom-call | tf_op jit(solution)/shard_map/side_d/pallas_call | solution.py:218
  45.1 0.5 %collective-permute-done.9.refs_0_ = bf16[1024,128]{1,0:T(8,128)(2,1)S(1)} collective-permute-done((bf16[1024,128]{1,0:T(8,128)(2,1)S(1)}, bf16[1024,128]{1,0:T(8,128)(2,1)S(1)}, u32[]{:S(2)}, u32[]{:S(2)}) %collective-permute-start.9) | collective-permute-done | bytes 262176 | tf_op jit(solution)/shard_map/ppermute | solution.py:250
  45.7 1.5 %side_x.3 = bf16[768,1024]{1,0:T(8,128)(2,1)} custom-call(f32[8,128]{1,0:T(8,128)S(1)} %get-tuple-element.45.scales_ref, bf16[768,1024]{1,0:T(8,128)(2,1)S(1)} %copy-done.1, bf16[768,768]{1,0:T(8,128)(2,1)S(1)} %get-tuple-element.46.own_ref, bf16[256,768]{1,0:T(8,128)(2,1)S(1)} %halo_x.1.halo_ref, ...), custom_call_target="tpu_custom_call", output_to_operand_aliasing={{}: (12, {})} | custom-call | tf_op jit(solution)/shard_map/side_x/pallas_call | solution.py:218
Async XLA Ops:
  0.0 5.1 %copy-start.2 = (bf16[6,5,128,128]{3,2,1,0:T(8,128)(2,1)S(1)}, bf16[6,5,128,128]{3,2,1,0:T(8,128)(2,1)}, u32[]{:S(2)}) copy-start(bf16[6,5,128,128]{3,2,1,0:T(8,128)(2,1)} %blocks_ref.1) | copy-start | bytes 2949124
  1.1 10.1 %collective-permute-start = (bf16[128,1024]{1,0:T(8,128)(2,1)S(1)}, bf16[128,1024]{1,0:T(8,128)(2,1)S(1)}, u32[]{:S(2)}, u32[]{:S(2)}) collective-permute-start(bf16[128,1024]{1,0:T(8,128)(2,1)S(1)} %slice.6), channel_id=1, source_target_pairs={{0,1},{1,0},{2,3},{3,2},{4,5},{5,4},{6,7},{7,6},{8,9},{9,8},{10,11... | collective-permute-start | bytes 786440 | tf_op jit(solution)/shard_map/ppermute | solution.py:250
  5.0 11.8 %collective-permute-start.5 = (bf16[128,1024]{1,0:T(8,128)(2,1)S(1)}, bf16[128,1024]{1,0:T(8,128)(2,1)S(1)}, u32[]{:S(2)}, u32[]{:S(2)}) collective-permute-start(bf16[128,1024]{1,0:T(8,128)(2,1)S(1)} %slice.7), channel_id=1, source_target_pairs={{0,1},{1,0},{2,3},{3,2},{4,5},{5,4},{6,7},{7,6},{8,9},{9,8},{10,11... | collective-permute-start | bytes 786440 | tf_op jit(solution)/shard_map/ppermute | solution.py:250
  5.1 1.4 %copy-start = (bf16[768,1024]{1,0:T(8,128)(2,1)S(1)}, bf16[768,1024]{1,0:T(8,128)(2,1)}, u32[]{:S(2)}) copy-start(bf16[768,1024]{1,0:T(8,128)(2,1)} %v_ref.10) | copy-start | bytes 4718596
  6.5 0.7 %copy-start.3 = (s32[6,5]{1,0:T(8,128)S(1)}, s32[6,5]{1,0:T(8,128)}, u32[]{:S(2)}) copy-start(s32[6,5]{1,0:T(8,128)} %cols_ref.1) | copy-start | bytes 364
  7.2 0.7 %copy-start.4 = (f32[2]{0:T(128)S(1)}, f32[2]{0:T(128)}, u32[]{:S(2)}) copy-start(f32[2]{0:T(128)} %bounds_ref.1) | copy-start | bytes 28
  7.9 27.8 %copy-start.1 = (bf16[768,1024]{1,0:T(8,128)(2,1)S(1)}, bf16[768,1024]{1,0:T(8,128)(2,1)}, u32[]{:S(2)}) copy-start(bf16[768,1024]{1,0:T(8,128)(2,1)} %v_ref.10) | copy-start | bytes 4718596
  11.2 10.6 %collective-permute-start.3 = (bf16[128,1024]{1,0:T(8,128)(2,1)S(1)}, bf16[128,1024]{1,0:T(8,128)(2,1)S(1)}, u32[]{:S(2)}, u32[]{:S(2)}) collective-permute-start(bf16[128,1024]{1,0:T(8,128)(2,1)S(1)} %collective-permute-done.low_ref), channel_id=1, source_target_pairs={{0,2},{1,31},{2,4},{3,1},{4,6},{5,3},{6,8},{7,5},{8,10},{9,7},{10,... | collective-permute-start | bytes 786440 | tf_op jit(solution)/shard_map/ppermute | solution.py:250
  13.3 11.0 %collective-permute-start.1 = (bf16[1024,128]{1,0:T(8,128)(2,1)S(1)}, bf16[1024,128]{1,0:T(8,128)(2,1)S(1)}, u32[]{:S(2)}, u32[]{:S(2)}) collective-permute-start(bf16[1024,128]{1,0:T(8,128)(2,1)S(1)} %get-tuple-element.49), channel_id=1, source_target_pairs={{0,1},{1,0},{2,3},{3,2},{4,5},{5,4},{6,7},{7,6},{8,9},{9,8},{10,11... | collective-permute-start | bytes 786440 | tf_op jit(solution)/shard_map/ppermute | solution.py:250
  15.2 9.1 %collective-permute-start.2 = (bf16[656,128]{1,0:T(8,128)(2,1)S(1)}, bf16[656,128]{1,0:T(8,128)(2,1)S(1)}, u32[]{:S(2)}, u32[]{:S(2)}) collective-permute-start(bf16[656,128]{1,0:T(8,128)(2,1)S(1)} %get-tuple-element.50), channel_id=1, source_target_pairs={{0,31},{1,2},{2,1},{3,4},{4,3},{5,6},{6,5},{7,8},{8,7},{9,10},{10,... | collective-permute-start | bytes 503816 | tf_op jit(solution)/shard_map/ppermute | solution.py:250
  16.8 14.0 %collective-permute-start.7 = (bf16[1024,128]{1,0:T(8,128)(2,1)S(1)}, bf16[1024,128]{1,0:T(8,128)(2,1)S(1)}, u32[]{:S(2)}, u32[]{:S(2)}) collective-permute-start(bf16[1024,128]{1,0:T(8,128)(2,1)S(1)} %get-tuple-element.60), channel_id=1, source_target_pairs={{0,1},{1,0},{2,3},{3,2},{4,5},{5,4},{6,7},{7,6},{8,9},{9,8},{10,11... | collective-permute-start | bytes 786440 | tf_op jit(solution)/shard_map/ppermute | solution.py:250
  17.7 13.2 %collective-permute-start.6 = (bf16[128,1024]{1,0:T(8,128)(2,1)S(1)}, bf16[128,1024]{1,0:T(8,128)(2,1)S(1)}, u32[]{:S(2)}, u32[]{:S(2)}) collective-permute-start(bf16[128,1024]{1,0:T(8,128)(2,1)S(1)} %collective-permute-done.5.high_ref), channel_id=1, source_target_pairs={{0,2},{1,31},{2,4},{3,1},{4,6},{5,3},{6,8},{7,5},{8,10},{9,7},{10,... | collective-permute-start | bytes 786440 | tf_op jit(solution)/shard_map/ppermute | solution.py:250
  24.3 15.7 %collective-permute-start.4 = (bf16[1680,128]{1,0:T(8,128)(2,1)S(1)}, bf16[1680,128]{1,0:T(8,128)(2,1)S(1)}, u32[]{:S(2)}, u32[]{:S(2)}) collective-permute-start(bf16[1680,128]{1,0:T(8,128)(2,1)S(1)} %get-tuple-element.55), channel_id=1, source_target_pairs={{0,1},{1,0},{2,3},{3,2},{4,5},{5,4},{6,7},{7,6},{8,9},{9,8},{10,11... | collective-permute-start | bytes 1290248 | tf_op jit(solution)/shard_map/ppermute | solution.py:250
  28.2 10.6 %collective-permute-start.8 = (bf16[1024,128]{1,0:T(8,128)(2,1)S(1)}, bf16[1024,128]{1,0:T(8,128)(2,1)S(1)}, u32[]{:S(2)}, u32[]{:S(2)}) collective-permute-start(bf16[1024,128]{1,0:T(8,128)(2,1)S(1)} %collective-permute-done.1), channel_id=1, source_target_pairs={{0,2},{1,31},{2,4},{3,1},{4,6},{5,3},{6,8},{7,5},{8,10},{9,7},{10,... | collective-permute-start | bytes 786440 | tf_op jit(solution)/shard_map/ppermute | solution.py:250
  30.9 13.5 %collective-permute-start.10 = (bf16[1024,128]{1,0:T(8,128)(2,1)S(1)}, bf16[1024,128]{1,0:T(8,128)(2,1)S(1)}, u32[]{:S(2)}, u32[]{:S(2)}) collective-permute-start(bf16[1024,128]{1,0:T(8,128)(2,1)S(1)} %collective-permute-done.7), channel_id=1, source_target_pairs={{0,2},{1,31},{2,4},{3,1},{4,6},{5,3},{6,8},{7,5},{8,10},{9,7},{10,... | collective-permute-start | bytes 786440 | tf_op jit(solution)/shard_map/ppermute | solution.py:250
  33.8 11.9 %collective-permute-start.9 = (bf16[1024,128]{1,0:T(8,128)(2,1)S(1)}, bf16[1024,128]{1,0:T(8,128)(2,1)S(1)}, u32[]{:S(2)}, u32[]{:S(2)}) collective-permute-start(bf16[1024,128]{1,0:T(8,128)(2,1)S(1)} %get-tuple-element.70), channel_id=1, source_target_pairs={{0,1},{1,0},{2,3},{3,2},{4,5},{5,4},{6,7},{7,6},{8,9},{9,8},{10,11... | collective-permute-start | bytes 786440 | tf_op jit(solution)/shard_map/ppermute | solution.py:250

commit v4 on v3

--- a/solution.py
+++ b/solution.py
@@ -14,7 +14,7 @@
 HEAD = 5 * B + 16
 LIMIT = pltpu.CompilerParams(vmem_limit_bytes=16 * 1024 * 1024)
 FREE = pl.CostEstimate(flops=0, bytes_accessed=0, transcendentals=0)
-TO_X = ((HEAD, 4), (0, 4))
+TO_X = ((HEAD, 4), (0, 4), )
 DIRECT = ((HEAD, 0),)
 VIA_X = ((0, 4), (0, 4))
 
@@ -132,7 +132,7 @@
     halo_ref[B:PAIR, far + B : far + PAIR] = sent_ref[4 * B : 5 * B, :]
 
 
-def side_kernel(side, first_slab, layout, scales_ref, v_ref, own_ref, halo_ref, low_ref, high_ref, *refs):
+def side_kernel(side, first_slab, held_slab, layout, scales_ref, v_ref, own_ref, halo_ref, low_ref, high_ref, *refs):
     near_refs, refs = refs[: len(layout)], refs[len(layout) :]
     if side == 0:
         g_ref, h_ref, h1_ref, h1_out, end_out = refs
@@ -155,13 +155,19 @@
     if side == 1:
         copies = [
             pltpu.make_async_copy(source, out_ref.at[natural(pair, pairs), all_lanes], sems.at[pair])
-            for pair, source in enumerate((zero_ref, mid_ref, end_ref))
+            for pair, source in ((1, mid_ref), (2, end_ref))
         ]
-        copies[0].start()
+        if held_slab == first_slab:
+            held = slice(held_slab * B, held_slab * B + zero_ref.shape[1])
+            copies.insert(
+                0, pltpu.make_async_copy(zero_ref, out_ref.at[natural(0, pairs), held], sems.at[0])
+            )
+            copies[0].start()
     for at in range(0, width, STEP):
         to = min(at + STEP, width)
         lanes = slice(first_slab * B + at, first_slab * B + to)
         here = slice(at, to)
+        held = slice((first_slab - held_slab) * B + at, (first_slab - held_slab) * B + to)
         near = jnp.concatenate(slabs[at // B : to // B], axis=1)
         v = v_ref[natural(edge, pairs), lanes]
         others = jnp.concatenate([v, low_ref[:, lanes], high_ref[:, lanes]], axis=0)
@@ -181,7 +187,7 @@
         if side == 0:
             h1_out[:, here] = h1_ref[:, lanes] + h1
         else:
-            h1 += h1_ref[:, here]
+            h1 += h1_ref[:, held]
             one = one_ref[:, lanes].astype(jnp.float32)
             v1 = v_ref[natural(1, pairs), lanes].astype(jnp.float32)
             mid_ref[:, here] = (2.0 * ((h1 - center * one) / halfwidth) - v1).astype(v.dtype)
@@ -191,7 +197,7 @@
             end_out[:, here] = end
         else:
             end_ref[:, here] = end
-    for copy in copies[1:]:
+    for copy in copies[-2:]:
         copy.start()
     for copy in copies:
         copy.wait()
@@ -266,17 +272,15 @@
 
     far_x = [send(part, over_x) for part in middle]
     near_d = [send(part, direct) for part in to_d]
-    far_x[0], via_x[0] = after(far_x[0], via_x[0])
     far_x[1], via_x[1] = after(far_x[1], via_x[1])
     far_d = [send(part, onward) for part in far_x]
     passing = [send(part, over_x) for part in via_x]
-    far_d[0], to_x[0] = after(far_d[0], to_x[0])
+    far_d[0], passing[0] = after(far_d[0], passing[0])
+    far_d[1], passing[1] = after(far_d[1], passing[1])
+    near_d += [send(part, onward) for part in passing]
+    passing[0], to_x[0] = after(passing[0], to_x[0])
     near_d[0], to_x[0] = after(near_d[0], to_x[0])
-    passing[0], to_x[0] = after(passing[0], to_x[0])
-    far_d[1], passing[1] = after(far_d[1], passing[1])
     passing[1], to_x[1] = after(passing[1], to_x[1])
-    near_d += [send(part, onward) for part in passing]
-    near_x = [send(part, over_x) for part in to_x]
 
     wide = lambda kind: pltpu.VMEM((PAIR, vec_width), kind)
     one, g0, g2, h0, h1, h2 = call(
@@ -284,36 +288,43 @@
     )
     band = [pltpu.VMEM((PAIR, 3 * PAIR), dtype)]
     (halo_d,) = call(functools.partial(halo_kernel, 0), band, [own, near_d[0]], "halo_d")
-    result = None
-    first_slab = 0
-    for c, (head, slabs) in enumerate(TO_X):
-        if c == 0:
-            layout, near = (DIRECT + VIA_X)[:2], near_d[:2]
+    result, mid, zero = None, None, None
+    first_slab, held_slab, c = 0, 0, -1
+    for part, (head, slabs) in zip(to_x, TO_X, strict=True):
+        near = None if first_slab else send(part, over_x)
+        if mid is None or first_slab * B == held_slab * B + mid.shape[1]:
+            c += 1
+            held_slab = first_slab
+            layout, near_c = ((DIRECT + VIA_X)[:2], near_d[:2]) if c == 0 else (VIA_X[c : c + 1], near_d[c + 1 : c + 2])
+            if result is not None:
+                near_c[0], result = after(near_c[0], result)
+            width = sum(count for _, count in layout) * B
+            mid, zero = call(
+                functools.partial(side_kernel, 0, first_slab, held_slab, layout),
+                [pltpu.VMEM((PAIR, width), jnp.float32), pltpu.VMEM((PAIR, width), dtype)],
+                [scale, vectors, own, halo_d, *far_d, *near_c, g0, h0, h1],
+                "side_d",
+            )
+        if near is None:
+            near = send(part, over_x)
+        if held_slab == first_slab:
+            near, zero = after(near, zero)
         else:
-            layout, near = VIA_X[c : c + 1], near_d[c + 1 : c + 2]
-            near[0], result = after(near[0], result)
-        chunk = lambda kind, slabs=slabs: pltpu.VMEM((PAIR, slabs * B), kind)
-        mid, zero = call(
-            functools.partial(side_kernel, 0, first_slab, layout),
-            [chunk(jnp.float32), chunk(dtype)],
-            [scale, vectors, own, halo_d, *far_d, *near, g0, h0, h1],
-            "side_d",
-        )
-        near_x[c], zero = after(near_x[c], zero)
-        if c == 0:
-            (halo_x,) = call(functools.partial(halo_kernel, 1), band, [own, near_x[0]], "halo_x")
-        args = [scale, vectors, own, halo_x, *far_x, near_x[c], g2, h2, mid, one, zero]
+            near, result = after(near, result)
+        if result is None:
+            (halo_x,) = call(functools.partial(halo_kernel, 1), band, [own, near], "halo_x")
+        args = [scale, vectors, own, halo_x, *far_x, near, g2, h2, mid, one, zero]
         aliases = {}
         if result is not None:
             aliases[len(args)] = 0
             args.append(result)
         (result,) = call(
-            functools.partial(side_kernel, 1, first_slab, ((head, slabs),)),
+            functools.partial(side_kernel, 1, first_slab, held_slab, ((head, slabs),)),
             [jax.ShapeDtypeStruct((rows, vec_width), dtype)],
             args,
             "side_x",
             aliases=aliases,
-            scratch=[chunk(dtype)] * 2 + [pltpu.SemaphoreType.DMA((3,))],
+            scratch=[pltpu.VMEM((PAIR, slabs * B), dtype)] * 2 + [pltpu.SemaphoreType.DMA((3,))],
         )
         first_slab += slabs
     return result

time: 47.7 us -> 47.4 us (level)
  starting transfers between devices: 23.8 us -> 21.9 us
  waiting for transfers between devices: 10.6 us -> 12.4 us
    ppermute x11, starting transfers between devices: 23.8 us -> 21.9 us  [send(): return lax.ppermute(part, AXES, perm)]
    ppermute x11, waiting for transfers between devices: 10.6 us -> 12.4 us  [send(): return lax.ppermute(part, AXES, perm)]
  transfers between devices with their start and end apart: 11 -> 11, of which waited for: 8 -> 7; matrix products, arithmetic and copies ran while one was open for 2% -> 2% of each run, Pallas kernels for 14% -> 14%
where the time goes in v4:
time: 47.4 us; the launch traced here: 47.2 us
  starting transfers between devices  21.9 us (46%)
  waiting for transfers between devices  12.4 us (26%)
  Pallas kernels  7.95 us (17%)
  local copies, waits for them, and re-layouts  4.77 us (10%)
    ppermute x11, starting transfers between devices, send(): return lax.ppermute(part, AXES, perm)  21.9 us
    ppermute x11, waiting for transfers between devices, send(): return lax.ppermute(part, AXES, perm)  12.4 us
    pallas_call x8, Pallas kernels, call(): pl.pallas_call(body, out_shape=outs, in_specs=[whole(space) for space in...  7.95 us
    unnamed x10, local copies, waits for them, and re-layouts  2.75 us
    slice x1, local copies, waits for them, and re-layouts, per_device(): low = lax.slice_in_dim(vectors, rows // 2 - B, rows // 2, axis=0)  1.05 us
    slice x1, local copies, waits for them, and re-layouts, per_device(): middle = [low, lax.slice_in_dim(rest, rows // 2, rows // 2 + B, axis=0)]  0.97 us
  transfers between devices with their start and end apart: 11, of which 7 were waited for; matrix products, arithmetic and copies ran while one was open for 2% of the time, Pallas kernels for 14%

profile of v4, /device:TPU:0, one launch (start us, length us, event | category | flops | bytes accessed | tf_op | source)
XLA Modules:
  0.0 47.2 jit_solution(14624172331101296752)
XLA Ops:
  0.0 0.0 copy-start.2
  0.0 1.1 %slice.6 = bf16[128,1024]{1,0:T(8,128)(2,1)S(1)} slice(bf16[768,1024]{1,0:T(8,128)(2,1)} %v_ref.10), slice={[256:384], [0:1024]} | slice | bytes 524288 | tf_op jit(solution)/shard_map/slice | solution.py:258
  1.1 3.0 %collective-permute-start.1 = (bf16[128,1024]{1,0:T(8,128)(2,1)S(1)}, bf16[128,1024]{1,0:T(8,128)(2,1)S(1)}, u32[]{:S(2)}, u32[]{:S(2)}) collective-permute-start(bf16[128,1024]{1,0:T(8,128)(2,1)S(1)} %slice.6), channel_id=1, source_target_pairs={{0,1},{1,0},{2,3},{3,2},{4,5},{5,4},{6,7},{7,6},{8,9},{9,8},{10,11... | collective-permute-start | bytes 786440 | tf_op jit(solution)/shard_map/ppermute | solution.py:256
  4.1 1.0 %slice.7 = bf16[128,1024]{1,0:T(8,128)(2,1)S(1)} slice(bf16[768,1024]{1,0:T(8,128)(2,1)} %v_ref.10), slice={[384:512], [0:1024]} | slice | bytes 524288 | tf_op jit(solution)/shard_map/slice | solution.py:260
  5.0 0.1 collective-permute-start.5
  5.1 0.0 copy-done.2
  5.1 0.0 copy-start
  5.1 1.4 %copy-done = bf16[768,1024]{1,0:T(8,128)(2,1)S(1)} copy-done((bf16[768,1024]{1,0:T(8,128)(2,1)S(1)}, bf16[768,1024]{1,0:T(8,128)(2,1)}, u32[]{:S(2)}) %copy-start) | copy-done | bytes 1572888
  6.5 0.0 copy-start.3
  6.5 0.7 %copy-done.3 = s32[6,5]{1,0:T(8,128)S(1)} copy-done((s32[6,5]{1,0:T(8,128)S(1)}, s32[6,5]{1,0:T(8,128)}, u32[]{:S(2)}) %copy-start.3) | copy-done | bytes 144
  7.2 0.0 copy-start.4
  7.2 0.7 %copy-done.4 = f32[2]{0:T(128)S(1)} copy-done((f32[2]{0:T(128)S(1)}, f32[2]{0:T(128)}, u32[]{:S(2)}) %copy-start.4) | copy-done | bytes 32
  7.9 0.0 copy-start.1
  7.9 1.3 %pack.1 = (f32[8,128]{1,0:T(8,128)S(1)}, bf16[768,768]{1,0:T(8,128)(2,1)S(1)}, bf16[1680,128]{1,0:T(8,128)(2,1)S(1)}, bf16[1024,128]{1,0:T(8,128)(2,1)S(1)}, bf1...) custom-call(s32[6,5]{1,0:T(8,128)S(1)} %copy-done.3, f32[2]{0:T(128)S(1)} %copy-done.4, ...), custom_call_target="tpu_custom_call" | custom-call | tf_op jit(solution)/shard_map/pack/pallas_call | solution.py:224
  9.2 2.1 %collective-permute-start.3 = (bf16[1024,128]{1,0:T(8,128)(2,1)S(1)}, bf16[1024,128]{1,0:T(8,128)(2,1)S(1)}, u32[]{:S(2)}, u32[]{:S(2)}) collective-permute-start(bf16[1024,128]{1,0:T(8,128)(2,1)S(1)} %get-tuple-element.45), channel_id=1, source_target_pairs={{0,1},{1,0},{2,3},{3,2},{4,5},{5,4},{6,7},{7,6},{8,9},{9,8},{10,11... | collective-permute-start | bytes 786440 | tf_op jit(solution)/shard_map/ppermute | solution.py:256
  11.2 0.0 collective-permute-done.1.low_ref
  11.3 2.1 %collective-permute-start.2 = (bf16[128,1024]{1,0:T(8,128)(2,1)S(1)}, bf16[128,1024]{1,0:T(8,128)(2,1)S(1)}, u32[]{:S(2)}, u32[]{:S(2)}) collective-permute-start(bf16[128,1024]{1,0:T(8,128)(2,1)S(1)} %collective-permute-done.1.low_ref), channel_id=1, source_target_pairs={{0,2},{1,31},{2,4},{3,1},{4,6},{5,3},{6,8},{7,5},{8,10},{9,7},{10,... | collective-permute-start | bytes 786440 | tf_op jit(solution)/shard_map/ppermute | solution.py:256
  13.3 1.5 %collective-permute-start = (bf16[656,128]{1,0:T(8,128)(2,1)S(1)}, bf16[656,128]{1,0:T(8,128)(2,1)S(1)}, u32[]{:S(2)}, u32[]{:S(2)}) collective-permute-start(bf16[656,128]{1,0:T(8,128)(2,1)S(1)} %get-tuple-element.43), channel_id=1, source_target_pairs={{0,31},{1,2},{2,1},{3,4},{4,3},{5,6},{6,5},{7,8},{8,7},{9,10},{10,... | collective-permute-start | bytes 503816 | tf_op jit(solution)/shard_map/ppermute | solution.py:256
  14.8 2.0 %collective-permute-done.5.high_ref = bf16[128,1024]{1,0:T(8,128)(2,1)S(1)} collective-permute-done((bf16[128,1024]{1,0:T(8,128)(2,1)S(1)}, bf16[128,1024]{1,0:T(8,128)(2,1)S(1)}, u32[]{:S(2)}, u32[]{:S(2)}) %collective-permute-start.5) | collective-permute-done | bytes 262176 | tf_op jit(solution)/shard_map/ppermute | solution.py:256
  16.8 2.1 %collective-permute-start.7 = (bf16[1024,128]{1,0:T(8,128)(2,1)S(1)}, bf16[1024,128]{1,0:T(8,128)(2,1)S(1)}, u32[]{:S(2)}, u32[]{:S(2)}) collective-permute-start(bf16[1024,128]{1,0:T(8,128)(2,1)S(1)} %get-tuple-element.54), channel_id=1, source_target_pairs={{0,1},{1,0},{2,3},{3,2},{4,5},{5,4},{6,7},{7,6},{8,9},{9,8},{10,11... | collective-permute-start | bytes 786440 | tf_op jit(solution)/shard_map/ppermute | solution.py:256
  18.9 3.5 %collective-permute-start.6 = (bf16[128,1024]{1,0:T(8,128)(2,1)S(1)}, bf16[128,1024]{1,0:T(8,128)(2,1)S(1)}, u32[]{:S(2)}, u32[]{:S(2)}) collective-permute-start(bf16[128,1024]{1,0:T(8,128)(2,1)S(1)} %collective-permute-done.5.high_ref), channel_id=1, source_target_pairs={{0,2},{1,31},{2,4},{3,1},{4,6},{5,3},{6,8},{7,5},{8,10},{9,7},{10,... | collective-permute-start | bytes 786440 | tf_op jit(solution)/shard_map/ppermute | solution.py:256
  22.3 3.7 %collective-permute-done.3 = bf16[1024,128]{1,0:T(8,128)(2,1)S(1)} collective-permute-done((bf16[1024,128]{1,0:T(8,128)(2,1)S(1)}, bf16[1024,128]{1,0:T(8,128)(2,1)S(1)}, u32[]{:S(2)}, u32[]{:S(2)}) %collective-permute-start.3) | collective-permute-done | bytes 262176 | tf_op jit(solution)/shard_map/ppermute | solution.py:256
  26.0 0.0 collective-permute-done.2.low_ref
  26.0 0.0 collective-permute-done.sent_ref.refs_0_
  26.0 2.0 %collective-permute-start.4 = (bf16[1680,128]{1,0:T(8,128)(2,1)S(1)}, bf16[1680,128]{1,0:T(8,128)(2,1)S(1)}, u32[]{:S(2)}, u32[]{:S(2)}) collective-permute-start(bf16[1680,128]{1,0:T(8,128)(2,1)S(1)} %get-tuple-element.49), channel_id=1, source_target_pairs={{0,1},{1,0},{2,3},{3,2},{4,5},{5,4},{6,7},{7,6},{8,9},{9,8},{10,11... | collective-permute-start | bytes 1290248 | tf_op jit(solution)/shard_map/ppermute | solution.py:256
  28.1 1.6 %collective-permute-start.8 = (bf16[1024,128]{1,0:T(8,128)(2,1)S(1)}, bf16[1024,128]{1,0:T(8,128)(2,1)S(1)}, u32[]{:S(2)}, u32[]{:S(2)}) collective-permute-start(bf16[1024,128]{1,0:T(8,128)(2,1)S(1)} %collective-permute-done.3), channel_id=1, source_target_pairs={{0,2},{1,31},{2,4},{3,1},{4,6},{5,3},{6,8},{7,5},{8,10},{9,7},{10,... | collective-permute-start | bytes 786440 | tf_op jit(solution)/shard_map/ppermute | solution.py:256
  29.7 2.0 %collective-permute-done.7 = bf16[1024,128]{1,0:T(8,128)(2,1)S(1)} collective-permute-done((bf16[1024,128]{1,0:T(8,128)(2,1)S(1)}, bf16[1024,128]{1,0:T(8,128)(2,1)S(1)}, u32[]{:S(2)}, u32[]{:S(2)}) %collective-permute-start.7) | collective-permute-done | bytes 262176 | tf_op jit(solution)/shard_map/ppermute | solution.py:256
  31.6 0.0 collective-permute-done.6.high_ref
  31.7 2.1 %collective-permute-start.10 = (bf16[1024,128]{1,0:T(8,128)(2,1)S(1)}, bf16[1024,128]{1,0:T(8,128)(2,1)S(1)}, u32[]{:S(2)}, u32[]{:S(2)}) collective-permute-start(bf16[1024,128]{1,0:T(8,128)(2,1)S(1)} %collective-permute-done.7), channel_id=1, source_target_pairs={{0,2},{1,31},{2,4},{3,1},{4,6},{5,3},{6,8},{7,5},{8,10},{9,7},{10,... | collective-permute-start | bytes 786440 | tf_op jit(solution)/shard_map/ppermute | solution.py:256
  33.8 1.9 %collective-permute-start.9 = (bf16[1024,128]{1,0:T(8,128)(2,1)S(1)}, bf16[1024,128]{1,0:T(8,128)(2,1)S(1)}, u32[]{:S(2)}, u32[]{:S(2)}) collective-permute-start(bf16[1024,128]{1,0:T(8,128)(2,1)S(1)} %get-tuple-element.63), channel_id=1, source_target_pairs={{0,1},{1,0},{2,3},{3,2},{4,5},{5,4},{6,7},{7,6},{8,9},{9,8},{10,11... | collective-permute-start | bytes 786440 | tf_op jit(solution)/shard_map/ppermute | solution.py:256
  35.7 0.0 copy-done.1
  35.7 1.8 %core.1 = (bf16[256,1024]{1,0:T(8,128)(2,1)S(1)}, f32[256,1024]{1,0:T(8,128)S(1)}, f32[256,1024]{1,0:T(8,128)S(1)}, f32[256,1024]{1,0:T(8,128)S(1)}, f32[256,1024]{1,0:T(8,128)S(1)}, /*index=5*/f32[256,1024]{1,0:T(8,128)S(1)}) custom-call(f32[8,128]{1,0:T(8,128)S(1)} %get-tuple-element.41.scales_ref, bf16[768,1024]{1,0:T(8,128)(2,1)S(1)} %copy-done.1, ...), custom_call_target="tpu_custom_call" | custom-call | tf_op jit(solution)/shard_map/core/pallas_call | solution.py:224
  37.5 0.1 halo_d.1.halo_ref
  37.7 1.3 %collective-permute-done.8.refs_1_ = bf16[1024,128]{1,0:T(8,128)(2,1)S(1)} collective-permute-done((bf16[1024,128]{1,0:T(8,128)(2,1)S(1)}, bf16[1024,128]{1,0:T(8,128)(2,1)S(1)}, u32[]{:S(2)}, u32[]{:S(2)}) %collective-permute-start.8) | collective-permute-done | bytes 262176 | tf_op jit(solution)/shard_map/ppermute | solution.py:256
  39.0 0.8 %side_d.2 = (f32[256,512]{1,0:T(8,128)S(1)}, bf16[256,512]{1,0:T(8,128)(2,1)S(1)}) custom-call(f32[8,128]{1,0:T(8,128)S(1)} %get-tuple-element.41.scales_ref, bf16[768,1024]{1,0:T(8,128)(2,1)S(1)} %copy-done.1, bf16[768,768]{1,0:T(8,128)(2,1)S(1)} %get-tuple-element.42.own_ref, bf16[256,768]{1,0:T(8,128)(2,1)S(1)} %halo_d.1.halo_ref, ...), custom_call_target="tpu_custom_call" | custom-call | tf_op jit(solution)/shard_map/side_d/pallas_call | solution.py:224
  39.8 1.1 %collective-permute-done.4.sent_ref.refs_0_ = bf16[1680,128]{1,0:T(8,128)(2,1)S(1)} collective-permute-done((bf16[1680,128]{1,0:T(8,128)(2,1)S(1)}, bf16[1680,128]{1,0:T(8,128)(2,1)S(1)}, u32[]{:S(2)}, u32[]{:S(2)}) %collective-permute-start.4) | collective-permute-done | bytes 430112 | tf_op jit(solution)/shard_map/ppermute | solution.py:256
  40.9 0.1 halo_x.1.halo_ref
  41.0 1.5 %side_x.2.refs_6_ = bf16[768,1024]{1,0:T(8,128)(2,1)} custom-call(f32[8,128]{1,0:T(8,128)S(1)} %get-tuple-element.41.scales_ref, bf16[768,1024]{1,0:T(8,128)(2,1)S(1)} %copy-done.1, bf16[768,768]{1,0:T(8,128)(2,1)S(1)} %get-tuple-element.42.own_ref, bf16[256,768]{1,0:T(8,128)(2,1)S(1)} %halo_x.1.halo_ref, ...), custom_call_target="tpu_custom_call" | custom-call | tf_op jit(solution)/shard_map/side_x/pallas_call | solution.py:224
  42.6 2.1 %collective-permute-done.10.refs_0_ = bf16[1024,128]{1,0:T(8,128)(2,1)S(1)} collective-permute-done((bf16[1024,128]{1,0:T(8,128)(2,1)S(1)}, bf16[1024,128]{1,0:T(8,128)(2,1)S(1)}, u32[]{:S(2)}, u32[]{:S(2)}) %collective-permute-start.10) | collective-permute-done | bytes 262176 | tf_op jit(solution)/shard_map/ppermute | solution.py:256
  44.6 0.8 %side_d.3 = (f32[256,512]{1,0:T(8,128)S(1)}, bf16[256,512]{1,0:T(8,128)(2,1)S(1)}) custom-call(f32[8,128]{1,0:T(8,128)S(1)} %get-tuple-element.41.scales_ref, bf16[768,1024]{1,0:T(8,128)(2,1)S(1)} %copy-done.1, bf16[768,768]{1,0:T(8,128)(2,1)S(1)} %get-tuple-element.42.own_ref, bf16[256,768]{1,0:T(8,128)(2,1)S(1)} %halo_d.1.halo_ref, ...), custom_call_target="tpu_custom_call" | custom-call | tf_op jit(solution)/shard_map/side_d/pallas_call | solution.py:224
  45.4 0.3 collective-permute-done.9.refs_0_
  45.7 1.5 %side_x.3 = bf16[768,1024]{1,0:T(8,128)(2,1)} custom-call(f32[8,128]{1,0:T(8,128)S(1)} %get-tuple-element.41.scales_ref, bf16[768,1024]{1,0:T(8,128)(2,1)S(1)} %copy-done.1, bf16[768,768]{1,0:T(8,128)(2,1)S(1)} %get-tuple-element.42.own_ref, bf16[256,768]{1,0:T(8,128)(2,1)S(1)} %halo_x.1.halo_ref, ...), custom_call_target="tpu_custom_call", output_to_operand_aliasing={{}: (12, {})} | custom-call | tf_op jit(solution)/shard_map/side_x/pallas_call | solution.py:224
Async XLA Ops:
  0.0 5.1 %copy-start.2 = (bf16[6,5,128,128]{3,2,1,0:T(8,128)(2,1)S(1)}, bf16[6,5,128,128]{3,2,1,0:T(8,128)(2,1)}, u32[]{:S(2)}) copy-start(bf16[6,5,128,128]{3,2,1,0:T(8,128)(2,1)} %blocks_ref.1) | copy-start | bytes 2949124
  1.1 10.2 %collective-permute-start.1 = (bf16[128,1024]{1,0:T(8,128)(2,1)S(1)}, bf16[128,1024]{1,0:T(8,128)(2,1)S(1)}, u32[]{:S(2)}, u32[]{:S(2)}) collective-permute-start(bf16[128,1024]{1,0:T(8,128)(2,1)S(1)} %slice.6), channel_id=1, source_target_pairs={{0,1},{1,0},{2,3},{3,2},{4,5},{5,4},{6,7},{7,6},{8,9},{9,8},{10,11... | collective-permute-start | bytes 786440 | tf_op jit(solution)/shard_map/ppermute | solution.py:256
  5.0 11.8 %collective-permute-start.5 = (bf16[128,1024]{1,0:T(8,128)(2,1)S(1)}, bf16[128,1024]{1,0:T(8,128)(2,1)S(1)}, u32[]{:S(2)}, u32[]{:S(2)}) collective-permute-start(bf16[128,1024]{1,0:T(8,128)(2,1)S(1)} %slice.7), channel_id=1, source_target_pairs={{0,1},{1,0},{2,3},{3,2},{4,5},{5,4},{6,7},{7,6},{8,9},{9,8},{10,11... | collective-permute-start | bytes 786440 | tf_op jit(solution)/shard_map/ppermute | solution.py:256
  5.1 1.4 %copy-start = (bf16[768,1024]{1,0:T(8,128)(2,1)S(1)}, bf16[768,1024]{1,0:T(8,128)(2,1)}, u32[]{:S(2)}) copy-start(bf16[768,1024]{1,0:T(8,128)(2,1)} %v_ref.10) | copy-start | bytes 4718596
  6.5 0.7 %copy-start.3 = (s32[6,5]{1,0:T(8,128)S(1)}, s32[6,5]{1,0:T(8,128)}, u32[]{:S(2)}) copy-start(s32[6,5]{1,0:T(8,128)} %cols_ref.1) | copy-start | bytes 364
  7.2 0.7 %copy-start.4 = (f32[2]{0:T(128)S(1)}, f32[2]{0:T(128)}, u32[]{:S(2)}) copy-start(f32[2]{0:T(128)} %bounds_ref.1) | copy-start | bytes 28
  7.9 27.8 %copy-start.1 = (bf16[768,1024]{1,0:T(8,128)(2,1)S(1)}, bf16[768,1024]{1,0:T(8,128)(2,1)}, u32[]{:S(2)}) copy-start(bf16[768,1024]{1,0:T(8,128)(2,1)} %v_ref.10) | copy-start | bytes 4718596
  9.2 16.8 %collective-permute-start.3 = (bf16[1024,128]{1,0:T(8,128)(2,1)S(1)}, bf16[1024,128]{1,0:T(8,128)(2,1)S(1)}, u32[]{:S(2)}, u32[]{:S(2)}) collective-permute-start(bf16[1024,128]{1,0:T(8,128)(2,1)S(1)} %get-tuple-element.45), channel_id=1, source_target_pairs={{0,1},{1,0},{2,3},{3,2},{4,5},{5,4},{6,7},{7,6},{8,9},{9,8},{10,11... | collective-permute-start | bytes 786440 | tf_op jit(solution)/shard_map/ppermute | solution.py:256
  11.3 14.8 %collective-permute-start.2 = (bf16[128,1024]{1,0:T(8,128)(2,1)S(1)}, bf16[128,1024]{1,0:T(8,128)(2,1)S(1)}, u32[]{:S(2)}, u32[]{:S(2)}) collective-permute-start(bf16[128,1024]{1,0:T(8,128)(2,1)S(1)} %collective-permute-done.1.low_ref), channel_id=1, source_target_pairs={{0,2},{1,31},{2,4},{3,1},{4,6},{5,3},{6,8},{7,5},{8,10},{9,7},{10,... | collective-permute-start | bytes 786440 | tf_op jit(solution)/shard_map/ppermute | solution.py:256
  13.3 12.7 %collective-permute-start = (bf16[656,128]{1,0:T(8,128)(2,1)S(1)}, bf16[656,128]{1,0:T(8,128)(2,1)S(1)}, u32[]{:S(2)}, u32[]{:S(2)}) collective-permute-start(bf16[656,128]{1,0:T(8,128)(2,1)S(1)} %get-tuple-element.43), channel_id=1, source_target_pairs={{0,31},{1,2},{2,1},{3,4},{4,3},{5,6},{6,5},{7,8},{8,7},{9,10},{10,... | collective-permute-start | bytes 503816 | tf_op jit(solution)/shard_map/ppermute | solution.py:256
  16.8 14.8 %collective-permute-start.7 = (bf16[1024,128]{1,0:T(8,128)(2,1)S(1)}, bf16[1024,128]{1,0:T(8,128)(2,1)S(1)}, u32[]{:S(2)}, u32[]{:S(2)}) collective-permute-start(bf16[1024,128]{1,0:T(8,128)(2,1)S(1)} %get-tuple-element.54), channel_id=1, source_target_pairs={{0,1},{1,0},{2,3},{3,2},{4,5},{5,4},{6,7},{7,6},{8,9},{9,8},{10,11... | collective-permute-start | bytes 786440 | tf_op jit(solution)/shard_map/ppermute | solution.py:256
  18.9 12.8 %collective-permute-start.6 = (bf16[128,1024]{1,0:T(8,128)(2,1)S(1)}, bf16[128,1024]{1,0:T(8,128)(2,1)S(1)}, u32[]{:S(2)}, u32[]{:S(2)}) collective-permute-start(bf16[128,1024]{1,0:T(8,128)(2,1)S(1)} %collective-permute-done.5.high_ref), channel_id=1, source_target_pairs={{0,2},{1,31},{2,4},{3,1},{4,6},{5,3},{6,8},{7,5},{8,10},{9,7},{10,... | collective-permute-start | bytes 786440 | tf_op jit(solution)/shard_map/ppermute | solution.py:256
  26.0 14.8 %collective-permute-start.4 = (bf16[1680,128]{1,0:T(8,128)(2,1)S(1)}, bf16[1680,128]{1,0:T(8,128)(2,1)S(1)}, u32[]{:S(2)}, u32[]{:S(2)}) collective-permute-start(bf16[1680,128]{1,0:T(8,128)(2,1)S(1)} %get-tuple-element.49), channel_id=1, source_target_pairs={{0,1},{1,0},{2,3},{3,2},{4,5},{5,4},{6,7},{7,6},{8,9},{9,8},{10,11... | collective-permute-start | bytes 1290248 | tf_op jit(solution)/shard_map/ppermute | solution.py:256
  28.1 10.9 %collective-permute-start.8 = (bf16[1024,128]{1,0:T(8,128)(2,1)S(1)}, bf16[1024,128]{1,0:T(8,128)(2,1)S(1)}, u32[]{:S(2)}, u32[]{:S(2)}) collective-permute-start(bf16[1024,128]{1,0:T(8,128)(2,1)S(1)} %collective-permute-done.3), channel_id=1, source_target_pairs={{0,2},{1,31},{2,4},{3,1},{4,6},{5,3},{6,8},{7,5},{8,10},{9,7},{10,... | collective-permute-start | bytes 786440 | tf_op jit(solution)/shard_map/ppermute | solution.py:256
  31.7 13.0 %collective-permute-start.10 = (bf16[1024,128]{1,0:T(8,128)(2,1)S(1)}, bf16[1024,128]{1,0:T(8,128)(2,1)S(1)}, u32[]{:S(2)}, u32[]{:S(2)}) collective-permute-start(bf16[1024,128]{1,0:T(8,128)(2,1)S(1)} %collective-permute-done.7), channel_id=1, source_target_pairs={{0,2},{1,31},{2,4},{3,1},{4,6},{5,3},{6,8},{7,5},{8,10},{9,7},{10,... | collective-permute-start | bytes 786440 | tf_op jit(solution)/shard_map/ppermute | solution.py:256
  33.8 11.9 %collective-permute-start.9 = (bf16[1024,128]{1,0:T(8,128)(2,1)S(1)}, bf16[1024,128]{1,0:T(8,128)(2,1)S(1)}, u32[]{:S(2)}, u32[]{:S(2)}) collective-permute-start(bf16[1024,128]{1,0:T(8,128)(2,1)S(1)} %get-tuple-element.63), channel_id=1, source_target_pairs={{0,1},{1,0},{2,3},{3,2},{4,5},{5,4},{6,7},{7,6},{8,9},{9,8},{10,11... | collective-permute-start | bytes 786440 | tf_op jit(solution)/shard_map/ppermute | solution.py:256

commit v5 on v4

--- a/solution.py
+++ b/solution.py
@@ -132,7 +132,18 @@
     halo_ref[B:PAIR, far + B : far + PAIR] = sent_ref[4 * B : 5 * B, :]
 
 
-def side_kernel(side, first_slab, held_slab, layout, scales_ref, v_ref, own_ref, halo_ref, low_ref, high_ref, *refs):
+def far_kernel(side, v_ref, halo_ref, low_ref, high_ref, far_ref):
+    pairs = v_ref.shape[0] // PAIR
+    band = jnp.concatenate([halo_ref[:, :PAIR], halo_ref[:, 2 * PAIR :]], axis=1)
+    for at in range(0, v_ref.shape[1], STEP):
+        lanes = slice(at, at + STEP)
+        edge = v_ref[natural(0 if side == 0 else 2, pairs), lanes]
+        far_ref[:, lanes] = dot(
+            band, jnp.concatenate([edge, low_ref[:, lanes], high_ref[:, lanes]], axis=0)
+        )
+
+
+def side_kernel(side, first_slab, held_slab, layout, scales_ref, v_ref, own_ref, halo_ref, far_ref, *refs):
     near_refs, refs = refs[: len(layout)], refs[len(layout) :]
     if side == 0:
         g_ref, h_ref, h1_ref, h1_out, end_out = refs
@@ -170,14 +181,11 @@
         held = slice((first_slab - held_slab) * B + at, (first_slab - held_slab) * B + to)
         near = jnp.concatenate(slabs[at // B : to // B], axis=1)
         v = v_ref[natural(edge, pairs), lanes]
-        others = jnp.concatenate([v, low_ref[:, lanes], high_ref[:, lanes]], axis=0)
         v32 = v.astype(jnp.float32)
         by_near = dot(jnp.concatenate([own_ref[rows, outward], halo_ref[:, PAIR : 2 * PAIR]], axis=0), near)
         image = g_ref[:, lanes] + by_near[:PAIR]
         edge_one = ((image - center * v32) / halfwidth).astype(v.dtype)
-        image = by_near[PAIR:] + dot(
-            jnp.concatenate([halo_ref[:, :PAIR], halo_ref[:, 2 * PAIR :]], axis=1), others
-        )
+        image = by_near[PAIR:] + far_ref[:, lanes]
         near_one = ((image - center * near.astype(jnp.float32)) / halfwidth).astype(v.dtype)
         by_edge = dot(
             jnp.concatenate([own_ref[PAIR : 2 * PAIR, outward], own_ref[rows, PAIR : 2 * PAIR]], axis=0),
@@ -272,14 +280,13 @@
 
     far_x = [send(part, over_x) for part in middle]
     near_d = [send(part, direct) for part in to_d]
-    far_x[1], via_x[1] = after(far_x[1], via_x[1])
     far_d = [send(part, onward) for part in far_x]
     passing = [send(part, over_x) for part in via_x]
-    far_d[0], passing[0] = after(far_d[0], passing[0])
     far_d[1], passing[1] = after(far_d[1], passing[1])
     near_d += [send(part, onward) for part in passing]
     passing[0], to_x[0] = after(passing[0], to_x[0])
     near_d[0], to_x[0] = after(near_d[0], to_x[0])
+    far_d[0], to_x[0] = after(far_d[0], to_x[0])
     passing[1], to_x[1] = after(passing[1], to_x[1])
 
     wide = lambda kind: pltpu.VMEM((PAIR, vec_width), kind)
@@ -288,6 +295,8 @@
     )
     band = [pltpu.VMEM((PAIR, 3 * PAIR), dtype)]
     (halo_d,) = call(functools.partial(halo_kernel, 0), band, [own, near_d[0]], "halo_d")
+    far = [wide(jnp.float32)]
+    (by_far_d,) = call(functools.partial(far_kernel, 0), far, [vectors, halo_d, *far_d], "far_d")
     result, mid, zero = None, None, None
     first_slab, held_slab, c = 0, 0, -1
     for part, (head, slabs) in zip(to_x, TO_X, strict=True):
@@ -302,7 +311,7 @@
             mid, zero = call(
                 functools.partial(side_kernel, 0, first_slab, held_slab, layout),
                 [pltpu.VMEM((PAIR, width), jnp.float32), pltpu.VMEM((PAIR, width), dtype)],
-                [scale, vectors, own, halo_d, *far_d, *near_c, g0, h0, h1],
+                [scale, vectors, own, halo_d, by_far_d, *near_c, g0, h0, h1],
                 "side_d",
             )
         if near is None:
@@ -313,7 +322,10 @@
             near, result = after(near, result)
         if result is None:
             (halo_x,) = call(functools.partial(halo_kernel, 1), band, [own, near], "halo_x")
-        args = [scale, vectors, own, halo_x, *far_x, near, g2, h2, mid, one, zero]
+            (by_far_x,) = call(
+                functools.partial(far_kernel, 1), far, [vectors, halo_x, *far_x], "far_x"
+            )
+        args = [scale, vectors, own, halo_x, by_far_x, near, g2, h2, mid, one, zero]
         aliases = {}
         if result is not None:
             aliases[len(args)] = 0

time: 47.4 us -> 47.3 us (level)
  starting transfers between devices: 21.9 us -> 21 us
  Pallas kernels: 7.95 us -> 8.51 us
    ppermute x11, starting transfers between devices: 21.9 us -> 21 us  [send(): return lax.ppermute(part, AXES, perm)]
    pallas_call x8 -> x10, Pallas kernels: 7.95 us -> 8.51 us  [call(): pl.pallas_call(body, out_shape=outs, in_specs=[whole(space) for space in...]
  transfers between devices with their start and end apart: 11 -> 11, of which waited for: 7 -> 7; matrix products, arithmetic and copies ran while one was open for 2% -> 2% of each run, Pallas kernels for 14% -> 15%
where the time goes in v5:
time: 47.3 us; the launch traced here: 47.1 us
  starting transfers between devices  21 us (44%)
  waiting for transfers between devices  12.7 us (27%)
  Pallas kernels  8.51 us (18%)
  local copies, waits for them, and re-layouts  4.77 us (10%)
    ppermute x11, starting transfers between devices, send(): return lax.ppermute(part, AXES, perm)  21 us
    ppermute x11, waiting for transfers between devices, send(): return lax.ppermute(part, AXES, perm)  12.7 us
    pallas_call x10, Pallas kernels, call(): pl.pallas_call(body, out_shape=outs, in_specs=[whole(space) for space in...  8.51 us
    unnamed x10, local copies, waits for them, and re-layouts  2.75 us
    slice x1, local copies, waits for them, and re-layouts, per_device(): low = lax.slice_in_dim(vectors, rows // 2 - B, rows // 2, axis=0)  1.05 us
    slice x1, local copies, waits for them, and re-layouts, per_device(): middle = [low, lax.slice_in_dim(rest, rows // 2, rows // 2 + B, axis=0)]  0.97 us
  transfers between devices with their start and end apart: 11, of which 7 were waited for; matrix products, arithmetic and copies ran while one was open for 2% of the time, Pallas kernels for 15%

profile of v5, /device:TPU:0, one launch (start us, length us, event | category | flops | bytes accessed | tf_op | source)
XLA Modules:
  0.0 47.1 jit_solution(11672412210503452167)
XLA Ops:
  0.0 0.0 copy-start.2
  0.0 1.1 %slice.6 = bf16[128,1024]{1,0:T(8,128)(2,1)S(1)} slice(bf16[768,1024]{1,0:T(8,128)(2,1)} %v_ref.14), slice={[256:384], [0:1024]} | slice | bytes 524288 | tf_op jit(solution)/shard_map/slice | solution.py:266
  1.1 3.0 %collective-permute-start = (bf16[128,1024]{1,0:T(8,128)(2,1)S(1)}, bf16[128,1024]{1,0:T(8,128)(2,1)S(1)}, u32[]{:S(2)}, u32[]{:S(2)}) collective-permute-start(bf16[128,1024]{1,0:T(8,128)(2,1)S(1)} %slice.6), channel_id=1, source_target_pairs={{0,1},{1,0},{2,3},{3,2},{4,5},{5,4},{6,7},{7,6},{8,9},{9,8},{10,11... | collective-permute-start | bytes 786440 | tf_op jit(solution)/shard_map/ppermute | solution.py:264
  4.1 1.0 %slice.7 = bf16[128,1024]{1,0:T(8,128)(2,1)S(1)} slice(bf16[768,1024]{1,0:T(8,128)(2,1)} %v_ref.14), slice={[384:512], [0:1024]} | slice | bytes 524288 | tf_op jit(solution)/shard_map/slice | solution.py:268
  5.0 0.1 collective-permute-start.5
  5.1 0.0 copy-done.2
  5.1 0.0 copy-start
  5.1 1.4 %copy-done = bf16[768,1024]{1,0:T(8,128)(2,1)S(1)} copy-done((bf16[768,1024]{1,0:T(8,128)(2,1)S(1)}, bf16[768,1024]{1,0:T(8,128)(2,1)}, u32[]{:S(2)}) %copy-start) | copy-done | bytes 1572888
  6.5 0.0 copy-start.3
  6.5 0.7 %copy-done.3 = s32[6,5]{1,0:T(8,128)S(1)} copy-done((s32[6,5]{1,0:T(8,128)S(1)}, s32[6,5]{1,0:T(8,128)}, u32[]{:S(2)}) %copy-start.3) | copy-done | bytes 144
  7.2 0.0 copy-start.4
  7.2 0.7 %copy-done.4 = f32[2]{0:T(128)S(1)} copy-done((f32[2]{0:T(128)S(1)}, f32[2]{0:T(128)}, u32[]{:S(2)}) %copy-start.4) | copy-done | bytes 32
  7.9 0.0 copy-start.1
  7.9 1.3 %pack.1 = (f32[8,128]{1,0:T(8,128)S(1)}, bf16[768,768]{1,0:T(8,128)(2,1)S(1)}, bf16[1680,128]{1,0:T(8,128)(2,1)S(1)}, bf16[1024,128]{1,0:T(8,128)(2,1)S(1)}, bf1...) custom-call(s32[6,5]{1,0:T(8,128)S(1)} %copy-done.3, f32[2]{0:T(128)S(1)} %copy-done.4, ...), custom_call_target="tpu_custom_call" | custom-call | tf_op jit(solution)/shard_map/pack/pallas_call | solution.py:232
  9.2 2.1 %collective-permute-start.3 = (bf16[1024,128]{1,0:T(8,128)(2,1)S(1)}, bf16[1024,128]{1,0:T(8,128)(2,1)S(1)}, u32[]{:S(2)}, u32[]{:S(2)}) collective-permute-start(bf16[1024,128]{1,0:T(8,128)(2,1)S(1)} %get-tuple-element.43), channel_id=1, source_target_pairs={{0,1},{1,0},{2,3},{3,2},{4,5},{5,4},{6,7},{7,6},{8,9},{9,8},{10,11... | collective-permute-start | bytes 786440 | tf_op jit(solution)/shard_map/ppermute | solution.py:264
  11.2 0.0 collective-permute-done.low_ref
  11.3 2.1 %collective-permute-start.1 = (bf16[128,1024]{1,0:T(8,128)(2,1)S(1)}, bf16[128,1024]{1,0:T(8,128)(2,1)S(1)}, u32[]{:S(2)}, u32[]{:S(2)}) collective-permute-start(bf16[128,1024]{1,0:T(8,128)(2,1)S(1)} %collective-permute-done.low_ref), channel_id=1, source_target_pairs={{0,2},{1,31},{2,4},{3,1},{4,6},{5,3},{6,8},{7,5},{8,10},{9,7},{10,... | collective-permute-start | bytes 786440 | tf_op jit(solution)/shard_map/ppermute | solution.py:264
  13.3 1.5 %collective-permute-start.2 = (bf16[656,128]{1,0:T(8,128)(2,1)S(1)}, bf16[656,128]{1,0:T(8,128)(2,1)S(1)}, u32[]{:S(2)}, u32[]{:S(2)}) collective-permute-start(bf16[656,128]{1,0:T(8,128)(2,1)S(1)} %get-tuple-element.42), channel_id=1, source_target_pairs={{0,31},{1,2},{2,1},{3,4},{4,3},{5,6},{6,5},{7,8},{8,7},{9,10},{10,... | collective-permute-start | bytes 503816 | tf_op jit(solution)/shard_map/ppermute | solution.py:264
  14.8 1.5 %collective-permute-start.7 = (bf16[1024,128]{1,0:T(8,128)(2,1)S(1)}, bf16[1024,128]{1,0:T(8,128)(2,1)S(1)}, u32[]{:S(2)}, u32[]{:S(2)}) collective-permute-start(bf16[1024,128]{1,0:T(8,128)(2,1)S(1)} %get-tuple-element.50), channel_id=1, source_target_pairs={{0,1},{1,0},{2,3},{3,2},{4,5},{5,4},{6,7},{7,6},{8,9},{9,8},{10,11... | collective-permute-start | bytes 786440 | tf_op jit(solution)/shard_map/ppermute | solution.py:264
  16.4 0.4 collective-permute-done.5.high_ref
  16.8 3.1 %collective-permute-start.6 = (bf16[128,1024]{1,0:T(8,128)(2,1)S(1)}, bf16[128,1024]{1,0:T(8,128)(2,1)S(1)}, u32[]{:S(2)}, u32[]{:S(2)}) collective-permute-start(bf16[128,1024]{1,0:T(8,128)(2,1)S(1)} %collective-permute-done.5.high_ref), channel_id=1, source_target_pairs={{0,2},{1,31},{2,4},{3,1},{4,6},{5,3},{6,8},{7,5},{8,10},{9,7},{10,... | collective-permute-start | bytes 786440 | tf_op jit(solution)/shard_map/ppermute | solution.py:264
  19.9 6.2 %collective-permute-done.3 = bf16[1024,128]{1,0:T(8,128)(2,1)S(1)} collective-permute-done((bf16[1024,128]{1,0:T(8,128)(2,1)S(1)}, bf16[1024,128]{1,0:T(8,128)(2,1)S(1)}, u32[]{:S(2)}, u32[]{:S(2)}) %collective-permute-start.3) | collective-permute-done | bytes 262176 | tf_op jit(solution)/shard_map/ppermute | solution.py:264
  26.0 0.0 collective-permute-done.2.sent_ref.refs_0_
  26.0 0.0 collective-permute-done.1.low_ref
  26.0 2.0 %collective-permute-start.4 = (bf16[1680,128]{1,0:T(8,128)(2,1)S(1)}, bf16[1680,128]{1,0:T(8,128)(2,1)S(1)}, u32[]{:S(2)}, u32[]{:S(2)}) collective-permute-start(bf16[1680,128]{1,0:T(8,128)(2,1)S(1)} %get-tuple-element.47), channel_id=1, source_target_pairs={{0,1},{1,0},{2,3},{3,2},{4,5},{5,4},{6,7},{7,6},{8,9},{9,8},{10,11... | collective-permute-start | bytes 1290248 | tf_op jit(solution)/shard_map/ppermute | solution.py:264
  28.1 1.6 %collective-permute-start.8 = (bf16[1024,128]{1,0:T(8,128)(2,1)S(1)}, bf16[1024,128]{1,0:T(8,128)(2,1)S(1)}, u32[]{:S(2)}, u32[]{:S(2)}) collective-permute-start(bf16[1024,128]{1,0:T(8,128)(2,1)S(1)} %collective-permute-done.3), channel_id=1, source_target_pairs={{0,2},{1,31},{2,4},{3,1},{4,6},{5,3},{6,8},{7,5},{8,10},{9,7},{10,... | collective-permute-start | bytes 786440 | tf_op jit(solution)/shard_map/ppermute | solution.py:264
  29.7 2.0 %collective-permute-done.7 = bf16[1024,128]{1,0:T(8,128)(2,1)S(1)} collective-permute-done((bf16[1024,128]{1,0:T(8,128)(2,1)S(1)}, bf16[1024,128]{1,0:T(8,128)(2,1)S(1)}, u32[]{:S(2)}, u32[]{:S(2)}) %collective-permute-start.7) | collective-permute-done | bytes 262176 | tf_op jit(solution)/shard_map/ppermute | solution.py:264
  31.6 0.0 collective-permute-done.6.high_ref
  31.7 2.1 %collective-permute-start.10 = (bf16[1024,128]{1,0:T(8,128)(2,1)S(1)}, bf16[1024,128]{1,0:T(8,128)(2,1)S(1)}, u32[]{:S(2)}, u32[]{:S(2)}) collective-permute-start(bf16[1024,128]{1,0:T(8,128)(2,1)S(1)} %collective-permute-done.7), channel_id=1, source_target_pairs={{0,2},{1,31},{2,4},{3,1},{4,6},{5,3},{6,8},{7,5},{8,10},{9,7},{10,... | collective-permute-start | bytes 786440 | tf_op jit(solution)/shard_map/ppermute | solution.py:264
  33.8 1.9 %collective-permute-start.9 = (bf16[1024,128]{1,0:T(8,128)(2,1)S(1)}, bf16[1024,128]{1,0:T(8,128)(2,1)S(1)}, u32[]{:S(2)}, u32[]{:S(2)}) collective-permute-start(bf16[1024,128]{1,0:T(8,128)(2,1)S(1)} %get-tuple-element.59), channel_id=1, source_target_pairs={{0,1},{1,0},{2,3},{3,2},{4,5},{5,4},{6,7},{7,6},{8,9},{9,8},{10,11... | collective-permute-start | bytes 786440 | tf_op jit(solution)/shard_map/ppermute | solution.py:264
  35.7 0.0 copy-done.1
  35.7 1.8 %core.1 = (bf16[256,1024]{1,0:T(8,128)(2,1)S(1)}, f32[256,1024]{1,0:T(8,128)S(1)}, f32[256,1024]{1,0:T(8,128)S(1)}, f32[256,1024]{1,0:T(8,128)S(1)}, f32[256,1024]{1,0:T(8,128)S(1)}, /*index=5*/f32[256,1024]{1,0:T(8,128)S(1)}) custom-call(f32[8,128]{1,0:T(8,128)S(1)} %get-tuple-element.39.scales_ref, bf16[768,1024]{1,0:T(8,128)(2,1)S(1)} %copy-done.1, ...), custom_call_target="tpu_custom_call" | custom-call | tf_op jit(solution)/shard_map/core/pallas_call | solution.py:232
  37.5 0.1 halo_d.1.halo_ref
  37.7 0.5 far_d.1.far_ref
  38.1 0.9 %collective-permute-done.8.refs_1_ = bf16[1024,128]{1,0:T(8,128)(2,1)S(1)} collective-permute-done((bf16[1024,128]{1,0:T(8,128)(2,1)S(1)}, bf16[1024,128]{1,0:T(8,128)(2,1)S(1)}, u32[]{:S(2)}, u32[]{:S(2)}) %collective-permute-start.8) | collective-permute-done | bytes 262176 | tf_op jit(solution)/shard_map/ppermute | solution.py:264
  39.0 0.7 %side_d.2 = (f32[256,512]{1,0:T(8,128)S(1)}, bf16[256,512]{1,0:T(8,128)(2,1)S(1)}) custom-call(f32[8,128]{1,0:T(8,128)S(1)} %get-tuple-element.39.scales_ref, bf16[768,1024]{1,0:T(8,128)(2,1)S(1)} %copy-done.1, bf16[768,768]{1,0:T(8,128)(2,1)S(1)} %get-tuple-element.40.own_ref, bf16[256,768]{1,0:T(8,128)(2,1)S(1)} %halo_d.1.halo_ref, ...), custom_call_target="tpu_custom_call" | custom-call | tf_op jit(solution)/shard_map/side_d/pallas_call | solution.py:232
  39.7 1.2 %collective-permute-done.4.sent_ref.refs_0_ = bf16[1680,128]{1,0:T(8,128)(2,1)S(1)} collective-permute-done((bf16[1680,128]{1,0:T(8,128)(2,1)S(1)}, bf16[1680,128]{1,0:T(8,128)(2,1)S(1)}, u32[]{:S(2)}, u32[]{:S(2)}) %collective-permute-start.4) | collective-permute-done | bytes 430112 | tf_op jit(solution)/shard_map/ppermute | solution.py:264
  40.9 0.1 halo_x.1.halo_ref
  41.0 0.5 far_x.1.far_ref
  41.5 1.4 %side_x.2.refs_6_ = bf16[768,1024]{1,0:T(8,128)(2,1)} custom-call(f32[8,128]{1,0:T(8,128)S(1)} %get-tuple-element.39.scales_ref, bf16[768,1024]{1,0:T(8,128)(2,1)S(1)} %copy-done.1, bf16[768,768]{1,0:T(8,128)(2,1)S(1)} %get-tuple-element.40.own_ref, bf16[256,768]{1,0:T(8,128)(2,1)S(1)} %halo_x.1.halo_ref, f32[256,1024]{1,0:T(8,128)S(1)} %far_x.1.far_ref, ...), custom_call_target="tpu_custom_call" | custom-call | tf_op jit(solution)/shard_map/side_x/pallas_call | solution.py:232
  42.9 1.7 %collective-permute-done.10.refs_0_ = bf16[1024,128]{1,0:T(8,128)(2,1)S(1)} collective-permute-done((bf16[1024,128]{1,0:T(8,128)(2,1)S(1)}, bf16[1024,128]{1,0:T(8,128)(2,1)S(1)}, u32[]{:S(2)}, u32[]{:S(2)}) %collective-permute-start.10) | collective-permute-done | bytes 262176 | tf_op jit(solution)/shard_map/ppermute | solution.py:264
  44.6 0.7 %side_d.3 = (f32[256,512]{1,0:T(8,128)S(1)}, bf16[256,512]{1,0:T(8,128)(2,1)S(1)}) custom-call(f32[8,128]{1,0:T(8,128)S(1)} %get-tuple-element.39.scales_ref, bf16[768,1024]{1,0:T(8,128)(2,1)S(1)} %copy-done.1, bf16[768,768]{1,0:T(8,128)(2,1)S(1)} %get-tuple-element.40.own_ref, bf16[256,768]{1,0:T(8,128)(2,1)S(1)} %halo_d.1.halo_ref, ...), custom_call_target="tpu_custom_call" | custom-call | tf_op jit(solution)/shard_map/side_d/pallas_call | solution.py:232
  45.3 0.3 collective-permute-done.9.refs_0_
  45.7 1.4 %side_x.3 = bf16[768,1024]{1,0:T(8,128)(2,1)} custom-call(f32[8,128]{1,0:T(8,128)S(1)} %get-tuple-element.39.scales_ref, bf16[768,1024]{1,0:T(8,128)(2,1)S(1)} %copy-done.1, bf16[768,768]{1,0:T(8,128)(2,1)S(1)} %get-tuple-element.40.own_ref, bf16[256,768]{1,0:T(8,128)(2,1)S(1)} %halo_x.1.halo_ref, ...), custom_call_target="tpu_custom_call", output_to_operand_aliasing={{}: (11, {})} | custom-call | tf_op jit(solution)/shard_map/side_x/pallas_call | solution.py:232
Async XLA Ops:
  0.0 5.1 %copy-start.2 = (bf16[6,5,128,128]{3,2,1,0:T(8,128)(2,1)S(1)}, bf16[6,5,128,128]{3,2,1,0:T(8,128)(2,1)}, u32[]{:S(2)}) copy-start(bf16[6,5,128,128]{3,2,1,0:T(8,128)(2,1)} %blocks_ref.1) | copy-start | bytes 2949124
  1.1 10.2 %collective-permute-start = (bf16[128,1024]{1,0:T(8,128)(2,1)S(1)}, bf16[128,1024]{1,0:T(8,128)(2,1)S(1)}, u32[]{:S(2)}, u32[]{:S(2)}) collective-permute-start(bf16[128,1024]{1,0:T(8,128)(2,1)S(1)} %slice.6), channel_id=1, source_target_pairs={{0,1},{1,0},{2,3},{3,2},{4,5},{5,4},{6,7},{7,6},{8,9},{9,8},{10,11... | collective-permute-start | bytes 786440 | tf_op jit(solution)/shard_map/ppermute | solution.py:264
  5.0 11.8 %collective-permute-start.5 = (bf16[128,1024]{1,0:T(8,128)(2,1)S(1)}, bf16[128,1024]{1,0:T(8,128)(2,1)S(1)}, u32[]{:S(2)}, u32[]{:S(2)}) collective-permute-start(bf16[128,1024]{1,0:T(8,128)(2,1)S(1)} %slice.7), channel_id=1, source_target_pairs={{0,1},{1,0},{2,3},{3,2},{4,5},{5,4},{6,7},{7,6},{8,9},{9,8},{10,11... | collective-permute-start | bytes 786440 | tf_op jit(solution)/shard_map/ppermute | solution.py:264
  5.1 1.4 %copy-start = (bf16[768,1024]{1,0:T(8,128)(2,1)S(1)}, bf16[768,1024]{1,0:T(8,128)(2,1)}, u32[]{:S(2)}) copy-start(bf16[768,1024]{1,0:T(8,128)(2,1)} %v_ref.14) | copy-start | bytes 4718596
  6.5 0.7 %copy-start.3 = (s32[6,5]{1,0:T(8,128)S(1)}, s32[6,5]{1,0:T(8,128)}, u32[]{:S(2)}) copy-start(s32[6,5]{1,0:T(8,128)} %cols_ref.1) | copy-start | bytes 364
  7.2 0.7 %copy-start.4 = (f32[2]{0:T(128)S(1)}, f32[2]{0:T(128)}, u32[]{:S(2)}) copy-start(f32[2]{0:T(128)} %bounds_ref.1) | copy-start | bytes 28
  7.9 27.8 %copy-start.1 = (bf16[768,1024]{1,0:T(8,128)(2,1)S(1)}, bf16[768,1024]{1,0:T(8,128)(2,1)}, u32[]{:S(2)}) copy-start(bf16[768,1024]{1,0:T(8,128)(2,1)} %v_ref.14) | copy-start | bytes 4718596
  9.2 16.8 %collective-permute-start.3 = (bf16[1024,128]{1,0:T(8,128)(2,1)S(1)}, bf16[1024,128]{1,0:T(8,128)(2,1)S(1)}, u32[]{:S(2)}, u32[]{:S(2)}) collective-permute-start(bf16[1024,128]{1,0:T(8,128)(2,1)S(1)} %get-tuple-element.43), channel_id=1, source_target_pairs={{0,1},{1,0},{2,3},{3,2},{4,5},{5,4},{6,7},{7,6},{8,9},{9,8},{10,11... | collective-permute-start | bytes 786440 | tf_op jit(solution)/shard_map/ppermute | solution.py:264
  11.3 14.8 %collective-permute-start.1 = (bf16[128,1024]{1,0:T(8,128)(2,1)S(1)}, bf16[128,1024]{1,0:T(8,128)(2,1)S(1)}, u32[]{:S(2)}, u32[]{:S(2)}) collective-permute-start(bf16[128,1024]{1,0:T(8,128)(2,1)S(1)} %collective-permute-done.low_ref), channel_id=1, source_target_pairs={{0,2},{1,31},{2,4},{3,1},{4,6},{5,3},{6,8},{7,5},{8,10},{9,7},{10,... | collective-permute-start | bytes 786440 | tf_op jit(solution)/shard_map/ppermute | solution.py:264
  13.3 12.7 %collective-permute-start.2 = (bf16[656,128]{1,0:T(8,128)(2,1)S(1)}, bf16[656,128]{1,0:T(8,128)(2,1)S(1)}, u32[]{:S(2)}, u32[]{:S(2)}) collective-permute-start(bf16[656,128]{1,0:T(8,128)(2,1)S(1)} %get-tuple-element.42), channel_id=1, source_target_pairs={{0,31},{1,2},{2,1},{3,4},{4,3},{5,6},{6,5},{7,8},{8,7},{9,10},{10,... | collective-permute-start | bytes 503816 | tf_op jit(solution)/shard_map/ppermute | solution.py:264
  14.8 16.8 %collective-permute-start.7 = (bf16[1024,128]{1,0:T(8,128)(2,1)S(1)}, bf16[1024,128]{1,0:T(8,128)(2,1)S(1)}, u32[]{:S(2)}, u32[]{:S(2)}) collective-permute-start(bf16[1024,128]{1,0:T(8,128)(2,1)S(1)} %get-tuple-element.50), channel_id=1, source_target_pairs={{0,1},{1,0},{2,3},{3,2},{4,5},{5,4},{6,7},{7,6},{8,9},{9,8},{10,11... | collective-permute-start | bytes 786440 | tf_op jit(solution)/shard_map/ppermute | solution.py:264
  16.8 14.8 %collective-permute-start.6 = (bf16[128,1024]{1,0:T(8,128)(2,1)S(1)}, bf16[128,1024]{1,0:T(8,128)(2,1)S(1)}, u32[]{:S(2)}, u32[]{:S(2)}) collective-permute-start(bf16[128,1024]{1,0:T(8,128)(2,1)S(1)} %collective-permute-done.5.high_ref), channel_id=1, source_target_pairs={{0,2},{1,31},{2,4},{3,1},{4,6},{5,3},{6,8},{7,5},{8,10},{9,7},{10,... | collective-permute-start | bytes 786440 | tf_op jit(solution)/shard_map/ppermute | solution.py:264
  26.0 14.8 %collective-permute-start.4 = (bf16[1680,128]{1,0:T(8,128)(2,1)S(1)}, bf16[1680,128]{1,0:T(8,128)(2,1)S(1)}, u32[]{:S(2)}, u32[]{:S(2)}) collective-permute-start(bf16[1680,128]{1,0:T(8,128)(2,1)S(1)} %get-tuple-element.47), channel_id=1, source_target_pairs={{0,1},{1,0},{2,3},{3,2},{4,5},{5,4},{6,7},{7,6},{8,9},{9,8},{10,11... | collective-permute-start | bytes 1290248 | tf_op jit(solution)/shard_map/ppermute | solution.py:264
  28.1 11.0 %collective-permute-start.8 = (bf16[1024,128]{1,0:T(8,128)(2,1)S(1)}, bf16[1024,128]{1,0:T(8,128)(2,1)S(1)}, u32[]{:S(2)}, u32[]{:S(2)}) collective-permute-start(bf16[1024,128]{1,0:T(8,128)(2,1)S(1)} %collective-permute-done.3), channel_id=1, source_target_pairs={{0,2},{1,31},{2,4},{3,1},{4,6},{5,3},{6,8},{7,5},{8,10},{9,7},{10,... | collective-permute-start | bytes 786440 | tf_op jit(solution)/shard_map/ppermute | solution.py:264
  31.7 13.0 %collective-permute-start.10 = (bf16[1024,128]{1,0:T(8,128)(2,1)S(1)}, bf16[1024,128]{1,0:T(8,128)(2,1)S(1)}, u32[]{:S(2)}, u32[]{:S(2)}) collective-permute-start(bf16[1024,128]{1,0:T(8,128)(2,1)S(1)} %collective-permute-done.7), channel_id=1, source_target_pairs={{0,2},{1,31},{2,4},{3,1},{4,6},{5,3},{6,8},{7,5},{8,10},{9,7},{10,... | collective-permute-start | bytes 786440 | tf_op jit(solution)/shard_map/ppermute | solution.py:264
  33.8 11.9 %collective-permute-start.9 = (bf16[1024,128]{1,0:T(8,128)(2,1)S(1)}, bf16[1024,128]{1,0:T(8,128)(2,1)S(1)}, u32[]{:S(2)}, u32[]{:S(2)}) collective-permute-start(bf16[1024,128]{1,0:T(8,128)(2,1)S(1)} %get-tuple-element.59), channel_id=1, source_target_pairs={{0,1},{1,0},{2,3},{3,2},{4,5},{5,4},{6,7},{7,6},{8,9},{9,8},{10,11... | collective-permute-start | bytes 786440 | tf_op jit(solution)/shard_map/ppermute | solution.py:264

commit v6 on v5

--- a/solution.py
+++ b/solution.py
@@ -10,6 +10,7 @@
 AXES = ("row", "col")
 B = 128
 PAIR = 2 * B
+LAST = 4 * B
 STEP = 4 * B
 HEAD = 5 * B + 16
 LIMIT = pltpu.CompilerParams(vmem_limit_bytes=16 * 1024 * 1024)
@@ -161,21 +162,21 @@
         for s in range(count)
     ]
     width = len(slabs) * B
-    all_lanes = slice(first_slab * B, first_slab * B + width)
+    step = STEP if side == 0 else LAST
     copies = []
-    if side == 1:
-        copies = [
-            pltpu.make_async_copy(source, out_ref.at[natural(pair, pairs), all_lanes], sems.at[pair])
-            for pair, source in ((1, mid_ref), (2, end_ref))
-        ]
-        if held_slab == first_slab:
-            held = slice(held_slab * B, held_slab * B + zero_ref.shape[1])
-            copies.insert(
-                0, pltpu.make_async_copy(zero_ref, out_ref.at[natural(0, pairs), held], sems.at[0])
+
+    def put(pair, source, columns):
+        copies.append(
+            pltpu.make_async_copy(
+                source, out_ref.at[natural(pair, pairs), columns], sems.at[len(copies)]
             )
-            copies[0].start()
-    for at in range(0, width, STEP):
-        to = min(at + STEP, width)
+        )
+        copies[-1].start()
+
+    if side == 1 and held_slab == first_slab:
+        put(0, zero_ref, slice(held_slab * B, held_slab * B + zero_ref.shape[1]))
+    for at in range(0, width, step):
+        to = min(at + step, width)
         lanes = slice(first_slab * B + at, first_slab * B + to)
         here = slice(at, to)
         held = slice((first_slab - held_slab) * B + at, (first_slab - held_slab) * B + to)
@@ -199,14 +200,14 @@
             one = one_ref[:, lanes].astype(jnp.float32)
             v1 = v_ref[natural(1, pairs), lanes].astype(jnp.float32)
             mid_ref[:, here] = (2.0 * ((h1 - center * one) / halfwidth) - v1).astype(v.dtype)
+            put(1, mid_ref.at[:, here], lanes)
         image = h_ref[:, lanes] + (by_edge[PAIR:] + dot(own_ref[rows, outward], near_one))
         end = (2.0 * ((image - center * edge_one.astype(jnp.float32)) / halfwidth) - v32).astype(v.dtype)
         if side == 0:
             end_out[:, here] = end
         else:
             end_ref[:, here] = end
-    for copy in copies[-2:]:
-        copy.start()
+            put(2, end_ref.at[:, here], lanes)
     for copy in copies:
         copy.wait()
 
@@ -336,7 +337,9 @@
             args,
             "side_x",
             aliases=aliases,
-            scratch=[pltpu.VMEM((PAIR, slabs * B), dtype)] * 2 + [pltpu.SemaphoreType.DMA((3,))],
+            scratch=[pltpu.VMEM((PAIR, slabs * B), dtype)] * 2 + [
+                pltpu.SemaphoreType.DMA((1 + 2 * pl.cdiv(slabs * B, LAST),))
+            ],
         )
         first_slab += slabs
     return result

time: 47.3 us -> 47.3 us (level)
  no operation moved by 1% of the time
where the time goes in v6:
time: 47.3 us; the launch traced here: 47.1 us
  starting transfers between devices  21 us (44%)
  waiting for transfers between devices  12.7 us (27%)
  Pallas kernels  8.51 us (18%)
  local copies, waits for them, and re-layouts  4.77 us (10%)
    ppermute x11, starting transfers between devices, send(): return lax.ppermute(part, AXES, perm)  21 us
    ppermute x11, waiting for transfers between devices, send(): return lax.ppermute(part, AXES, perm)  12.7 us
    pallas_call x10, Pallas kernels, call(): pl.pallas_call(body, out_shape=outs, in_specs=[whole(space) for space in...  8.51 us
    unnamed x10, local copies, waits for them, and re-layouts  2.75 us
    slice x1, local copies, waits for them, and re-layouts, per_device(): low = lax.slice_in_dim(vectors, rows // 2 - B, rows // 2, axis=0)  1.05 us
    slice x1, local copies, waits for them, and re-layouts, per_device(): middle = [low, lax.slice_in_dim(rest, rows // 2, rows // 2 + B, axis=0)]  0.97 us
  transfers between devices with their start and end apart: 11, of which 7 were waited for; matrix products, arithmetic and copies ran while one was open for 2% of the time, Pallas kernels for 15%

profile of v6, /device:TPU:0, one launch (start us, length us, event | category | flops | bytes accessed | tf_op | source)
XLA Modules:
  0.0 47.1 jit_solution(11672412210503452167)
XLA Ops:
  0.0 0.0 copy-start.2
  0.0 1.1 %slice.6 = bf16[128,1024]{1,0:T(8,128)(2,1)S(1)} slice(bf16[768,1024]{1,0:T(8,128)(2,1)} %v_ref.14), slice={[256:384], [0:1024]} | slice | bytes 524288 | tf_op jit(solution)/shard_map/slice | solution.py:267
  1.1 3.0 %collective-permute-start = (bf16[128,1024]{1,0:T(8,128)(2,1)S(1)}, bf16[128,1024]{1,0:T(8,128)(2,1)S(1)}, u32[]{:S(2)}, u32[]{:S(2)}) collective-permute-start(bf16[128,1024]{1,0:T(8,128)(2,1)S(1)} %slice.6), channel_id=1, source_target_pairs={{0,1},{1,0},{2,3},{3,2},{4,5},{5,4},{6,7},{7,6},{8,9},{9,8},{10,11... | collective-permute-start | bytes 786440 | tf_op jit(solution)/shard_map/ppermute | solution.py:265
  4.1 1.0 %slice.7 = bf16[128,1024]{1,0:T(8,128)(2,1)S(1)} slice(bf16[768,1024]{1,0:T(8,128)(2,1)} %v_ref.14), slice={[384:512], [0:1024]} | slice | bytes 524288 | tf_op jit(solution)/shard_map/slice | solution.py:269
  5.0 0.1 collective-permute-start.5
  5.1 0.0 copy-done.2
  5.1 0.0 copy-start
  5.1 1.4 %copy-done = bf16[768,1024]{1,0:T(8,128)(2,1)S(1)} copy-done((bf16[768,1024]{1,0:T(8,128)(2,1)S(1)}, bf16[768,1024]{1,0:T(8,128)(2,1)}, u32[]{:S(2)}) %copy-start) | copy-done | bytes 1572888
  6.5 0.0 copy-start.3
  6.5 0.7 %copy-done.3 = s32[6,5]{1,0:T(8,128)S(1)} copy-done((s32[6,5]{1,0:T(8,128)S(1)}, s32[6,5]{1,0:T(8,128)}, u32[]{:S(2)}) %copy-start.3) | copy-done | bytes 144
  7.2 0.0 copy-start.4
  7.2 0.7 %copy-done.4 = f32[2]{0:T(128)S(1)} copy-done((f32[2]{0:T(128)S(1)}, f32[2]{0:T(128)}, u32[]{:S(2)}) %copy-start.4) | copy-done | bytes 32
  7.9 0.0 copy-start.1
  7.9 1.3 %pack.1 = (f32[8,128]{1,0:T(8,128)S(1)}, bf16[768,768]{1,0:T(8,128)(2,1)S(1)}, bf16[1680,128]{1,0:T(8,128)(2,1)S(1)}, bf16[1024,128]{1,0:T(8,128)(2,1)S(1)}, bf1...) custom-call(s32[6,5]{1,0:T(8,128)S(1)} %copy-done.3, f32[2]{0:T(128)S(1)} %copy-done.4, ...), custom_call_target="tpu_custom_call" | custom-call | tf_op jit(solution)/shard_map/pack/pallas_call | solution.py:233
  9.2 2.1 %collective-permute-start.3 = (bf16[1024,128]{1,0:T(8,128)(2,1)S(1)}, bf16[1024,128]{1,0:T(8,128)(2,1)S(1)}, u32[]{:S(2)}, u32[]{:S(2)}) collective-permute-start(bf16[1024,128]{1,0:T(8,128)(2,1)S(1)} %get-tuple-element.43), channel_id=1, source_target_pairs={{0,1},{1,0},{2,3},{3,2},{4,5},{5,4},{6,7},{7,6},{8,9},{9,8},{10,11... | collective-permute-start | bytes 786440 | tf_op jit(solution)/shard_map/ppermute | solution.py:265
  11.2 0.0 collective-permute-done.low_ref
  11.3 2.1 %collective-permute-start.1 = (bf16[128,1024]{1,0:T(8,128)(2,1)S(1)}, bf16[128,1024]{1,0:T(8,128)(2,1)S(1)}, u32[]{:S(2)}, u32[]{:S(2)}) collective-permute-start(bf16[128,1024]{1,0:T(8,128)(2,1)S(1)} %collective-permute-done.low_ref), channel_id=1, source_target_pairs={{0,2},{1,31},{2,4},{3,1},{4,6},{5,3},{6,8},{7,5},{8,10},{9,7},{10,... | collective-permute-start | bytes 786440 | tf_op jit(solution)/shard_map/ppermute | solution.py:265
  13.3 1.5 %collective-permute-start.2 = (bf16[656,128]{1,0:T(8,128)(2,1)S(1)}, bf16[656,128]{1,0:T(8,128)(2,1)S(1)}, u32[]{:S(2)}, u32[]{:S(2)}) collective-permute-start(bf16[656,128]{1,0:T(8,128)(2,1)S(1)} %get-tuple-element.42), channel_id=1, source_target_pairs={{0,31},{1,2},{2,1},{3,4},{4,3},{5,6},{6,5},{7,8},{8,7},{9,10},{10,... | collective-permute-start | bytes 503816 | tf_op jit(solution)/shard_map/ppermute | solution.py:265
  14.8 1.5 %collective-permute-start.7 = (bf16[1024,128]{1,0:T(8,128)(2,1)S(1)}, bf16[1024,128]{1,0:T(8,128)(2,1)S(1)}, u32[]{:S(2)}, u32[]{:S(2)}) collective-permute-start(bf16[1024,128]{1,0:T(8,128)(2,1)S(1)} %get-tuple-element.50), channel_id=1, source_target_pairs={{0,1},{1,0},{2,3},{3,2},{4,5},{5,4},{6,7},{7,6},{8,9},{9,8},{10,11... | collective-permute-start | bytes 786440 | tf_op jit(solution)/shard_map/ppermute | solution.py:265
  16.4 0.4 collective-permute-done.5.high_ref
  16.8 3.1 %collective-permute-start.6 = (bf16[128,1024]{1,0:T(8,128)(2,1)S(1)}, bf16[128,1024]{1,0:T(8,128)(2,1)S(1)}, u32[]{:S(2)}, u32[]{:S(2)}) collective-permute-start(bf16[128,1024]{1,0:T(8,128)(2,1)S(1)} %collective-permute-done.5.high_ref), channel_id=1, source_target_pairs={{0,2},{1,31},{2,4},{3,1},{4,6},{5,3},{6,8},{7,5},{8,10},{9,7},{10,... | collective-permute-start | bytes 786440 | tf_op jit(solution)/shard_map/ppermute | solution.py:265
  19.9 6.2 %collective-permute-done.3 = bf16[1024,128]{1,0:T(8,128)(2,1)S(1)} collective-permute-done((bf16[1024,128]{1,0:T(8,128)(2,1)S(1)}, bf16[1024,128]{1,0:T(8,128)(2,1)S(1)}, u32[]{:S(2)}, u32[]{:S(2)}) %collective-permute-start.3) | collective-permute-done | bytes 262176 | tf_op jit(solution)/shard_map/ppermute | solution.py:265
  26.0 0.0 collective-permute-done.2.sent_ref.refs_0_
  26.0 0.0 collective-permute-done.1.low_ref
  26.0 2.0 %collective-permute-start.4 = (bf16[1680,128]{1,0:T(8,128)(2,1)S(1)}, bf16[1680,128]{1,0:T(8,128)(2,1)S(1)}, u32[]{:S(2)}, u32[]{:S(2)}) collective-permute-start(bf16[1680,128]{1,0:T(8,128)(2,1)S(1)} %get-tuple-element.47), channel_id=1, source_target_pairs={{0,1},{1,0},{2,3},{3,2},{4,5},{5,4},{6,7},{7,6},{8,9},{9,8},{10,11... | collective-permute-start | bytes 1290248 | tf_op jit(solution)/shard_map/ppermute | solution.py:265
  28.1 1.6 %collective-permute-start.8 = (bf16[1024,128]{1,0:T(8,128)(2,1)S(1)}, bf16[1024,128]{1,0:T(8,128)(2,1)S(1)}, u32[]{:S(2)}, u32[]{:S(2)}) collective-permute-start(bf16[1024,128]{1,0:T(8,128)(2,1)S(1)} %collective-permute-done.3), channel_id=1, source_target_pairs={{0,2},{1,31},{2,4},{3,1},{4,6},{5,3},{6,8},{7,5},{8,10},{9,7},{10,... | collective-permute-start | bytes 786440 | tf_op jit(solution)/shard_map/ppermute | solution.py:265
  29.7 2.0 %collective-permute-done.7 = bf16[1024,128]{1,0:T(8,128)(2,1)S(1)} collective-permute-done((bf16[1024,128]{1,0:T(8,128)(2,1)S(1)}, bf16[1024,128]{1,0:T(8,128)(2,1)S(1)}, u32[]{:S(2)}, u32[]{:S(2)}) %collective-permute-start.7) | collective-permute-done | bytes 262176 | tf_op jit(solution)/shard_map/ppermute | solution.py:265
  31.6 0.0 collective-permute-done.6.high_ref
  31.7 2.1 %collective-permute-start.10 = (bf16[1024,128]{1,0:T(8,128)(2,1)S(1)}, bf16[1024,128]{1,0:T(8,128)(2,1)S(1)}, u32[]{:S(2)}, u32[]{:S(2)}) collective-permute-start(bf16[1024,128]{1,0:T(8,128)(2,1)S(1)} %collective-permute-done.7), channel_id=1, source_target_pairs={{0,2},{1,31},{2,4},{3,1},{4,6},{5,3},{6,8},{7,5},{8,10},{9,7},{10,... | collective-permute-start | bytes 786440 | tf_op jit(solution)/shard_map/ppermute | solution.py:265
  33.8 1.9 %collective-permute-start.9 = (bf16[1024,128]{1,0:T(8,128)(2,1)S(1)}, bf16[1024,128]{1,0:T(8,128)(2,1)S(1)}, u32[]{:S(2)}, u32[]{:S(2)}) collective-permute-start(bf16[1024,128]{1,0:T(8,128)(2,1)S(1)} %get-tuple-element.59), channel_id=1, source_target_pairs={{0,1},{1,0},{2,3},{3,2},{4,5},{5,4},{6,7},{7,6},{8,9},{9,8},{10,11... | collective-permute-start | bytes 786440 | tf_op jit(solution)/shard_map/ppermute | solution.py:265
  35.7 0.0 copy-done.1
  35.7 1.8 %core.1 = (bf16[256,1024]{1,0:T(8,128)(2,1)S(1)}, f32[256,1024]{1,0:T(8,128)S(1)}, f32[256,1024]{1,0:T(8,128)S(1)}, f32[256,1024]{1,0:T(8,128)S(1)}, f32[256,1024]{1,0:T(8,128)S(1)}, /*index=5*/f32[256,1024]{1,0:T(8,128)S(1)}) custom-call(f32[8,128]{1,0:T(8,128)S(1)} %get-tuple-element.39.scales_ref, bf16[768,1024]{1,0:T(8,128)(2,1)S(1)} %copy-done.1, ...), custom_call_target="tpu_custom_call" | custom-call | tf_op jit(solution)/shard_map/core/pallas_call | solution.py:233
  37.5 0.1 halo_d.1.halo_ref
  37.7 0.5 far_d.1.far_ref
  38.1 0.9 %collective-permute-done.8.refs_1_ = bf16[1024,128]{1,0:T(8,128)(2,1)S(1)} collective-permute-done((bf16[1024,128]{1,0:T(8,128)(2,1)S(1)}, bf16[1024,128]{1,0:T(8,128)(2,1)S(1)}, u32[]{:S(2)}, u32[]{:S(2)}) %collective-permute-start.8) | collective-permute-done | bytes 262176 | tf_op jit(solution)/shard_map/ppermute | solution.py:265
  39.0 0.7 %side_d.2 = (f32[256,512]{1,0:T(8,128)S(1)}, bf16[256,512]{1,0:T(8,128)(2,1)S(1)}) custom-call(f32[8,128]{1,0:T(8,128)S(1)} %get-tuple-element.39.scales_ref, bf16[768,1024]{1,0:T(8,128)(2,1)S(1)} %copy-done.1, bf16[768,768]{1,0:T(8,128)(2,1)S(1)} %get-tuple-element.40.own_ref, bf16[256,768]{1,0:T(8,128)(2,1)S(1)} %halo_d.1.halo_ref, ...), custom_call_target="tpu_custom_call" | custom-call | tf_op jit(solution)/shard_map/side_d/pallas_call | solution.py:233
  39.7 1.2 %collective-permute-done.4.sent_ref.refs_0_ = bf16[1680,128]{1,0:T(8,128)(2,1)S(1)} collective-permute-done((bf16[1680,128]{1,0:T(8,128)(2,1)S(1)}, bf16[1680,128]{1,0:T(8,128)(2,1)S(1)}, u32[]{:S(2)}, u32[]{:S(2)}) %collective-permute-start.4) | collective-permute-done | bytes 430112 | tf_op jit(solution)/shard_map/ppermute | solution.py:265
  40.9 0.1 halo_x.1.halo_ref
  41.0 0.5 far_x.1.far_ref
  41.5 1.4 %side_x.2.refs_6_ = bf16[768,1024]{1,0:T(8,128)(2,1)} custom-call(f32[8,128]{1,0:T(8,128)S(1)} %get-tuple-element.39.scales_ref, bf16[768,1024]{1,0:T(8,128)(2,1)S(1)} %copy-done.1, bf16[768,768]{1,0:T(8,128)(2,1)S(1)} %get-tuple-element.40.own_ref, bf16[256,768]{1,0:T(8,128)(2,1)S(1)} %halo_x.1.halo_ref, f32[256,1024]{1,0:T(8,128)S(1)} %far_x.1.far_ref, ...), custom_call_target="tpu_custom_call" | custom-call | tf_op jit(solution)/shard_map/side_x/pallas_call | solution.py:233
  42.9 1.7 %collective-permute-done.10.refs_0_ = bf16[1024,128]{1,0:T(8,128)(2,1)S(1)} collective-permute-done((bf16[1024,128]{1,0:T(8,128)(2,1)S(1)}, bf16[1024,128]{1,0:T(8,128)(2,1)S(1)}, u32[]{:S(2)}, u32[]{:S(2)}) %collective-permute-start.10) | collective-permute-done | bytes 262176 | tf_op jit(solution)/shard_map/ppermute | solution.py:265
  44.6 0.7 %side_d.3 = (f32[256,512]{1,0:T(8,128)S(1)}, bf16[256,512]{1,0:T(8,128)(2,1)S(1)}) custom-call(f32[8,128]{1,0:T(8,128)S(1)} %get-tuple-element.39.scales_ref, bf16[768,1024]{1,0:T(8,128)(2,1)S(1)} %copy-done.1, bf16[768,768]{1,0:T(8,128)(2,1)S(1)} %get-tuple-element.40.own_ref, bf16[256,768]{1,0:T(8,128)(2,1)S(1)} %halo_d.1.halo_ref, ...), custom_call_target="tpu_custom_call" | custom-call | tf_op jit(solution)/shard_map/side_d/pallas_call | solution.py:233
  45.3 0.3 collective-permute-done.9.refs_0_
  45.7 1.4 %side_x.3 = bf16[768,1024]{1,0:T(8,128)(2,1)} custom-call(f32[8,128]{1,0:T(8,128)S(1)} %get-tuple-element.39.scales_ref, bf16[768,1024]{1,0:T(8,128)(2,1)S(1)} %copy-done.1, bf16[768,768]{1,0:T(8,128)(2,1)S(1)} %get-tuple-element.40.own_ref, bf16[256,768]{1,0:T(8,128)(2,1)S(1)} %halo_x.1.halo_ref, ...), custom_call_target="tpu_custom_call", output_to_operand_aliasing={{}: (11, {})} | custom-call | tf_op jit(solution)/shard_map/side_x/pallas_call | solution.py:233
Async XLA Ops:
  0.0 5.1 %copy-start.2 = (bf16[6,5,128,128]{3,2,1,0:T(8,128)(2,1)S(1)}, bf16[6,5,128,128]{3,2,1,0:T(8,128)(2,1)}, u32[]{:S(2)}) copy-start(bf16[6,5,128,128]{3,2,1,0:T(8,128)(2,1)} %blocks_ref.1) | copy-start | bytes 2949124
  1.1 10.2 %collective-permute-start = (bf16[128,1024]{1,0:T(8,128)(2,1)S(1)}, bf16[128,1024]{1,0:T(8,128)(2,1)S(1)}, u32[]{:S(2)}, u32[]{:S(2)}) collective-permute-start(bf16[128,1024]{1,0:T(8,128)(2,1)S(1)} %slice.6), channel_id=1, source_target_pairs={{0,1},{1,0},{2,3},{3,2},{4,5},{5,4},{6,7},{7,6},{8,9},{9,8},{10,11... | collective-permute-start | bytes 786440 | tf_op jit(solution)/shard_map/ppermute | solution.py:265
  5.0 11.8 %collective-permute-start.5 = (bf16[128,1024]{1,0:T(8,128)(2,1)S(1)}, bf16[128,1024]{1,0:T(8,128)(2,1)S(1)}, u32[]{:S(2)}, u32[]{:S(2)}) collective-permute-start(bf16[128,1024]{1,0:T(8,128)(2,1)S(1)} %slice.7), channel_id=1, source_target_pairs={{0,1},{1,0},{2,3},{3,2},{4,5},{5,4},{6,7},{7,6},{8,9},{9,8},{10,11... | collective-permute-start | bytes 786440 | tf_op jit(solution)/shard_map/ppermute | solution.py:265
  5.1 1.4 %copy-start = (bf16[768,1024]{1,0:T(8,128)(2,1)S(1)}, bf16[768,1024]{1,0:T(8,128)(2,1)}, u32[]{:S(2)}) copy-start(bf16[768,1024]{1,0:T(8,128)(2,1)} %v_ref.14) | copy-start | bytes 4718596
  6.5 0.7 %copy-start.3 = (s32[6,5]{1,0:T(8,128)S(1)}, s32[6,5]{1,0:T(8,128)}, u32[]{:S(2)}) copy-start(s32[6,5]{1,0:T(8,128)} %cols_ref.1) | copy-start | bytes 364
  7.2 0.7 %copy-start.4 = (f32[2]{0:T(128)S(1)}, f32[2]{0:T(128)}, u32[]{:S(2)}) copy-start(f32[2]{0:T(128)} %bounds_ref.1) | copy-start | bytes 28
  7.9 27.8 %copy-start.1 = (bf16[768,1024]{1,0:T(8,128)(2,1)S(1)}, bf16[768,1024]{1,0:T(8,128)(2,1)}, u32[]{:S(2)}) copy-start(bf16[768,1024]{1,0:T(8,128)(2,1)} %v_ref.14) | copy-start | bytes 4718596
  9.2 16.8 %collective-permute-start.3 = (bf16[1024,128]{1,0:T(8,128)(2,1)S(1)}, bf16[1024,128]{1,0:T(8,128)(2,1)S(1)}, u32[]{:S(2)}, u32[]{:S(2)}) collective-permute-start(bf16[1024,128]{1,0:T(8,128)(2,1)S(1)} %get-tuple-element.43), channel_id=1, source_target_pairs={{0,1},{1,0},{2,3},{3,2},{4,5},{5,4},{6,7},{7,6},{8,9},{9,8},{10,11... | collective-permute-start | bytes 786440 | tf_op jit(solution)/shard_map/ppermute | solution.py:265
  11.3 14.8 %collective-permute-start.1 = (bf16[128,1024]{1,0:T(8,128)(2,1)S(1)}, bf16[128,1024]{1,0:T(8,128)(2,1)S(1)}, u32[]{:S(2)}, u32[]{:S(2)}) collective-permute-start(bf16[128,1024]{1,0:T(8,128)(2,1)S(1)} %collective-permute-done.low_ref), channel_id=1, source_target_pairs={{0,2},{1,31},{2,4},{3,1},{4,6},{5,3},{6,8},{7,5},{8,10},{9,7},{10,... | collective-permute-start | bytes 786440 | tf_op jit(solution)/shard_map/ppermute | solution.py:265
  13.3 12.7 %collective-permute-start.2 = (bf16[656,128]{1,0:T(8,128)(2,1)S(1)}, bf16[656,128]{1,0:T(8,128)(2,1)S(1)}, u32[]{:S(2)}, u32[]{:S(2)}) collective-permute-start(bf16[656,128]{1,0:T(8,128)(2,1)S(1)} %get-tuple-element.42), channel_id=1, source_target_pairs={{0,31},{1,2},{2,1},{3,4},{4,3},{5,6},{6,5},{7,8},{8,7},{9,10},{10,... | collective-permute-start | bytes 503816 | tf_op jit(solution)/shard_map/ppermute | solution.py:265
  14.8 16.8 %collective-permute-start.7 = (bf16[1024,128]{1,0:T(8,128)(2,1)S(1)}, bf16[1024,128]{1,0:T(8,128)(2,1)S(1)}, u32[]{:S(2)}, u32[]{:S(2)}) collective-permute-start(bf16[1024,128]{1,0:T(8,128)(2,1)S(1)} %get-tuple-element.50), channel_id=1, source_target_pairs={{0,1},{1,0},{2,3},{3,2},{4,5},{5,4},{6,7},{7,6},{8,9},{9,8},{10,11... | collective-permute-start | bytes 786440 | tf_op jit(solution)/shard_map/ppermute | solution.py:265
  16.8 14.8 %collective-permute-start.6 = (bf16[128,1024]{1,0:T(8,128)(2,1)S(1)}, bf16[128,1024]{1,0:T(8,128)(2,1)S(1)}, u32[]{:S(2)}, u32[]{:S(2)}) collective-permute-start(bf16[128,1024]{1,0:T(8,128)(2,1)S(1)} %collective-permute-done.5.high_ref), channel_id=1, source_target_pairs={{0,2},{1,31},{2,4},{3,1},{4,6},{5,3},{6,8},{7,5},{8,10},{9,7},{10,... | collective-permute-start | bytes 786440 | tf_op jit(solution)/shard_map/ppermute | solution.py:265
  26.0 14.8 %collective-permute-start.4 = (bf16[1680,128]{1,0:T(8,128)(2,1)S(1)}, bf16[1680,128]{1,0:T(8,128)(2,1)S(1)}, u32[]{:S(2)}, u32[]{:S(2)}) collective-permute-start(bf16[1680,128]{1,0:T(8,128)(2,1)S(1)} %get-tuple-element.47), channel_id=1, source_target_pairs={{0,1},{1,0},{2,3},{3,2},{4,5},{5,4},{6,7},{7,6},{8,9},{9,8},{10,11... | collective-permute-start | bytes 1290248 | tf_op jit(solution)/shard_map/ppermute | solution.py:265
  28.1 11.0 %collective-permute-start.8 = (bf16[1024,128]{1,0:T(8,128)(2,1)S(1)}, bf16[1024,128]{1,0:T(8,128)(2,1)S(1)}, u32[]{:S(2)}, u32[]{:S(2)}) collective-permute-start(bf16[1024,128]{1,0:T(8,128)(2,1)S(1)} %collective-permute-done.3), channel_id=1, source_target_pairs={{0,2},{1,31},{2,4},{3,1},{4,6},{5,3},{6,8},{7,5},{8,10},{9,7},{10,... | collective-permute-start | bytes 786440 | tf_op jit(solution)/shard_map/ppermute | solution.py:265
  31.7 13.0 %collective-permute-start.10 = (bf16[1024,128]{1,0:T(8,128)(2,1)S(1)}, bf16[1024,128]{1,0:T(8,128)(2,1)S(1)}, u32[]{:S(2)}, u32[]{:S(2)}) collective-permute-start(bf16[1024,128]{1,0:T(8,128)(2,1)S(1)} %collective-permute-done.7), channel_id=1, source_target_pairs={{0,2},{1,31},{2,4},{3,1},{4,6},{5,3},{6,8},{7,5},{8,10},{9,7},{10,... | collective-permute-start | bytes 786440 | tf_op jit(solution)/shard_map/ppermute | solution.py:265
  33.8 11.9 %collective-permute-start.9 = (bf16[1024,128]{1,0:T(8,128)(2,1)S(1)}, bf16[1024,128]{1,0:T(8,128)(2,1)S(1)}, u32[]{:S(2)}, u32[]{:S(2)}) collective-permute-start(bf16[1024,128]{1,0:T(8,128)(2,1)S(1)} %get-tuple-element.59), channel_id=1, source_target_pairs={{0,1},{1,0},{2,3},{3,2},{4,5},{5,4},{6,7},{7,6},{8,9},{9,8},{10,11... | collective-permute-start | bytes 786440 | tf_op jit(solution)/shard_map/ppermute | solution.py:265

commit v7 on v5

--- a/solution.py
+++ b/solution.py
@@ -280,6 +280,7 @@
 
     far_x = [send(part, over_x) for part in middle]
     near_d = [send(part, direct) for part in to_d]
+    far_x[0], via_x[1] = after(far_x[0], via_x[1])
     far_d = [send(part, onward) for part in far_x]
     passing = [send(part, over_x) for part in via_x]
     far_d[1], passing[1] = after(far_d[1], passing[1])

time: 47.3 us -> 47.3 us (level)
  starting transfers between devices: 21 us -> 21.9 us
  waiting for transfers between devices: 12.7 us -> 11.8 us
    ppermute x11, waiting for transfers between devices: 12.7 us -> 11.8 us  [send(): return lax.ppermute(part, AXES, perm)]
    ppermute x11, starting transfers between devices: 21 us -> 21.9 us  [send(): return lax.ppermute(part, AXES, perm)]
  transfers between devices with their start and end apart: 11 -> 11, of which waited for: 7 -> 8; matrix products, arithmetic and copies ran while one was open for 2% -> 2% of each run, Pallas kernels for 15% -> 15%
where the time goes in v7:
time: 47.3 us; the launch traced here: 47.1 us
  starting transfers between devices  21.9 us (46%)
  waiting for transfers between devices  11.8 us (25%)
  Pallas kernels  8.51 us (18%)
  local copies, waits for them, and re-layouts  4.77 us (10%)
    ppermute x11, starting transfers between devices, send(): return lax.ppermute(part, AXES, perm)  21.9 us
    ppermute x11, waiting for transfers between devices, send(): return lax.ppermute(part, AXES, perm)  11.8 us
    pallas_call x10, Pallas kernels, call(): pl.pallas_call(body, out_shape=outs, in_specs=[whole(space) for space in...  8.51 us
    unnamed x10, local copies, waits for them, and re-layouts  2.75 us
    slice x1, local copies, waits for them, and re-layouts, per_device(): low = lax.slice_in_dim(vectors, rows // 2 - B, rows // 2, axis=0)  1.05 us
    slice x1, local copies, waits for them, and re-layouts, per_device(): middle = [low, lax.slice_in_dim(rest, rows // 2, rows // 2 + B, axis=0)]  0.97 us
  transfers between devices with their start and end apart: 11, of which 8 were waited for; matrix products, arithmetic and copies ran while one was open for 2% of the time, Pallas kernels for 15%

profile of v7, /device:TPU:0, one launch (start us, length us, event | category | flops | bytes accessed | tf_op | source)
XLA Modules:
  0.0 47.1 jit_solution(7512466568618195948)
XLA Ops:
  0.0 0.0 copy-start.2
  0.0 1.1 %slice.6 = bf16[128,1024]{1,0:T(8,128)(2,1)S(1)} slice(bf16[768,1024]{1,0:T(8,128)(2,1)} %v_ref.14), slice={[256:384], [0:1024]} | slice | bytes 524288 | tf_op jit(solution)/shard_map/slice | solution.py:266
  1.1 3.0 %collective-permute-start = (bf16[128,1024]{1,0:T(8,128)(2,1)S(1)}, bf16[128,1024]{1,0:T(8,128)(2,1)S(1)}, u32[]{:S(2)}, u32[]{:S(2)}) collective-permute-start(bf16[128,1024]{1,0:T(8,128)(2,1)S(1)} %slice.6), channel_id=1, source_target_pairs={{0,1},{1,0},{2,3},{3,2},{4,5},{5,4},{6,7},{7,6},{8,9},{9,8},{10,11... | collective-permute-start | bytes 786440 | tf_op jit(solution)/shard_map/ppermute | solution.py:264
  4.1 1.0 %slice.7 = bf16[128,1024]{1,0:T(8,128)(2,1)S(1)} slice(bf16[768,1024]{1,0:T(8,128)(2,1)} %v_ref.14), slice={[384:512], [0:1024]} | slice | bytes 524288 | tf_op jit(solution)/shard_map/slice | solution.py:268
  5.0 0.1 collective-permute-start.5
  5.1 0.0 copy-done.2
  5.1 0.0 copy-start
  5.1 1.4 %copy-done = bf16[768,1024]{1,0:T(8,128)(2,1)S(1)} copy-done((bf16[768,1024]{1,0:T(8,128)(2,1)S(1)}, bf16[768,1024]{1,0:T(8,128)(2,1)}, u32[]{:S(2)}) %copy-start) | copy-done | bytes 1572888
  6.5 0.0 copy-start.3
  6.5 0.7 %copy-done.3 = s32[6,5]{1,0:T(8,128)S(1)} copy-done((s32[6,5]{1,0:T(8,128)S(1)}, s32[6,5]{1,0:T(8,128)}, u32[]{:S(2)}) %copy-start.3) | copy-done | bytes 144
  7.2 0.0 copy-start.4
  7.2 0.7 %copy-done.4 = f32[2]{0:T(128)S(1)} copy-done((f32[2]{0:T(128)S(1)}, f32[2]{0:T(128)}, u32[]{:S(2)}) %copy-start.4) | copy-done | bytes 32
  7.9 0.0 copy-start.1
  7.9 1.3 %pack.1 = (f32[8,128]{1,0:T(8,128)S(1)}, bf16[768,768]{1,0:T(8,128)(2,1)S(1)}, bf16[1680,128]{1,0:T(8,128)(2,1)S(1)}, bf16[1024,128]{1,0:T(8,128)(2,1)S(1)}, bf1...) custom-call(s32[6,5]{1,0:T(8,128)S(1)} %copy-done.3, f32[2]{0:T(128)S(1)} %copy-done.4, ...), custom_call_target="tpu_custom_call" | custom-call | tf_op jit(solution)/shard_map/pack/pallas_call | solution.py:232
  9.2 2.1 %collective-permute-start.3 = (bf16[1024,128]{1,0:T(8,128)(2,1)S(1)}, bf16[1024,128]{1,0:T(8,128)(2,1)S(1)}, u32[]{:S(2)}, u32[]{:S(2)}) collective-permute-start(bf16[1024,128]{1,0:T(8,128)(2,1)S(1)} %get-tuple-element.47), channel_id=1, source_target_pairs={{0,1},{1,0},{2,3},{3,2},{4,5},{5,4},{6,7},{7,6},{8,9},{9,8},{10,11... | collective-permute-start | bytes 786440 | tf_op jit(solution)/shard_map/ppermute | solution.py:264
  11.2 0.0 collective-permute-done.low_ref
  11.3 2.1 %collective-permute-start.1 = (bf16[128,1024]{1,0:T(8,128)(2,1)S(1)}, bf16[128,1024]{1,0:T(8,128)(2,1)S(1)}, u32[]{:S(2)}, u32[]{:S(2)}) collective-permute-start(bf16[128,1024]{1,0:T(8,128)(2,1)S(1)} %collective-permute-done.low_ref), channel_id=1, source_target_pairs={{0,2},{1,31},{2,4},{3,1},{4,6},{5,3},{6,8},{7,5},{8,10},{9,7},{10,... | collective-permute-start | bytes 786440 | tf_op jit(solution)/shard_map/ppermute | solution.py:264
  13.3 1.5 %collective-permute-start.2 = (bf16[656,128]{1,0:T(8,128)(2,1)S(1)}, bf16[656,128]{1,0:T(8,128)(2,1)S(1)}, u32[]{:S(2)}, u32[]{:S(2)}) collective-permute-start(bf16[656,128]{1,0:T(8,128)(2,1)S(1)} %get-tuple-element.46), channel_id=1, source_target_pairs={{0,31},{1,2},{2,1},{3,4},{4,3},{5,6},{6,5},{7,8},{8,7},{9,10},{10,... | collective-permute-start | bytes 503816 | tf_op jit(solution)/shard_map/ppermute | solution.py:264
  14.8 2.0 %collective-permute-done.5.high_ref = bf16[128,1024]{1,0:T(8,128)(2,1)S(1)} collective-permute-done((bf16[128,1024]{1,0:T(8,128)(2,1)S(1)}, bf16[128,1024]{1,0:T(8,128)(2,1)S(1)}, u32[]{:S(2)}, u32[]{:S(2)}) %collective-permute-start.5) | collective-permute-done | bytes 262176 | tf_op jit(solution)/shard_map/ppermute | solution.py:264
  16.8 3.1 %collective-permute-start.6 = (bf16[128,1024]{1,0:T(8,128)(2,1)S(1)}, bf16[128,1024]{1,0:T(8,128)(2,1)S(1)}, u32[]{:S(2)}, u32[]{:S(2)}) collective-permute-start(bf16[128,1024]{1,0:T(8,128)(2,1)S(1)} %collective-permute-done.5.high_ref), channel_id=1, source_target_pairs={{0,2},{1,31},{2,4},{3,1},{4,6},{5,3},{6,8},{7,5},{8,10},{9,7},{10,... | collective-permute-start | bytes 786440 | tf_op jit(solution)/shard_map/ppermute | solution.py:264
  19.9 1.0 %collective-permute-start.7 = (bf16[1024,128]{1,0:T(8,128)(2,1)S(1)}, bf16[1024,128]{1,0:T(8,128)(2,1)S(1)}, u32[]{:S(2)}, u32[]{:S(2)}) collective-permute-start(bf16[1024,128]{1,0:T(8,128)(2,1)S(1)} %get-tuple-element.54), channel_id=1, source_target_pairs={{0,1},{1,0},{2,3},{3,2},{4,5},{5,4},{6,7},{7,6},{8,9},{9,8},{10,11... | collective-permute-start | bytes 786440 | tf_op jit(solution)/shard_map/ppermute | solution.py:264
  20.9 4.3 %collective-permute-done.3 = bf16[1024,128]{1,0:T(8,128)(2,1)S(1)} collective-permute-done((bf16[1024,128]{1,0:T(8,128)(2,1)S(1)}, bf16[1024,128]{1,0:T(8,128)(2,1)S(1)}, u32[]{:S(2)}, u32[]{:S(2)}) %collective-permute-start.3) | collective-permute-done | bytes 262176 | tf_op jit(solution)/shard_map/ppermute | solution.py:264
  25.1 0.0 collective-permute-done.2.sent_ref.refs_0_
  25.1 0.0 collective-permute-done.1.low_ref
  25.1 2.9 %collective-permute-start.4 = (bf16[1680,128]{1,0:T(8,128)(2,1)S(1)}, bf16[1680,128]{1,0:T(8,128)(2,1)S(1)}, u32[]{:S(2)}, u32[]{:S(2)}) collective-permute-start(bf16[1680,128]{1,0:T(8,128)(2,1)S(1)} %get-tuple-element.51), channel_id=1, source_target_pairs={{0,1},{1,0},{2,3},{3,2},{4,5},{5,4},{6,7},{7,6},{8,9},{9,8},{10,11... | collective-permute-start | bytes 1290248 | tf_op jit(solution)/shard_map/ppermute | solution.py:264
  28.1 1.6 %collective-permute-start.8 = (bf16[1024,128]{1,0:T(8,128)(2,1)S(1)}, bf16[1024,128]{1,0:T(8,128)(2,1)S(1)}, u32[]{:S(2)}, u32[]{:S(2)}) collective-permute-start(bf16[1024,128]{1,0:T(8,128)(2,1)S(1)} %collective-permute-done.3), channel_id=1, source_target_pairs={{0,2},{1,31},{2,4},{3,1},{4,6},{5,3},{6,8},{7,5},{8,10},{9,7},{10,... | collective-permute-start | bytes 786440 | tf_op jit(solution)/shard_map/ppermute | solution.py:264
  29.7 1.3 %collective-permute-done.6.high_ref = bf16[128,1024]{1,0:T(8,128)(2,1)S(1)} collective-permute-done((bf16[128,1024]{1,0:T(8,128)(2,1)S(1)}, bf16[128,1024]{1,0:T(8,128)(2,1)S(1)}, u32[]{:S(2)}, u32[]{:S(2)}) %collective-permute-start.6) | collective-permute-done | bytes 262176 | tf_op jit(solution)/shard_map/ppermute | solution.py:264
  31.0 0.1 collective-permute-done.7
  31.1 2.7 %collective-permute-start.10 = (bf16[1024,128]{1,0:T(8,128)(2,1)S(1)}, bf16[1024,128]{1,0:T(8,128)(2,1)S(1)}, u32[]{:S(2)}, u32[]{:S(2)}) collective-permute-start(bf16[1024,128]{1,0:T(8,128)(2,1)S(1)} %collective-permute-done.7), channel_id=1, source_target_pairs={{0,2},{1,31},{2,4},{3,1},{4,6},{5,3},{6,8},{7,5},{8,10},{9,7},{10,... | collective-permute-start | bytes 786440 | tf_op jit(solution)/shard_map/ppermute | solution.py:264
  33.8 1.9 %collective-permute-start.9 = (bf16[1024,128]{1,0:T(8,128)(2,1)S(1)}, bf16[1024,128]{1,0:T(8,128)(2,1)S(1)}, u32[]{:S(2)}, u32[]{:S(2)}) collective-permute-start(bf16[1024,128]{1,0:T(8,128)(2,1)S(1)} %get-tuple-element.63), channel_id=1, source_target_pairs={{0,1},{1,0},{2,3},{3,2},{4,5},{5,4},{6,7},{7,6},{8,9},{9,8},{10,11... | collective-permute-start | bytes 786440 | tf_op jit(solution)/shard_map/ppermute | solution.py:264
  35.7 0.0 copy-done.1
  35.7 1.8 %core.1 = (bf16[256,1024]{1,0:T(8,128)(2,1)S(1)}, f32[256,1024]{1,0:T(8,128)S(1)}, f32[256,1024]{1,0:T(8,128)S(1)}, f32[256,1024]{1,0:T(8,128)S(1)}, f32[256,1024]{1,0:T(8,128)S(1)}, /*index=5*/f32[256,1024]{1,0:T(8,128)S(1)}) custom-call(f32[8,128]{1,0:T(8,128)S(1)} %get-tuple-element.41.scales_ref, bf16[768,1024]{1,0:T(8,128)(2,1)S(1)} %copy-done.1, ...), custom_call_target="tpu_custom_call" | custom-call | tf_op jit(solution)/shard_map/core/pallas_call | solution.py:232
  37.5 0.1 halo_d.1.halo_ref
  37.7 0.5 far_d.1.far_ref
  38.1 0.9 %collective-permute-done.8.refs_1_ = bf16[1024,128]{1,0:T(8,128)(2,1)S(1)} collective-permute-done((bf16[1024,128]{1,0:T(8,128)(2,1)S(1)}, bf16[1024,128]{1,0:T(8,128)(2,1)S(1)}, u32[]{:S(2)}, u32[]{:S(2)}) %collective-permute-start.8) | collective-permute-done | bytes 262176 | tf_op jit(solution)/shard_map/ppermute | solution.py:264
  39.0 0.7 %side_d.2 = (f32[256,512]{1,0:T(8,128)S(1)}, bf16[256,512]{1,0:T(8,128)(2,1)S(1)}) custom-call(f32[8,128]{1,0:T(8,128)S(1)} %get-tuple-element.41.scales_ref, bf16[768,1024]{1,0:T(8,128)(2,1)S(1)} %copy-done.1, bf16[768,768]{1,0:T(8,128)(2,1)S(1)} %get-tuple-element.42.own_ref, bf16[256,768]{1,0:T(8,128)(2,1)S(1)} %halo_d.1.halo_ref, ...), custom_call_target="tpu_custom_call" | custom-call | tf_op jit(solution)/shard_map/side_d/pallas_call | solution.py:232
  39.7 0.6 %collective-permute-done.4.sent_ref.refs_0_ = bf16[1680,128]{1,0:T(8,128)(2,1)S(1)} collective-permute-done((bf16[1680,128]{1,0:T(8,128)(2,1)S(1)}, bf16[1680,128]{1,0:T(8,128)(2,1)S(1)}, u32[]{:S(2)}, u32[]{:S(2)}) %collective-permute-start.4) | collective-permute-done | bytes 430112 | tf_op jit(solution)/shard_map/ppermute | solution.py:264
  40.3 0.1 halo_x.1.halo_ref
  40.4 0.5 far_x.1.far_ref
  40.9 1.4 %side_x.2.refs_6_ = bf16[768,1024]{1,0:T(8,128)(2,1)} custom-call(f32[8,128]{1,0:T(8,128)S(1)} %get-tuple-element.41.scales_ref, bf16[768,1024]{1,0:T(8,128)(2,1)S(1)} %copy-done.1, bf16[768,768]{1,0:T(8,128)(2,1)S(1)} %get-tuple-element.42.own_ref, bf16[256,768]{1,0:T(8,128)(2,1)S(1)} %halo_x.1.halo_ref, f32[256,1024]{1,0:T(8,128)S(1)} %far_x.1.far_ref, ...), custom_call_target="tpu_custom_call" | custom-call | tf_op jit(solution)/shard_map/side_x/pallas_call | solution.py:232
  42.4 2.3 %collective-permute-done.10.refs_0_ = bf16[1024,128]{1,0:T(8,128)(2,1)S(1)} collective-permute-done((bf16[1024,128]{1,0:T(8,128)(2,1)S(1)}, bf16[1024,128]{1,0:T(8,128)(2,1)S(1)}, u32[]{:S(2)}, u32[]{:S(2)}) %collective-permute-start.10) | collective-permute-done | bytes 262176 | tf_op jit(solution)/shard_map/ppermute | solution.py:264
  44.6 0.7 %side_d.3 = (f32[256,512]{1,0:T(8,128)S(1)}, bf16[256,512]{1,0:T(8,128)(2,1)S(1)}) custom-call(f32[8,128]{1,0:T(8,128)S(1)} %get-tuple-element.41.scales_ref, bf16[768,1024]{1,0:T(8,128)(2,1)S(1)} %copy-done.1, bf16[768,768]{1,0:T(8,128)(2,1)S(1)} %get-tuple-element.42.own_ref, bf16[256,768]{1,0:T(8,128)(2,1)S(1)} %halo_d.1.halo_ref, ...), custom_call_target="tpu_custom_call" | custom-call | tf_op jit(solution)/shard_map/side_d/pallas_call | solution.py:232
  45.3 0.3 collective-permute-done.9.refs_0_
  45.7 1.4 %side_x.3 = bf16[768,1024]{1,0:T(8,128)(2,1)} custom-call(f32[8,128]{1,0:T(8,128)S(1)} %get-tuple-element.41.scales_ref, bf16[768,1024]{1,0:T(8,128)(2,1)S(1)} %copy-done.1, bf16[768,768]{1,0:T(8,128)(2,1)S(1)} %get-tuple-element.42.own_ref, bf16[256,768]{1,0:T(8,128)(2,1)S(1)} %halo_x.1.halo_ref, ...), custom_call_target="tpu_custom_call", output_to_operand_aliasing={{}: (11, {})} | custom-call | tf_op jit(solution)/shard_map/side_x/pallas_call | solution.py:232
Async XLA Ops:
  0.0 5.1 %copy-start.2 = (bf16[6,5,128,128]{3,2,1,0:T(8,128)(2,1)S(1)}, bf16[6,5,128,128]{3,2,1,0:T(8,128)(2,1)}, u32[]{:S(2)}) copy-start(bf16[6,5,128,128]{3,2,1,0:T(8,128)(2,1)} %blocks_ref.1) | copy-start | bytes 2949124
  1.1 10.2 %collective-permute-start = (bf16[128,1024]{1,0:T(8,128)(2,1)S(1)}, bf16[128,1024]{1,0:T(8,128)(2,1)S(1)}, u32[]{:S(2)}, u32[]{:S(2)}) collective-permute-start(bf16[128,1024]{1,0:T(8,128)(2,1)S(1)} %slice.6), channel_id=1, source_target_pairs={{0,1},{1,0},{2,3},{3,2},{4,5},{5,4},{6,7},{7,6},{8,9},{9,8},{10,11... | collective-permute-start | bytes 786440 | tf_op jit(solution)/shard_map/ppermute | solution.py:264
  5.0 11.8 %collective-permute-start.5 = (bf16[128,1024]{1,0:T(8,128)(2,1)S(1)}, bf16[128,1024]{1,0:T(8,128)(2,1)S(1)}, u32[]{:S(2)}, u32[]{:S(2)}) collective-permute-start(bf16[128,1024]{1,0:T(8,128)(2,1)S(1)} %slice.7), channel_id=1, source_target_pairs={{0,1},{1,0},{2,3},{3,2},{4,5},{5,4},{6,7},{7,6},{8,9},{9,8},{10,11... | collective-permute-start | bytes 786440 | tf_op jit(solution)/shard_map/ppermute | solution.py:264
  5.1 1.4 %copy-start = (bf16[768,1024]{1,0:T(8,128)(2,1)S(1)}, bf16[768,1024]{1,0:T(8,128)(2,1)}, u32[]{:S(2)}) copy-start(bf16[768,1024]{1,0:T(8,128)(2,1)} %v_ref.14) | copy-start | bytes 4718596
  6.5 0.7 %copy-start.3 = (s32[6,5]{1,0:T(8,128)S(1)}, s32[6,5]{1,0:T(8,128)}, u32[]{:S(2)}) copy-start(s32[6,5]{1,0:T(8,128)} %cols_ref.1) | copy-start | bytes 364
  7.2 0.7 %copy-start.4 = (f32[2]{0:T(128)S(1)}, f32[2]{0:T(128)}, u32[]{:S(2)}) copy-start(f32[2]{0:T(128)} %bounds_ref.1) | copy-start | bytes 28
  7.9 27.8 %copy-start.1 = (bf16[768,1024]{1,0:T(8,128)(2,1)S(1)}, bf16[768,1024]{1,0:T(8,128)(2,1)}, u32[]{:S(2)}) copy-start(bf16[768,1024]{1,0:T(8,128)(2,1)} %v_ref.14) | copy-start | bytes 4718596
  9.2 15.9 %collective-permute-start.3 = (bf16[1024,128]{1,0:T(8,128)(2,1)S(1)}, bf16[1024,128]{1,0:T(8,128)(2,1)S(1)}, u32[]{:S(2)}, u32[]{:S(2)}) collective-permute-start(bf16[1024,128]{1,0:T(8,128)(2,1)S(1)} %get-tuple-element.47), channel_id=1, source_target_pairs={{0,1},{1,0},{2,3},{3,2},{4,5},{5,4},{6,7},{7,6},{8,9},{9,8},{10,11... | collective-permute-start | bytes 786440 | tf_op jit(solution)/shard_map/ppermute | solution.py:264
  11.3 13.9 %collective-permute-start.1 = (bf16[128,1024]{1,0:T(8,128)(2,1)S(1)}, bf16[128,1024]{1,0:T(8,128)(2,1)S(1)}, u32[]{:S(2)}, u32[]{:S(2)}) collective-permute-start(bf16[128,1024]{1,0:T(8,128)(2,1)S(1)} %collective-permute-done.low_ref), channel_id=1, source_target_pairs={{0,2},{1,31},{2,4},{3,1},{4,6},{5,3},{6,8},{7,5},{8,10},{9,7},{10,... | collective-permute-start | bytes 786440 | tf_op jit(solution)/shard_map/ppermute | solution.py:264
  13.3 11.8 %collective-permute-start.2 = (bf16[656,128]{1,0:T(8,128)(2,1)S(1)}, bf16[656,128]{1,0:T(8,128)(2,1)S(1)}, u32[]{:S(2)}, u32[]{:S(2)}) collective-permute-start(bf16[656,128]{1,0:T(8,128)(2,1)S(1)} %get-tuple-element.46), channel_id=1, source_target_pairs={{0,31},{1,2},{2,1},{3,4},{4,3},{5,6},{6,5},{7,8},{8,7},{9,10},{10,... | collective-permute-start | bytes 503816 | tf_op jit(solution)/shard_map/ppermute | solution.py:264
  16.8 14.2 %collective-permute-start.6 = (bf16[128,1024]{1,0:T(8,128)(2,1)S(1)}, bf16[128,1024]{1,0:T(8,128)(2,1)S(1)}, u32[]{:S(2)}, u32[]{:S(2)}) collective-permute-start(bf16[128,1024]{1,0:T(8,128)(2,1)S(1)} %collective-permute-done.5.high_ref), channel_id=1, source_target_pairs={{0,2},{1,31},{2,4},{3,1},{4,6},{5,3},{6,8},{7,5},{8,10},{9,7},{10,... | collective-permute-start | bytes 786440 | tf_op jit(solution)/shard_map/ppermute | solution.py:264
  19.9 11.2 %collective-permute-start.7 = (bf16[1024,128]{1,0:T(8,128)(2,1)S(1)}, bf16[1024,128]{1,0:T(8,128)(2,1)S(1)}, u32[]{:S(2)}, u32[]{:S(2)}) collective-permute-start(bf16[1024,128]{1,0:T(8,128)(2,1)S(1)} %get-tuple-element.54), channel_id=1, source_target_pairs={{0,1},{1,0},{2,3},{3,2},{4,5},{5,4},{6,7},{7,6},{8,9},{9,8},{10,11... | collective-permute-start | bytes 786440 | tf_op jit(solution)/shard_map/ppermute | solution.py:264
  25.1 15.2 %collective-permute-start.4 = (bf16[1680,128]{1,0:T(8,128)(2,1)S(1)}, bf16[1680,128]{1,0:T(8,128)(2,1)S(1)}, u32[]{:S(2)}, u32[]{:S(2)}) collective-permute-start(bf16[1680,128]{1,0:T(8,128)(2,1)S(1)} %get-tuple-element.51), channel_id=1, source_target_pairs={{0,1},{1,0},{2,3},{3,2},{4,5},{5,4},{6,7},{7,6},{8,9},{9,8},{10,11... | collective-permute-start | bytes 1290248 | tf_op jit(solution)/shard_map/ppermute | solution.py:264
  28.1 10.9 %collective-permute-start.8 = (bf16[1024,128]{1,0:T(8,128)(2,1)S(1)}, bf16[1024,128]{1,0:T(8,128)(2,1)S(1)}, u32[]{:S(2)}, u32[]{:S(2)}) collective-permute-start(bf16[1024,128]{1,0:T(8,128)(2,1)S(1)} %collective-permute-done.3), channel_id=1, source_target_pairs={{0,2},{1,31},{2,4},{3,1},{4,6},{5,3},{6,8},{7,5},{8,10},{9,7},{10,... | collective-permute-start | bytes 786440 | tf_op jit(solution)/shard_map/ppermute | solution.py:264
  31.1 13.6 %collective-permute-start.10 = (bf16[1024,128]{1,0:T(8,128)(2,1)S(1)}, bf16[1024,128]{1,0:T(8,128)(2,1)S(1)}, u32[]{:S(2)}, u32[]{:S(2)}) collective-permute-start(bf16[1024,128]{1,0:T(8,128)(2,1)S(1)} %collective-permute-done.7), channel_id=1, source_target_pairs={{0,2},{1,31},{2,4},{3,1},{4,6},{5,3},{6,8},{7,5},{8,10},{9,7},{10,... | collective-permute-start | bytes 786440 | tf_op jit(solution)/shard_map/ppermute | solution.py:264
  33.8 11.9 %collective-permute-start.9 = (bf16[1024,128]{1,0:T(8,128)(2,1)S(1)}, bf16[1024,128]{1,0:T(8,128)(2,1)S(1)}, u32[]{:S(2)}, u32[]{:S(2)}) collective-permute-start(bf16[1024,128]{1,0:T(8,128)(2,1)S(1)} %get-tuple-element.63), channel_id=1, source_target_pairs={{0,1},{1,0},{2,3},{3,2},{4,5},{5,4},{6,7},{7,6},{8,9},{9,8},{10,11... | collective-permute-start | bytes 786440 | tf_op jit(solution)/shard_map/ppermute | solution.py:264
